TPU v7x, 128 devices: a whole 4x4x4 slice. The times are simulated.
128 devices in a mesh: dom: 32 (over y, z, core), case: 4 (over x).
Axes of the slice: x: 4, y: 4, z: 4, core: 2. Of those that a mesh axis runs over, the one named last changes fastest.
Arguments:
- dual_ops: float32 [64, 1536, 1536], P('dom')
- modes: bfloat16 [64, 16, 1536], P('dom'), may hold values from -0.15625 to 0.15625
- coarse_rows: float32 [64, 8, 16, 16], P('dom'), may hold values from -1 to 1
- coarse_cols: int32 [64, 8], P('dom'), may hold values from 0 to 63, as said below
- row_perm: int32 [64, 1536], P('dom'), may hold values from 0 to 1535, each once within a row
- iface_size: int32 [64], P('dom'), may hold values from 256 to 768, as said below
- rhs: float32 [64, 768, 512], P('dom', None, 'case'), may hold values from -6 to 6
Outputs:
- solution: float32 [64, 768, 512], P('dom', None, 'case')
- residual: float32 [64, 768, 512], P('dom', None, 'case')
- history: float32 [4, 512], P(None, 'case')
- peak_norm: float32 [4], replicated
Inputs may be any that keep to these rules, and one draw needn't show every extreme that they name: `iface_size`: interfaces carry between 256 and 768 multipliers; both ends are reached in every draw. `coarse_cols`: for every subdomain s the first three entries are s, (s - 1) mod 64 and (s + 1) mod 64; the others are any subdomains, repeats allowed. `row_perm`: each row is a permutation of the local rows.
All inputs are finite; a program needn't handle non-finite values.
Results may differ from a plain program's by a relative error of at most 0.0056.
Values may be sent and summed in bfloat16 or wider, within the bound.
No kernel may reach another device: no remote copies, remote signals or barrier semaphores. Data moves between devices by JAX's collectives and lax.ppermute only.
A program may use at most 192 MiB of HBM per device.

v0:
```python
import jax
import jax.numpy as jnp
from jax import lax
from jax.sharding import PartitionSpec as P

STEPS = 4


low_bound = 2.0
high_bound = 14.0
epsilon = 1e-06
highest = lax.Precision.HIGHEST


def from_behind(block, axis, distance):
    devices = range(lax.axis_size(axis))
    route = [((i - distance) % len(devices), i) for i in devices]
    return lax.ppermute(block, axis, route)


def copy_for_each(value, axis):
    size = lax.axis_size(axis)
    return lax.all_to_all(
        jnp.broadcast_to(value[None], (size, *value.shape)), axis, 0, 0, tiled=True
    )


def in_order(tiles, dim):
    tiles = jnp.moveaxis(tiles, 0, dim)
    dims = tiles.shape
    return tiles.reshape(*dims[:dim], dims[dim] * dims[dim + 1], *dims[dim + 2 :])


def gather_directly(value, axis, dim):
    tiles = copy_for_each(value, axis)
    return in_order(tiles, dim)


def of_everyone(value, axis):
    everything = copy_for_each(value, axis)
    return jnp.sum(everything, axis=0)


def slot_form(left_side, right_side):
    return jnp.concatenate([-left_side, right_side], axis=1)


def shards(dual_ops, modes, coarse_rows, coarse_cols, row_perm, iface_size, rhs):
    sub_count, half_width, case_count = rhs.shape
    dom_count = lax.axis_size("dom") * sub_count
    live_mask = (
        lax.broadcasted_iota(jnp.int32, (sub_count, half_width), 1) < iface_size[:, None]
    ).astype(jnp.float32)[:, :, None]
    slot_ops = jax.vmap(lambda matrix, ordering: matrix[ordering].T[ordering])(dual_ops, row_perm)
    slot_modes_low = jax.vmap(lambda block_rows, ordering: block_rows[:, ordering])(modes, row_perm)
    slot_modes = slot_modes_low.astype(jnp.float32)
    int_pack = jnp.concatenate([coarse_cols, iface_size[:, None]], axis=1)
    prior_ints = from_behind(int_pack[-1], "dom", 1)
    next_ints = from_behind(int_pack[0], "dom", -1)
    prior_modes = from_behind(slot_modes_low[-1], "dom", 1)
    next_modes = from_behind(slot_modes_low[0], "dom", -1)
    prior_blocks = from_behind(coarse_rows[-1], "dom", 1)
    next_blocks = from_behind(coarse_rows[0], "dom", -1)
    ext_ints = jnp.concatenate([prior_ints[None], int_pack, next_ints[None]], axis=0)
    block_count = coarse_cols.shape[1]
    ext_cols = ext_ints[:, :block_count]
    ext_size = ext_ints[:, block_count]
    ext_modes = jnp.concatenate(
        [prior_modes[None], slot_modes_low, next_modes[None]], axis=0
    ).astype(jnp.float32)
    ext_blocks = jnp.concatenate([prior_blocks[None], coarse_rows, next_blocks[None]], axis=0)
    ext_live = (
        lax.broadcasted_iota(jnp.int32, (sub_count + 2, half_width), 1) < ext_size[:, None]
    ).astype(jnp.float32)[:, :, None]

    def build_local(vector):
        prior_rim = from_behind(vector[-1], "dom", 1)
        left_side = jnp.concatenate([prior_rim[None], vector[:-1]], axis=0)
        return slot_form(left_side, vector)

    def select_columns(columns, all_coefficients):
        table = (
            columns[:, :, None] == lax.broadcasted_iota(jnp.int32, (1, 1, dom_count), 2)
        ).astype(jnp.float32)
        return jnp.einsum(
            "sqd,djc->sqjc", table, all_coefficients.astype(jnp.float32), precision=highest
        )

    def gather_coefficients(slot_rows):
        coefficients = jnp.einsum("sjn,snc->sjc", slot_modes, slot_rows, precision=highest).astype(
            jnp.bfloat16
        )
        return gather_directly(coefficients, "dom", 0)

    centre = 0.5 * (high_bound + low_bound)
    radius = 0.5 * (high_bound - low_bound)
    spread_ratio = centre / radius
    ratio_now = 1.0 / spread_ratio
    start_vector = rhs * live_mask
    picked = select_columns(coarse_cols, gather_coefficients(build_local(start_vector)))
    amounts = jnp.einsum("sqij,sqjc->sic", coarse_rows, picked, precision=highest)
    slot_rows = jnp.einsum("sjn,sjc->snc", slot_modes, amounts, precision=highest)
    lower_half = slot_rows[:, :half_width]
    upper_half = slot_rows[:, half_width:]
    later_rim = from_behind(lower_half[0], "dom", -1)
    following = jnp.concatenate([lower_half[1:], later_rim[None]], axis=0)
    residual = start_vector - (upper_half - following) * live_mask
    direction = residual / centre
    local_residual = build_local(residual)
    local_direction = local_residual / centre
    solution = jnp.zeros_like(rhs)
    norm_list = []
    for turn_index in range(STEPS):
        solution = solution + direction
        product = jnp.einsum("smn,smc->snc", slot_ops, local_direction, precision=highest)
        local_lower_half = product[:, :half_width]
        local_upper_half = product[:, half_width:]
        prior_upper = from_behind(local_upper_half[-1], "dom", 1)
        later_lower = from_behind(local_lower_half[0], "dom", -1)
        local_following = jnp.concatenate([local_lower_half[1:], later_lower[None]], axis=0)
        mapped = (local_upper_half - local_following) * live_mask
        first_value = (prior_upper - local_lower_half[0]) * ext_live[0]
        local_left_side = jnp.concatenate([first_value[None], mapped[:-1]], axis=0)
        mapped, local_mapped = (mapped, slot_form(local_left_side, mapped))
        wide_picked = select_columns(ext_cols, gather_coefficients(local_mapped))
        wide_amounts = jnp.einsum("sqij,sqjc->sic", ext_blocks, wide_picked, precision=highest)
        spread = jnp.einsum("sjn,sjc->snc", ext_modes, wide_amounts, precision=highest)
        lower_part = spread[:, :half_width]
        upper_part = spread[:, half_width:]
        joined = (upper_part[:-1] - lower_part[1:]) * ext_live[:-1]
        correction = joined[1:]
        local_correction = slot_form(joined[:-1], joined[1:])
        residual = residual - (mapped - correction)
        local_residual = local_residual - (local_mapped - local_correction)
        partial_value = jnp.sum(residual * residual, axis=(0, 1))
        norm_list.append(partial_value)
        if turn_index + 1 < STEPS:
            ratio_next = 1.0 / (2.0 * spread_ratio - ratio_now)
            direction = ratio_next * ratio_now * direction + 2.0 * ratio_next / radius * residual
            local_direction = (
                ratio_next * ratio_now * local_direction
                + 2.0 * ratio_next / radius * local_residual
            )
            ratio_now = ratio_next
    totals = of_everyone(jnp.stack(norm_list), "dom")
    history = jnp.sqrt(totals + epsilon)
    peak_norm = lax.pmax(jnp.max(history, axis=1), "case")
    return (solution, residual, history, peak_norm)


def solution(mesh):
    in_specs = (
        P("dom", None, None),
        P("dom", None, None),
        P("dom", None, None, None),
        P("dom", None),
        P("dom", None),
        P("dom"),
        P("dom", None, "case"),
    )
    out_specs = (P("dom", None, "case"), P("dom", None, "case"), P(None, "case"), P())
    return jax.shard_map(shards, mesh=mesh, in_specs=in_specs, out_specs=out_specs, check_vma=False)
```

profile of v0, /device:TPU:0, one launch (start us, length us, event | category | flops | bytes accessed | tf_op | source)
XLA Modules:
  0.0 526.0 jit_solution(13051343531225521670)
XLA Ops:
  1.4 1.4 broadcast_multiply_fusion
  4.0 16.5 %gather_fusion = bf16[3072,16]{1,0:T(8,128)(2,1)S(1)} fusion(bf16[2,16,1536]{1,2,0:T(8,128)(2,1)S(1)} %copy.58, s32[3072]{0:T(1024)S(1)} %reshape.61), kind=kCustom, calls=%fused_computation | custom fusion | bytes 221184 | tf_op jit(solution)/shard_map/vmap()/gather | solution.py:55
  22.4 9.6 %all-to-all-start = ((bf16[32,2,16,128]{3,1,2,0:T(2,128)(2,1)}), bf16[32,2,16,128]{3,1,2,0:T(2,128)(2,1)S(1)}, u32[]{:S(2)}, u32[]{:S(2)}) async-start(bf16[32,2,16,128]{3,1,2,0:T(2,128)(2,1)} %broadcast_in_dim.52), calls=%async_computation | async-start | bytes 524288 | tf_op jit(solution)/shard_map/all_to_all | solution.py:23
  32.1 8.8 %all-to-all-done = bf16[32,2,16,128]{3,1,2,0:T(2,128)(2,1)S(1)} async-done(((bf16[32,2,16,128]{3,1,2,0:T(2,128)(2,1)}), bf16[32,2,16,128]{3,1,2,0:T(2,128)(2,1)S(1)}, u32[]{:S(2)}, u32[]{:S(2)}) %all-to-all-start) | async-done | bytes 262176 | tf_op jit(solution)/shard_map/all_to_all | solution.py:23
  43.4 1.8 collective-permute-start.1
  45.3 5.1 collective-permute-done.1
  51.2 1.7 fusion.44
  53.4 4.9 collective-permute-start.9
  59.0 5.1 collective-permute-start.7
  64.3 68.2 %gather_fusion.1 = f32[3072,1536]{1,0:T(8,128)} fusion(f32[2,1536,1536]{2,1,0:T(8,128)} %param.7, s32[3072]{0:T(1024)S(1)} %reshape.61), kind=kCustom, calls=%fused_computation.1 | custom fusion | bytes 37773312 | tf_op jit(solution)/shard_map/vmap()/gather | solution.py:54
  132.5 18.7 %copy.65 = f32[2,1536,1536]{1,2,0:T(8,128)} copy(f32[2,1536,1536]{2,1,0:T(8,128)} %bitcast.154) | data formatting | bytes 37748736 | tf_op jit(solution)/shard_map/vmap()/gather | solution.py:54
  151.2 68.1 %gather_fusion.2 = f32[3072,1536]{1,0:T(8,128)} fusion(f32[2,1536,1536]{2,1,0:T(8,128)} %bitcast.147, s32[3072]{0:T(1024)S(1)} %reshape.61), kind=kCustom, calls=%fused_computation.2 | custom fusion | bytes 37773312 | tf_op jit(solution)/shard_map/vmap()/gather | solution.py:54
  219.5 33.0 %fusion.18 = f32[2,1536,128]{2,1,0:T(8,128)S(1)} fusion(f32[2,1536,1536]{2,1,0:T(8,128)} %bitcast.148, f32[2,768,128]{2,1,0:T(8,128)S(1)} %fusion.44, f32[2,768,128]{2,1,0:T(8,128)S(1)} %maximum_negate_fusion.1), kind=kOutput, calls=%fused_computation.29 | convolution fusion | flops 7248543744 | bytes 22020096 | tf_op jit(solution)/shard_map/smn,smc->snc/dot_general | solution.py:115
  252.6 5.1 collective-permute-start.3
  258.1 4.9 collective-permute-done.3
  264.2 4.3 collective-permute-done.10
  270.5 4.6 all-to-all-start.1
  275.8 4.9 collective-permute-start.5
  280.7 3.4 all-to-all-done.1
  284.1 1.2 copy.71
  286.2 1.6 collective-permute-done.4
  287.8 2.4 fusion.99
  293.8 43.9 %fusion.105 = f32[2,1536,128]{2,1,0:T(8,128)S(1)} fusion(f32[2,1536,1536]{2,1,0:T(8,128)} %bitcast.149, f32[2,1536,128]{2,1,0:T(8,128)S(1)} %multiply_add_fusion.1), kind=kOutput, calls=%fused_computation.172 | convolution fusion | flops 7247757312 | bytes 22020096 | tf_op jit(solution)/shard_map/smn,smc->snc/dot_general | solution.py:115
  338.3 4.9 collective-permute-done.11
  343.6 4.8 collective-permute-done.12
  349.8 11.9 %all_to_all.30 = bf16[32,2,16,128]{3,1,2,0:T(2,128)(2,1)S(1)} all-to-all(bf16[32,2,16,128]{3,1,2,0:T(2,128)(2,1)S(1)} %broadcast_in_dim.120), channel_id=1, replica_groups=mesh['dom'=32,'case'=4] {'dom'}, dimensions={0} | all-to-all | bytes 524288 | tf_op jit(solution)/shard_map/all_to_all | solution.py:23
  362.9 2.8 fusion.98
  366.1 1.3 multiply_reduce_fusion.2
  367.3 1.6 fusion.5
  368.9 33.2 %fusion.20 = f32[2,1536,128]{2,1,0:T(8,128)} fusion(f32[2,1536,1536]{2,1,0:T(8,128)S(1)} %bitcast.152, f32[2,1536,128]{2,1,0:T(8,128)} %fusion.5, f32[2,1536,128]{2,1,0:T(8,128)S(1)} %multiply_add_fusion.1), kind=kOutput, calls=%fused_computation.31 | convolution fusion | flops 7248936960 | bytes 23592960 | tf_op jit(solution)/shard_map/smn,smc->snc/dot_general | solution.py:115
  402.1 1.4 slice_bitcast_fusion.2
  403.5 1.8 collective-permute-start.13
  405.3 5.3 %collective-permute-done.13 = f32[768,128]{1,0:T(8,128)S(1)} collective-permute-done((f32[768,128]{1,0:T(8,128)S(1)}, f32[768,128]{1,0:T(8,128)S(1)}, u32[]{:S(2)}, u32[]{:S(2)}) %collective-permute-start.13) | collective-permute-done | bytes 393248 | tf_op jit(solution)/shard_map/ppermute | solution.py:18
  411.0 4.8 collective-permute-done.14
  417.2 11.9 %all_to_all.31 = bf16[32,2,16,128]{3,1,2,0:T(2,128)(2,1)S(1)} all-to-all(bf16[32,2,16,128]{3,1,2,0:T(2,128)(2,1)S(1)} %broadcast_in_dim.123), channel_id=1, replica_groups=mesh['dom'=32,'case'=4] {'dom'}, dimensions={0} | all-to-all | bytes 524288 | tf_op jit(solution)/shard_map/all_to_all | solution.py:23
  430.3 2.4 fusion.97
  433.8 1.7 multiply_reduce_fusion.1
  435.7 32.6 %fusion.9 = f32[2,1536,128]{2,1,0:T(8,128)S(1)} fusion(f32[2,1536,1536]{2,1,0:T(8,128)S(1)} %bitcast.153, f32[2,1536,128]{2,1,0:T(8,128)S(1)} %copy-done.4, f32[2,768,128]{2,1,0:T(8,128)} %get-tuple-element.31, f32[2,768,128]{2,1,0:T(8,128)} %get-tuple-element.30, f32[2,1536,128]{2,1,0:T(8,128)S(1)} %multiply_add_fusion.1, f32[2,768,128]{2,1,0:T(8,128)S(1)} %fusion.40, ...), kind=kOutput, calls=%fused_computation.19 | convolution fusion | flops 7251689472 | bytes 26738688 | tf_op jit(solution)/shard_map/smn,smc->snc/dot_general | solution.py:115
  468.3 1.8 collective-permute-start.15
  470.1 5.3 %collective-permute-done.15 = f32[768,128]{1,0:T(8,128)S(1)} collective-permute-done((f32[768,128]{1,0:T(8,128)S(1)}, f32[768,128]{1,0:T(8,128)S(1)}, u32[]{:S(2)}, u32[]{:S(2)}) %collective-permute-start.15) | collective-permute-done | bytes 393248 | tf_op jit(solution)/shard_map/ppermute | solution.py:18
  475.8 4.8 collective-permute-done.16
  482.7 3.9 all-to-all-start.4
  486.6 8.9 %all-to-all-done.4 = bf16[32,2,16,128]{3,1,2,0:T(2,128)(2,1)S(1)} async-done(((bf16[32,2,16,128]{3,1,2,0:T(2,128)(2,1)}), bf16[32,2,16,128]{3,1,2,0:T(2,128)(2,1)S(1)}, u32[]{:S(2)}, u32[]{:S(2)}) %all-to-all-start.4) | async-done | bytes 262176 | tf_op jit(solution)/shard_map/all_to_all | solution.py:23
  496.7 2.4 fusion.96
  499.3 1.2 copy-done.1
  501.2 1.7 multiply_reduce_fusion
  502.9 11.0 %all_to_all.32 = f32[32,4,128]{2,1,0:T(4,128)S(1)} all-to-all(f32[32,4,128]{2,1,0:T(4,128)S(1)} %broadcast_in_dim.127), channel_id=1, replica_groups=mesh['dom'=32,'case'=4] {'dom'}, dimensions={0} | all-to-all | bytes 131072 | tf_op jit(solution)/shard_map/all_to_all | solution.py:23
  514.7 11.0 %pmax.7 = f32[4]{0:T(128)} all-reduce(f32[4]{0:T(128)S(1)} %get-tuple-element.4), channel_id=1, replica_groups=mesh['dom'=32,'case'=4] {'case'}, use_global_device_ids=true, to_apply=%region_6.0 | all-reduce | flops 4 | bytes 32 | tf_op jit(solution)/shard_map/pmax | solution.py:147
  (163 shorter events, 30.8 us)
Async XLA Ops:
  1.4 2.3 copy-start.24
  2.8 1.2 copy-start.25
  3.6 16.9 %collective-permute-start = (f32[768,128]{1,0:T(8,128)}, f32[768,128]{1,0:T(8,128)S(1)}, u32[]{:S(2)}, u32[]{:S(2)}) collective-permute-start(f32[768,128]{1,0:T(8,128)} %get-tuple-element.39), channel_id=1, source_target_pairs={{124,0},{0,4},{4,8},{8,12},{12,16},{16,20},{20,24},{24,28},{28,32}... | collective-permute-start | bytes 1179656 | tf_op jit(solution)/shard_map/ppermute | solution.py:18
  20.6 11.4 %copy-start.17 = (f32[2,8,16,16]{3,2,1,0:T(8,128)S(1)}, f32[2,8,16,16]{3,2,1,0:T(8,128)}, u32[]{:S(2)}) copy-start(f32[2,8,16,16]{3,2,1,0:T(8,128)} %param.9) | copy-start | bytes 49156
  20.6 20.6 %copy-start.26 = (s32[2,8]{1,0:T(2,128)S(1)}, s32[2,8]{1,0:T(2,128)}, u32[]{:S(2)}) copy-start(s32[2,8]{1,0:T(2,128)} %param.10) | copy-start | bytes 196
  22.4 18.5 %all-to-all-start = ((bf16[32,2,16,128]{3,1,2,0:T(2,128)(2,1)}), bf16[32,2,16,128]{3,1,2,0:T(2,128)(2,1)S(1)}, u32[]{:S(2)}, u32[]{:S(2)}) async-start(bf16[32,2,16,128]{3,1,2,0:T(2,128)(2,1)} %broadcast_in_dim.52), calls=%async_computation | async-start | bytes 524288 | tf_op jit(solution)/shard_map/all_to_all | solution.py:23
  41.8 3.4 copy-start.27
  43.4 7.1 %collective-permute-start.1 = (f32[768,128]{1,0:T(8,128)S(1)}, f32[768,128]{1,0:T(8,128)S(1)}, u32[]{:S(2)}, u32[]{:S(2)}) collective-permute-start(f32[768,128]{1,0:T(8,128)S(1)} %get-tuple-element.29), channel_id=1, source_target_pairs={{4,0},{8,4},{12,8},{16,12},{20,16},{24,20},{28,24},{32,28},{36,32}... | collective-permute-start | bytes 1179656 | tf_op jit(solution)/shard_map/ppermute | solution.py:18
  52.9 166.5 %collective-permute-start.2 = (f32[768,128]{1,0:T(8,128)S(1)}, f32[768,128]{1,0:T(8,128)S(1)}, u32[]{:S(2)}, u32[]{:S(2)}) collective-permute-start(f32[768,128]{1,0:T(8,128)S(1)} %get-tuple-element.37), channel_id=1, source_target_pairs={{124,0},{0,4},{4,8},{8,12},{12,16},{16,20},{20,24},{24,28},{28,32}... | collective-permute-start | bytes 1179656 | tf_op jit(solution)/shard_map/ppermute | solution.py:18
  53.4 165.9 %collective-permute-start.9 = (s32[9]{0:T(128)S(1)}, s32[9]{0:T(128)S(1)}, u32[]{:S(2)}, u32[]{:S(2)}) collective-permute-start(s32[9]{0:T(128)S(1)} %get-tuple-element.46), channel_id=1, source_target_pairs={{4,0},{8,4},{12,8},{16,12},{20,16},{24,20},{28,24},{32,28},{36,32}... | collective-permute-start | bytes 116 | tf_op jit(solution)/shard_map/ppermute | solution.py:18
  58.3 161.0 %collective-permute-start.8 = (s32[9]{0:T(128)S(1)}, s32[9]{0:T(128)S(1)}, u32[]{:S(2)}, u32[]{:S(2)}) collective-permute-start(s32[9]{0:T(128)S(1)} %get-tuple-element.45), channel_id=1, source_target_pairs={{124,0},{0,4},{4,8},{8,12},{12,16},{16,20},{20,24},{24,28},{28,32}... | collective-permute-start | bytes 116 | tf_op jit(solution)/shard_map/ppermute | solution.py:18
  59.0 226.5 %collective-permute-start.7 = (f32[8,16,16]{2,1,0:T(8,128)}, f32[8,16,16]{2,1,0:T(8,128)S(1)}, u32[]{:S(2)}, u32[]{:S(2)}) collective-permute-start(f32[8,16,16]{2,1,0:T(8,128)} %get-tuple-element.42), channel_id=1, source_target_pairs={{4,0},{8,4},{12,8},{16,12},{20,16},{24,20},{28,24},{32,28},{36,32}... | collective-permute-start | bytes 24584 | tf_op jit(solution)/shard_map/ppermute | solution.py:18
  64.0 221.5 %collective-permute-start.6 = (f32[8,16,16]{2,1,0:T(8,128)}, f32[8,16,16]{2,1,0:T(8,128)S(1)}, u32[]{:S(2)}, u32[]{:S(2)}) collective-permute-start(f32[8,16,16]{2,1,0:T(8,128)} %get-tuple-element.41), channel_id=1, source_target_pairs={{124,0},{0,4},{4,8},{8,12},{12,16},{16,20},{20,24},{24,28},{28,32}... | collective-permute-start | bytes 24584 | tf_op jit(solution)/shard_map/ppermute | solution.py:18
  219.4 33.0 %copy-start.6 = (f32[2,768,128]{2,1,0:T(8,128)}, f32[2,768,128]{2,1,0:T(8,128)S(1)}, u32[]{:S(2)}) copy-start(f32[2,768,128]{2,1,0:T(8,128)S(1)} %maximum_negate_fusion.1) | copy-start | bytes 2359300
  252.6 11.6 %copy-start.18 = (f32[1,768,128]{2,1,0:T(8,128)}, f32[1,768,128]{2,1,0:T(8,128)S(1)}, u32[]{:S(2)}) copy-start(f32[1,768,128]{2,1,0:T(8,128)S(1)} %get-tuple-element.27) | copy-start | bytes 1179652
  252.6 10.4 %collective-permute-start.3 = (f32[768,128]{1,0:T(8,128)S(1)}, f32[768,128]{1,0:T(8,128)S(1)}, u32[]{:S(2)}, u32[]{:S(2)}) collective-permute-start(f32[768,128]{1,0:T(8,128)S(1)} %get-tuple-element.26), channel_id=1, source_target_pairs={{4,0},{8,4},{12,8},{16,12},{20,16},{24,20},{28,24},{32,28},{36,32}... | collective-permute-start | bytes 1179656 | tf_op jit(solution)/shard_map/ppermute | solution.py:18
  257.9 10.6 %collective-permute-start.10 = (f32[768,128]{1,0:T(8,128)S(1)}, f32[768,128]{1,0:T(8,128)S(1)}, u32[]{:S(2)}, u32[]{:S(2)}) collective-permute-start(f32[768,128]{1,0:T(8,128)S(1)} %get-tuple-element.25), channel_id=1, source_target_pairs={{124,0},{0,4},{4,8},{8,12},{12,16},{16,20},{20,24},{24,28},{28,32}... | collective-permute-start | bytes 1179656 | tf_op jit(solution)/shard_map/ppermute | solution.py:18
  264.2 4.6 copy-start.2
  270.5 13.5 %all-to-all-start.1 = ((bf16[32,2,16,128]{3,1,2,0:T(2,128)(2,1)}), bf16[32,2,16,128]{3,1,2,0:T(2,128)(2,1)}, u32[]{:S(2)}, u32[]{:S(2)}) async-start(bf16[32,2,16,128]{3,1,2,0:T(2,128)(2,1)} %broadcast_in_dim.117), calls=%async_computation.1 | async-start | bytes 524288 | tf_op jit(solution)/shard_map/all_to_all | solution.py:23
  275.8 10.4 %collective-permute-start.5 = (bf16[16,1536]{1,0:T(8,128)(2,1)}, bf16[16,1536]{1,0:T(8,128)(2,1)}, u32[]{:S(2)}, u32[]{:S(2)}) collective-permute-start(bf16[16,1536]{1,0:T(8,128)(2,1)} %get-tuple-element.44), channel_id=1, source_target_pairs={{4,0},{8,4},{12,8},{16,12},{20,16},{24,20},{28,24},{32,28},{36,32}... | collective-permute-start | bytes 147464 | tf_op jit(solution)/shard_map/ppermute | solution.py:18
  280.7 7.2 %collective-permute-start.4 = (bf16[16,1536]{1,0:T(8,128)(2,1)}, bf16[16,1536]{1,0:T(8,128)(2,1)}, u32[]{:S(2)}, u32[]{:S(2)}) collective-permute-start(bf16[16,1536]{1,0:T(8,128)(2,1)} %get-tuple-element.43), channel_id=1, source_target_pairs={{124,0},{0,4},{4,8},{8,12},{12,16},{16,20},{20,24},{24,28},{28,32}... | collective-permute-start | bytes 147464 | tf_op jit(solution)/shard_map/ppermute | solution.py:18
  291.3 1.1 copy-start.3
  291.3 1.4 copy-start.7
  291.3 2.1 copy-start.9
  291.8 1.9 copy-start.10
  291.8 74.2 %copy-start.12 = (f32[2,768,128]{2,1,0:T(8,128)}, f32[2,768,128]{2,1,0:T(8,128)S(1)}, u32[]{:S(2)}) copy-start(f32[2,768,128]{2,1,0:T(8,128)S(1)} %get-tuple-element.7) | copy-start | bytes 2359300
  293.8 75.1 %slice-start = ((s8[18874368]{0:T(1024)(128)(4,1)}), s8[4194304]{0:T(1024)(128)(4,1)S(1)}, s32[]{:S(2)}) async-start(s8[18874368]{0:T(1024)(128)(4,1)} %bitcast.150), calls=%async_computation.6 | async-start | bytes 8388608
  293.8 75.1 %slice-start.1 = ((s8[18874368]{0:T(1024)(128)(4,1)}), s8[4194304]{0:T(1024)(128)(4,1)S(1)}, s32[]{:S(2)}) async-start(s8[18874368]{0:T(1024)(128)(4,1)} %bitcast.150), calls=%async_computation.7 | async-start | bytes 8388608
  337.6 31.3 %slice-start.2 = ((s8[18874368]{0:T(1024)(128)(4,1)}), s8[4194304]{0:T(1024)(128)(4,1)S(1)}, s32[]{:S(2)}) async-start(s8[18874368]{0:T(1024)(128)(4,1)} %bitcast.150), calls=%async_computation.8 | async-start | bytes 8388608
  337.7 5.5 %collective-permute-start.11 = (f32[768,128]{1,0:T(8,128)S(1)}, f32[768,128]{1,0:T(8,128)S(1)}, u32[]{:S(2)}, u32[]{:S(2)}) collective-permute-start(f32[768,128]{1,0:T(8,128)S(1)} %get-tuple-element.23), channel_id=1, source_target_pairs={{4,0},{8,4},{12,8},{16,12},{20,16},{24,20},{28,24},{32,28},{36,32}... | collective-permute-start | bytes 1179656 | tf_op jit(solution)/shard_map/ppermute | solution.py:18
  337.9 10.5 %collective-permute-start.12 = (f32[768,128]{1,0:T(8,128)S(1)}, f32[768,128]{1,0:T(8,128)S(1)}, u32[]{:S(2)}, u32[]{:S(2)}) collective-permute-start(f32[768,128]{1,0:T(8,128)S(1)} %get-tuple-element.22), channel_id=1, source_target_pairs={{124,0},{0,4},{4,8},{8,12},{12,16},{16,20},{20,24},{24,28},{28,32}... | collective-permute-start | bytes 1179656 | tf_op jit(solution)/shard_map/ppermute | solution.py:18
  362.2 6.7 %slice-start.3 = ((s8[18874368]{0:T(1024)(128)(4,1)}), s8[4194304]{0:T(1024)(128)(4,1)S(1)}, s32[]{:S(2)}) async-start(s8[18874368]{0:T(1024)(128)(4,1)} %bitcast.150), calls=%async_computation.9 | async-start | bytes 8388608
  366.0 1.3 copy-start.11
  366.1 2.9 slice-start.4
  402.1 8.5 %copy-start.5 = (f32[2,1536,128]{2,1,0:T(8,128)S(1)}, f32[2,1536,128]{2,1,0:T(8,128)}, u32[]{:S(2)}) copy-start(f32[2,1536,128]{2,1,0:T(8,128)} %fusion.20) | copy-start | bytes 4718596
  403.5 7.1 %collective-permute-start.13 = (f32[768,128]{1,0:T(8,128)S(1)}, f32[768,128]{1,0:T(8,128)S(1)}, u32[]{:S(2)}, u32[]{:S(2)}) collective-permute-start(f32[768,128]{1,0:T(8,128)S(1)} %get-tuple-element.20), channel_id=1, source_target_pairs={{4,0},{8,4},{12,8},{16,12},{20,16},{24,20},{28,24},{32,28},{36,32}... | collective-permute-start | bytes 1179656 | tf_op jit(solution)/shard_map/ppermute | solution.py:18
  405.3 10.5 %collective-permute-start.14 = (f32[768,128]{1,0:T(8,128)S(1)}, f32[768,128]{1,0:T(8,128)S(1)}, u32[]{:S(2)}, u32[]{:S(2)}) collective-permute-start(f32[768,128]{1,0:T(8,128)S(1)} %get-tuple-element.19), channel_id=1, source_target_pairs={{124,0},{0,4},{4,8},{8,12},{12,16},{16,20},{20,24},{24,28},{28,32}... | collective-permute-start | bytes 1179656 | tf_op jit(solution)/shard_map/ppermute | solution.py:18
  416.1 13.0 %copy-start.16 = (f32[2,768,128]{2,1,0:T(8,128)}, f32[2,768,128]{2,1,0:T(8,128)S(1)}, u32[]{:S(2)}) copy-start(f32[2,768,128]{2,1,0:T(8,128)S(1)} %maximum_negate_fusion.4) | copy-start | bytes 2359300
  432.7 1.1 copy-start.14
  433.8 1.8 copy-start.4
  468.2 12.4 %copy-start = (f32[2,1536,128]{2,1,0:T(8,128)}, f32[2,1536,128]{2,1,0:T(8,128)S(1)}, u32[]{:S(2)}) copy-start(f32[2,1536,128]{2,1,0:T(8,128)S(1)} %fusion.9) | copy-start | bytes 4718596
  468.3 7.1 %collective-permute-start.15 = (f32[768,128]{1,0:T(8,128)S(1)}, f32[768,128]{1,0:T(8,128)S(1)}, u32[]{:S(2)}, u32[]{:S(2)}) collective-permute-start(f32[768,128]{1,0:T(8,128)S(1)} %get-tuple-element.17), channel_id=1, source_target_pairs={{4,0},{8,4},{12,8},{16,12},{20,16},{24,20},{28,24},{32,28},{36,32}... | collective-permute-start | bytes 1179656 | tf_op jit(solution)/shard_map/ppermute | solution.py:18
  470.1 10.5 %collective-permute-start.16 = (f32[768,128]{1,0:T(8,128)S(1)}, f32[768,128]{1,0:T(8,128)S(1)}, u32[]{:S(2)}, u32[]{:S(2)}) collective-permute-start(f32[768,128]{1,0:T(8,128)S(1)} %get-tuple-element.16), channel_id=1, source_target_pairs={{124,0},{0,4},{4,8},{8,12},{12,16},{16,20},{20,24},{24,28},{28,32}... | collective-permute-start | bytes 1179656 | tf_op jit(solution)/shard_map/ppermute | solution.py:18
  482.7 12.8 %all-to-all-start.4 = ((bf16[32,2,16,128]{3,1,2,0:T(2,128)(2,1)}), bf16[32,2,16,128]{3,1,2,0:T(2,128)(2,1)S(1)}, u32[]{:S(2)}, u32[]{:S(2)}) async-start(bf16[32,2,16,128]{3,1,2,0:T(2,128)(2,1)} %broadcast_in_dim.126), calls=%async_computation.4 | async-start | bytes 524288 | tf_op jit(solution)/shard_map/all_to_all | solution.py:23
  499.1 1.4 copy-start.1
  499.1 1.6 copy-start.13
  499.1 1.8 copy-start.15
  499.1 2.1 copy-start.20
  (5 other events, 4.5 us)
where the time goes:
time: 537 us; the launch traced here: 526 us
  local copies, waits for them, and re-layouts  189 us (35%)
  matrix products  162 us (30%)
  waiting for transfers between devices  67.1 us (12%)
  blocking collectives  45.9 us (9%)
  starting transfers between devices  44.5 us (8%)
  other arithmetic  15.6 us (3%)
    gather x3, local copies, waits for them, and re-layouts, shards(): matrix[ordering].T[ordering]  155 us
    dot_general x4, matrix products, shards(): jnp.einsum('smn,smc->snc', slot_ops, local_direction, precision=highest)  143 us
    ppermute x17, waiting for transfers between devices, from_behind(): return lax.ppermute(block, axis, route)  45.9 us
    all_to_all x3, blocking collectives, copy_for_each(): lax.all_to_all(jnp.broadcast_to(value[None], (size, *value.shape)), axis,...  34.9 us
    ppermute x17, starting transfers between devices, from_behind(): return lax.ppermute(block, axis, route)  26.5 us
    all_to_all x3, waiting for transfers between devices, copy_for_each(): lax.all_to_all(jnp.broadcast_to(value[None], (size, *value.shape)), axis,...  21.1 us
    all_to_all x3, starting transfers between devices, copy_for_each(): lax.all_to_all(jnp.broadcast_to(value[None], (size, *value.shape)), axis,...  18.1 us
    gather x3, local copies, waits for them, and re-layouts, shards(): block_rows[:, ordering]  16.7 us
  transfers between devices with their start and end apart: 20, of which 13 were waited for; matrix products, arithmetic and copies ran while one was open for 40% of the time, Pallas kernels for 0%

commit v1 on v0

v1 whole, which is shorter than its diff:
```python
import jax
import jax.numpy as jnp
from jax import lax
from jax.experimental import pallas as pl
from jax.experimental.pallas import tpu as pltpu
from jax.sharding import PartitionSpec as P

STEPS = 4

low_bound = 2.0
high_bound = 14.0
epsilon = 1e-06
f32 = jnp.float32
bf16 = jnp.bfloat16
BLK = 256
VMEM = pl.BlockSpec(memory_space=pltpu.VMEM)
SMEM = pl.BlockSpec(memory_space=pltpu.SMEM)
ANY = pl.BlockSpec(memory_space=pl.ANY)
PARAMS = pltpu.CompilerParams(vmem_limit_bytes=40 * 1024 * 1024)


def from_behind(block, axis, distance):
    count = lax.axis_size(axis)
    route = [((i - distance) % count, i) for i in range(count)]
    return lax.ppermute(block, axis, route)


def dot(a, b):
    return jnp.dot(a, b, preferred_element_type=f32)


def split(value):
    high = value.astype(bf16)
    low = (value - high.astype(f32)).astype(bf16)
    return high, low


def slot_modes_kernel(modes_ref, perm_ref, left_ref, right_ref, to_next_ref, to_prior_ref):
    count, rows, width = modes_ref.shape
    half = width // 2
    for s in range(count):
        for at in range(0, width, BLK):
            one_hot = (
                lax.broadcasted_iota(jnp.int32, (width, BLK), 0) == perm_ref[s : s + 1, at : at + BLK]
            ).astype(f32).astype(bf16)
            part = dot(modes_ref[s], one_hot).astype(bf16)
            if at < half:
                left_ref[s, :, at : at + BLK] = part
                if s == 0:
                    to_prior_ref[:, at : at + BLK] = part
            else:
                right_ref[s, :, at - half : at - half + BLK] = part
                if s == count - 1:
                    to_next_ref[:, at - half : at - half + BLK] = part


def slot_modes(modes, row_perm):
    count, rows, width = modes.shape
    half = width // 2
    side = jax.ShapeDtypeStruct((count, rows, half), bf16)
    rim = jax.ShapeDtypeStruct((rows, half), bf16)
    return pl.pallas_call(
        slot_modes_kernel,
        out_shape=(side, side, rim, rim),
        in_specs=[VMEM, VMEM],
        out_specs=[VMEM] * 4,
        compiler_params=PARAMS,
        name="slot_modes",
    )(modes, row_perm)


def slot_op_kernel(ops_ref, perm_ref, out_ref, diag_ref, cols_done, one_hot, diag_row):
    width = one_hot.shape[0]
    blocks = width // BLK
    at = pl.program_id(0)

    @pl.when(at == 0)
    def _():
        for k in range(blocks):
            one_hot[k * BLK : (k + 1) * BLK, :] = (
                lax.broadcasted_iota(jnp.int32, (BLK, width), 0) + k * BLK == perm_ref[...]
            ).astype(f32).astype(bf16)
        diag_row[...] = jnp.zeros_like(diag_row)

    @pl.when(at < blocks)
    def _():
        block = ops_ref[0]
        on_diag = lax.broadcasted_iota(jnp.int32, (BLK, width), 0) + at * BLK == (
            lax.broadcasted_iota(jnp.int32, (BLK, width), 1)
        )
        diag_row[0:1, :] += jnp.sum(jnp.where(on_diag, block, 0.0), axis=0, keepdims=True)
        rest = jnp.where(on_diag, 0.0, block).astype(bf16)
        rows = pl.ds(pl.multiple_of(at * BLK, BLK), BLK)
        cols_done[rows, :] = dot(rest, one_hot[...]).astype(bf16)

    @pl.when(at >= blocks)
    def _():
        place = pl.multiple_of((at - blocks) * BLK, BLK)
        perm_part = perm_ref[:, pl.ds(place, BLK)].astype(f32)
        owner = jnp.transpose(jnp.broadcast_to(perm_part, (128, BLK)))
        total = jnp.zeros((BLK, 128), f32)
        pieces = []
        for k in range(0, width, 128):
            here = (lax.broadcasted_iota(jnp.int32, (BLK, 128), 1) + k).astype(f32) == owner
            pieces.append(here.astype(f32).astype(bf16))
            total += jnp.where(here, diag_row[0:1, k : k + 128], 0.0)
        out_ref[...] = dot(jnp.concatenate(pieces, axis=1), cols_done[...]).astype(bf16)
        diag_ref[...] = jnp.broadcast_to(jnp.sum(total, axis=1, keepdims=True), (BLK, 128))


def slot_op(dual_ops, perm_row, which):
    width = dual_ops.shape[1]
    blocks = width // BLK
    return pl.pallas_call(
        slot_op_kernel,
        grid=(2 * blocks,),
        out_shape=(
            jax.ShapeDtypeStruct((width, width), bf16),
            jax.ShapeDtypeStruct((width, 128), f32),
        ),
        in_specs=[
            pl.BlockSpec((1, BLK, width), lambda i: (which, jnp.minimum(i, blocks - 1), 0)),
            pl.BlockSpec((1, width), lambda i: (0, 0)),
        ],
        out_specs=[
            pl.BlockSpec((BLK, width), lambda i: (jnp.maximum(i - blocks, 0), 0)),
            pl.BlockSpec((BLK, 128), lambda i: (jnp.maximum(i - blocks, 0), 0)),
        ],
        scratch_shapes=[
            pltpu.VMEM((width, width), bf16),
            pltpu.VMEM((width, width), bf16),
            pltpu.VMEM((8, width), f32),
        ],
        compiler_params=PARAMS,
        cost_estimate=pl.CostEstimate(
            flops=4 * width**3, bytes_accessed=6 * width * width, transcendentals=0
        ),
        name="slot_op",
    )(dual_ops, perm_row)


def alive(size, rows):
    return lax.broadcasted_iota(jnp.int32, (rows, 128), 0) < size


def partial_coefficients(rows_ref, shares, part_ref):
    modes = part_ref.shape[1]
    sums = []
    for e, share in enumerate(shares):
        if share is None:
            sums.append(jnp.zeros((2 * modes, 128), f32))
            continue
        high, low = split(share)
        both = dot(rows_ref[e], jnp.concatenate([high, low], axis=1))
        sums.append(both[:, :128] + both[:, 128:])
    part_ref[0] = sums[0][:modes]
    part_ref[1] = sums[0][modes:] + sums[1][:modes]
    part_ref[2] = sums[1][modes:] + sums[2][:modes]
    part_ref[3] = sums[2][modes:]


def start_kernel(
    sizes_ref, left_ref, right_ref, prior_ref, next_ref, rhs_ref, rows_ref, cols_ref, part_ref
):
    half = rhs_ref.shape[1]
    pairs = [
        (prior_ref[...], left_ref[0]),
        (right_ref[0], left_ref[1]),
        (right_ref[1], next_ref[...]),
    ]
    for e, (above, below) in enumerate(pairs):
        stack = jnp.concatenate([above.astype(f32), -below.astype(f32)], axis=0)
        rows_ref[e] = stack.astype(bf16)
        cols_ref[e] = jnp.transpose(jnp.concatenate([stack, stack], axis=0)).astype(bf16)
    shares = [None]
    for e in range(2):
        shares.append(jnp.where(alive(sizes_ref[e + 1], half), -rhs_ref[e], 0.0))
    partial_coefficients(rows_ref, shares, part_ref)


def start(sizes, left, right, prior, following, rhs):
    half = rhs.shape[1]
    modes = left.shape[1]
    return pl.pallas_call(
        start_kernel,
        out_shape=(
            jax.ShapeDtypeStruct((3, 2 * modes, half), bf16),
            jax.ShapeDtypeStruct((3, half, 4 * modes), bf16),
            jax.ShapeDtypeStruct((4, modes, 128), f32),
        ),
        in_specs=[SMEM] + [VMEM] * 5,
        out_specs=[VMEM] * 3,
        compiler_params=PARAMS,
        name="start",
    )(sizes, left, right, prior, following, rhs)


def step_kernel(first, last, old, new, *refs):
    refs = list(refs)
    take = lambda n: [refs.pop(0) for _ in range(n)]
    sizes_ref, own_ref, other_ref = take(3)
    all_ref, blocks_ref, rows_ref, cols_ref = take(4)
    if first:
        rhs_ref, from_prior_ref = take(2)
    else:
        wa_ref, wb_ref, wc_ref, from_prior_ref, from_next_ref, res_ref = take(6)
    if not last:
        if not first:
            dir_ref, sol_ref = take(2)
        op_refs = take(2)
        diag_refs = take(2)
    res_out, norm_out = take(2)
    if not last:
        dir_out, sol_out, wa_out, wb_out, wc_out, part_out = take(6)
    picked = take(1)[0]
    if not last:
        held, slots, sems = take(3)
        copies = []
        for s in range(2):
            copies.append(pltpu.make_async_copy(op_refs[s], held.at[s], sems.at[s]))
            copies[-1].start()
    half = res_out.shape[1]
    modes = all_ref.shape[1]
    subs, _, width = blocks_ref.shape
    count = width // modes
    amounts = []
    for s in range(subs):
        for q in range(count):
            value = all_ref[own_ref[s * count + q]] + all_ref[other_ref[s * count + q]]
            picked[s, q * modes : (q + 1) * modes, :] = value.astype(bf16)
        high, low = split(blocks_ref[s])
        both = dot(jnp.concatenate([high, low], axis=0), picked[s])
        amounts.append(both[:modes] + both[modes:])
    total = jnp.zeros((1, 128), f32)
    live = [alive(sizes_ref[e], half) for e in range(3)]
    for e in range(3):
        high, low = split(jnp.concatenate([amounts[e], amounts[e + 1]], axis=0))
        spread = dot(cols_ref[e], jnp.concatenate([high, low], axis=0))
        if first:
            field = -from_prior_ref[...] if e == 0 else -rhs_ref[e - 1]
            residual = jnp.where(live[e], spread - field, 0.0)
        else:
            field = (wa_ref, wb_ref, wc_ref)[e][...]
            if e == 0:
                field = field + from_prior_ref[...]
            if e == 2:
                field = field + from_next_ref[...]
            residual = res_ref[e] + (jnp.where(live[e], spread, 0.0) - field)
        if last:
            if e > 0:
                res_out[e - 1] = residual
        else:
            res_out[e] = residual
        if e > 0:
            total += jnp.sum(residual * residual, axis=0, keepdims=True)
        if not last:
            direction = new * residual
            if not first:
                direction = direction + old * dir_ref[e]
            dir_out[e] = direction
            if e > 0:
                sol_out[e - 1] = direction if first else sol_ref[e - 1] + direction
            low_form = direction.astype(bf16)
            if e < 2:
                slots[e, :half] = -low_form
            if e > 0:
                slots[e - 1, half:] = low_form
    norm_out[...] = total
    if last:
        return
    sides = []
    for s in range(2):
        copies[s].wait()
        left_at, right_at = s, s + 1
        for side, (e, sign) in enumerate(((left_at, -1.0), (right_at, 1.0))):
            parts = []
            for at in range(0, half, BLK):
                here = slice(side * half + at, side * half + at + BLK)
                exact = diag_refs[s][here, :] * dir_out[e, at : at + BLK, :]
                parts.append(dot(held[s, here, :], slots[s]) + sign * exact)
            sides.append(jnp.concatenate(parts, axis=0))
    shares = [
        jnp.where(live[0], -sides[0], 0.0),
        jnp.where(live[1], sides[1] - sides[2], 0.0),
        jnp.where(live[2], sides[3], 0.0),
    ]
    wa_out[...], wb_out[...], wc_out[...] = shares
    partial_coefficients(rows_ref, shares, part_out)


def step(first, last, old, new, ints, constants, fields, ops=()):
    half, lanes = fields[-1].shape[-2:]
    modes = constants[0].shape[1]
    field = jax.ShapeDtypeStruct((half, lanes), f32)
    three = jax.ShapeDtypeStruct((3, half, lanes), f32)
    two = jax.ShapeDtypeStruct((2, half, lanes), f32)
    norm = jax.ShapeDtypeStruct((1, lanes), f32)
    subs, _, width = constants[1].shape
    out = [two if last else three, norm]
    scratch = [pltpu.VMEM((subs, width, lanes), bf16)]
    specs = [SMEM] * len(ints) + [VMEM] * (len(constants) + len(fields))
    if not last:
        part = jax.ShapeDtypeStruct((4, modes, lanes), f32)
        out += [three, two, field, field, field, part]
        scratch += [
            pltpu.VMEM((2, 2 * half, 2 * half), bf16),
            pltpu.VMEM((2, 2 * half, lanes), bf16),
            pltpu.SemaphoreType.DMA((2,)),
        ]
        specs += [ANY, ANY, VMEM, VMEM]

    def body(*refs):
        step_kernel(first, last, old, new, *refs)

    return pl.pallas_call(
        body,
        out_shape=tuple(out),
        in_specs=specs,
        out_specs=[VMEM] * len(out),
        scratch_shapes=scratch,
        compiler_params=PARAMS,
        cost_estimate=pl.CostEstimate(
            flops=10**9, bytes_accessed=15 * 10**6, transcendentals=0
        ),
        name="last_step" if last else "step",
    )(*ints, *constants, *fields, *ops)


def to_everyone(value, axis):
    size = lax.psum(1, axis)
    return lax.all_to_all(
        jnp.broadcast_to(value[None], (size, *value.shape)), axis, 0, 0, tiled=True
    )


def shards(dual_ops, modes, coarse_rows, coarse_cols, row_perm, iface_size, rhs):
    doms = lax.axis_size("dom")
    count, blocks, rows, _ = coarse_rows.shape
    flat = jnp.swapaxes(coarse_rows, 1, 2).reshape(count, rows, blocks * rows)
    whole = jnp.concatenate([coarse_cols, iface_size[:, None]], axis=1).astype(f32)
    whole = jnp.pad(whole, ((0, 0), (0, blocks * rows - whole.shape[1])))
    pack = jnp.concatenate([flat, jnp.broadcast_to(whole[:, None], (count, 8, blocks * rows))], axis=1)
    prior_pack = from_behind(pack[-1], "dom", 1)
    next_pack = from_behind(pack[0], "dom", -1)
    prior_rhs = from_behind(rhs[-1], "dom", 1)
    left, right, to_next, to_prior = slot_modes(modes, row_perm)
    prior_modes = from_behind(to_next, "dom", 1)
    next_modes = from_behind(to_prior, "dom", -1)
    ext = jnp.concatenate([prior_pack[None], pack, next_pack[None]], axis=0)
    ext_blocks = ext[:, :rows]
    ext_whole = ext[:, rows].astype(jnp.int32)
    cols = ext_whole[:, :blocks].reshape(-1)
    sizes = ext_whole[:3, blocks]
    odd = cols % 2
    own = 4 * (cols // 2) + 1 + odd
    other = (own + 4 * odd - 2) % (4 * doms)
    ints = (sizes, own, other)

    ops_a, diag_a = slot_op(dual_ops, row_perm[0:1], 0)
    row_forms, col_forms, part = start(sizes, left, right, prior_modes, next_modes, rhs)
    second_perm, _ = lax.optimization_barrier((row_perm[1:2], part))
    everything = to_everyone(part, "dom").reshape(4 * doms, rows, -1)
    ops_b, diag_b = slot_op(dual_ops, second_perm, 1)
    ops = (ops_a, ops_b, diag_a, diag_b)

    centre = 0.5 * (high_bound + low_bound)
    radius = 0.5 * (high_bound - low_bound)
    spread_ratio = centre / radius
    ratio_now = 1.0 / spread_ratio
    norms = []
    old, new = 0.0, 1.0 / centre
    constants = (everything, ext_blocks, row_forms, col_forms)
    residual, _, direction, solution, wa, wb, wc, part = step(
        True, False, old, new, ints, constants, (rhs, prior_rhs), ops
    )
    for turn in range(STEPS):
        from_prior = from_behind(wc, "dom", 1)
        from_next = from_behind(wa, "dom", -1)
        everything = to_everyone(part, "dom").reshape(4 * doms, rows, -1)
        constants = (everything, ext_blocks, row_forms, col_forms)
        fields = (wa, wb, wc, from_prior, from_next, residual)
        if turn + 1 < STEPS:
            ratio_next = 1.0 / (2.0 * spread_ratio - ratio_now)
            old, new = ratio_next * ratio_now, 2.0 * ratio_next / radius
            ratio_now = ratio_next
            residual, norm, direction, solution, wa, wb, wc, part = step(
                False, False, old, new, ints, constants, fields + (direction, solution), ops
            )
        else:
            residual, norm = step(False, True, 0.0, 0.0, ints, constants, fields)
        norms.append(norm)
    sums = to_everyone(jnp.concatenate(norms, axis=0), ("dom", "case"))
    cases = lax.axis_size("case")
    totals = jnp.sum(sums.reshape(doms, cases, STEPS, -1), axis=0)
    whole_history = jnp.sqrt(totals + epsilon)
    history = lax.dynamic_index_in_dim(whole_history, lax.axis_index("case"), 0, keepdims=False)
    peak_norm = jnp.max(whole_history, axis=(0, 2))
    return (solution, residual, history, peak_norm)


def solution(mesh):
    in_specs = (
        P("dom", None, None),
        P("dom", None, None),
        P("dom", None, None, None),
        P("dom", None),
        P("dom", None),
        P("dom"),
        P("dom", None, "case"),
    )
    out_specs = (P("dom", None, "case"), P("dom", None, "case"), P(None, "case"), P())
    return jax.shard_map(shards, mesh=mesh, in_specs=in_specs, out_specs=out_specs, check_vma=False)
```

time: 537 us -> 291 us (0.54); the launches traced: 526 us -> 288 us
  matrix products: 162 us -> 0 us
  local copies, waits for them, and re-layouts: 189 us -> 73.8 us
  Pallas kernels: 0 us -> 71.9 us
  blocking collectives: 45.9 us -> 0 us
  starting transfers between devices: 44.5 us -> 63.3 us
  other arithmetic: 15.6 us -> 1.51 us
  waiting for transfers between devices: 67.1 us -> 76.3 us
    gather x6 -> x0, local copies, waits for them, and re-layouts: 172 us -> none  [the longest x3 155 us: shards(): matrix[ordering].T[ordering]]
    dot_general x24 -> x0, matrix products: 162 us -> none  [the longest x4 143 us: shards(): jnp.einsum('smn,smc->snc', slot_ops, local_direction, precision=highest)]
    pallas_call x0 -> x9, Pallas kernels: none -> 71.9 us  [the longest x2 42.2 us: slot_op(): pl.pallas_call(slot_op_kernel, grid=(2 * blocks,), out_shape=(jax.ShapeDt...]
    unnamed x68 -> x132, local copies, waits for them, and re-layouts: 7.17 us -> 63.2 us
    all_to_all x3 -> x0, blocking collectives: 34.9 us -> none  [copy_for_each(): lax.all_to_all(jnp.broadcast_to(value[None], (size, *value.shape)), axis,...]
    ppermute x17 -> x13, waiting for transfers between devices: 45.9 us -> 65.8 us  [from_behind(): return lax.ppermute(block, axis, route)]
    all_to_all x3 -> x6, starting transfers between devices: 18.1 us -> 31.7 us  [to_everyone(): lax.all_to_all(jnp.broadcast_to(value[None], (size, *value.shape)), axis,...]
    pmax x1 -> x0, blocking collectives: 11 us -> none  [shards(): peak_norm = lax.pmax(jnp.max(history, axis=1), 'case')]
  transfers between devices with their start and end apart: 20 -> 19, of which waited for: 13 -> 6; matrix products, arithmetic and copies ran while one was open for 40% -> 1% of each run, Pallas kernels for 0% -> 15%
where the time goes in v1:
time: 291 us; the launch traced here: 288 us
  waiting for transfers between devices  76.3 us (26%)
  local copies, waits for them, and re-layouts  73.8 us (25%)
  Pallas kernels  71.9 us (25%)
  starting transfers between devices  63.3 us (22%)
    ppermute x13, waiting for transfers between devices, from_behind(): return lax.ppermute(block, axis, route)  65.8 us
    unnamed x132, local copies, waits for them, and re-layouts  63.2 us
    pallas_call x2, Pallas kernels, slot_op(): pl.pallas_call(slot_op_kernel, grid=(2 * blocks,), out_shape=(jax.ShapeDt...  42.2 us
    all_to_all x6, starting transfers between devices, to_everyone(): lax.all_to_all(jnp.broadcast_to(value[None], (size, *value.shape)), axis,...  31.7 us
    ppermute x13, starting transfers between devices, from_behind(): return lax.ppermute(block, axis, route)  31.6 us
    pallas_call x5, Pallas kernels, step(): pl.pallas_call(body, out_shape=tuple(out), in_specs=specs, out_specs=[VME...  27.5 us
    all_to_all x6, waiting for transfers between devices, to_everyone(): lax.all_to_all(jnp.broadcast_to(value[None], (size, *value.shape)), axis,...  10.5 us
    broadcast_in_dim x6, local copies, waits for them, and re-layouts, to_everyone(): jnp.broadcast_to(value[None], (size, *value.shape))  6.22 us
  transfers between devices with their start and end apart: 19, of which 6 were waited for; matrix products, arithmetic and copies ran while one was open for 1% of the time, Pallas kernels for 15%

profile of v1, /device:TPU:0, one launch (start us, length us, event | category | flops | bytes accessed | tf_op | source)
XLA Modules:
  0.0 287.8 jit_solution(329198958336244719)
XLA Ops:
  3.3 6.1 %collective-permute-start.1 = (f32[24,128]{1,0:T(8,128)S(1)}, f32[24,128]{1,0:T(8,128)S(1)}, u32[]{:S(2)}, u32[]{:S(2)}) collective-permute-start(f32[24,128]{1,0:T(8,128)S(1)} %get-tuple-element.95), channel_id=1, source_target_pairs={{4,0},{8,4},{12,8},{16,12},{20,16},{24,20},{28,24},{32,28},{36,32}... | collective-permute-start | bytes 36872 | tf_op jit(solution)/shard_map/ppermute | solution.py:25
  11.0 1.3 slot_modes.1
  12.3 5.1 %collective-permute-start.3 = (bf16[16,768]{1,0:T(8,128)(2,1)S(1)}, bf16[16,768]{1,0:T(8,128)(2,1)S(1)}, u32[]{:S(2)}, u32[]{:S(2)}) collective-permute-start(bf16[16,768]{1,0:T(8,128)(2,1)S(1)} %get-tuple-element.51), channel_id=1, source_target_pairs={{4,0},{8,4},{12,8},{16,12},{20,16},{24,20},{28,24},{32,28},{36,32}... | collective-permute-start | bytes 73736 | tf_op jit(solution)/shard_map/ppermute | solution.py:25
  17.4 1.8 slice_bitcast_fusion
  19.2 21.1 %slot_op.2 = (bf16[1536,1536]{1,0:T(8,128)(2,1)S(1)}, f32[1536,128]{1,0:T(8,128)S(1)}) custom-call(f32[2,1536,1536]{2,1,0:T(8,128)} %ops_ref.3, s32[1,1536]{1,0:T(1,128)S(1)} %get-tuple-element.97.perm_ref), custom_call_target="tpu_custom_call" | custom-call | flops 14495514624 | bytes 14155776 | tf_op jit(solution)/shard_map/slot_op/pallas_call | solution.py:114
  40.3 2.2 copy-done
  43.7 1.1 broadcast_in_dim.24
  44.9 7.0 %all-to-all-start = ((f32[32,4,16,128]{3,2,1,0:T(8,128)}), f32[32,4,16,128]{3,2,1,0:T(8,128)}, u32[]{:S(2)}, u32[]{:S(2)}) async-start(f32[32,4,16,128]{3,2,1,0:T(8,128)} %broadcast_in_dim.24), calls=%async_computation | async-start | bytes 2097152 | tf_op jit(solution)/shard_map/all_to_all | solution.py:331
  51.9 21.1 %slot_op.3 = (bf16[1536,1536]{1,0:T(8,128)(2,1)S(1)}, f32[1536,128]{1,0:T(8,128)S(1)}) custom-call(f32[2,1536,1536]{2,1,0:T(8,128)} %ops_ref.3, s32[1,1536]{1,0:T(1,128)S(1)} %get-tuple-element.56.perm_ref), custom_call_target="tpu_custom_call" | custom-call | flops 14495514624 | bytes 14155776 | tf_op jit(solution)/shard_map/slot_op/pallas_call | solution.py:114
  73.0 2.2 copy-done.2
  75.2 2.3 copy-done.1
  77.5 6.1 %step.4 = (f32[3,768,128]{2,1,0:T(8,128)S(1)}, f32[1,128]{1,0:T(1,128)}, f32[3,768,128]{2,1,0:T(8,128)S(1)}, f32[2,768,128]{2,1,0:T(8,128)S(1)}, f32[768,128]{1,...) custom-call(s32[3]{0:T(128)S(1)} %slice_reduce_fusion.sizes_ref.refs_0_, ...), custom_call_target="tpu_custom_call" | custom-call | flops 1000000000 | bytes 15000000 | tf_op jit(solution)/shard_map/step/pallas_call | solution.py:315
  84.6 1.1 copy-done.14
  88.8 1.1 broadcast_in_dim.25
  89.9 7.1 %all-to-all-start.1 = ((f32[32,4,16,128]{3,2,1,0:T(8,128)}), f32[32,4,16,128]{3,2,1,0:T(8,128)S(1)}, u32[]{:S(2)}, u32[]{:S(2)}) async-start(f32[32,4,16,128]{3,2,1,0:T(8,128)} %broadcast_in_dim.25), calls=%async_computation.1 | async-start | bytes 2097152 | tf_op jit(solution)/shard_map/all_to_all | solution.py:331
  97.4 4.8 %collective-permute-start.6 = (f32[768,128]{1,0:T(8,128)}, f32[768,128]{1,0:T(8,128)S(1)}, u32[]{:S(2)}, u32[]{:S(2)}) collective-permute-start(f32[768,128]{1,0:T(8,128)} %copy-done.46), channel_id=1, source_target_pairs={{4,0},{8,4},{12,8},{16,12},{20,16},{24,20},{28,24},{32,28},{36,32}... | collective-permute-start | bytes 1179656 | tf_op jit(solution)/shard_map/ppermute | solution.py:25
  102.2 16.6 %collective-permute-done.5.refs_10_ = f32[768,128]{1,0:T(8,128)S(1)} collective-permute-done((f32[768,128]{1,0:T(8,128)}, f32[768,128]{1,0:T(8,128)S(1)}, u32[]{:S(2)}, u32[]{:S(2)}) %collective-permute-start.5) | collective-permute-done | bytes 393248 | tf_op jit(solution)/shard_map/ppermute | solution.py:25
  120.3 1.3 copy-done.13
  121.6 1.3 copy-done.15
  122.9 1.1 copy-done.23
  129.0 6.0 %step.5 = (f32[3,768,128]{2,1,0:T(8,128)S(1)}, f32[1,128]{1,0:T(1,128)S(1)}, f32[3,768,128]{2,1,0:T(8,128)S(1)}, f32[2,768,128]{2,1,0:T(8,128)S(1)}, f32[768,128...) custom-call(s32[3]{0:T(128)S(1)} %slice_reduce_fusion.sizes_ref.refs_0_, ...), custom_call_target="tpu_custom_call" | custom-call | flops 1000000000 | bytes 15000000 | tf_op jit(solution)/shard_map/step/pallas_call | solution.py:315
  136.0 1.1 copy-done.10
  140.2 1.1 broadcast_in_dim.26
  141.3 4.2 %all-to-all-start.2 = ((f32[32,4,16,128]{3,2,1,0:T(8,128)}), f32[32,4,16,128]{3,2,1,0:T(8,128)S(1)}, u32[]{:S(2)}, u32[]{:S(2)}) async-start(f32[32,4,16,128]{3,2,1,0:T(8,128)} %broadcast_in_dim.26), calls=%async_computation.2 | async-start | bytes 2097152 | tf_op jit(solution)/shard_map/all_to_all | solution.py:331
  145.7 4.9 %collective-permute-start.8 = (f32[768,128]{1,0:T(8,128)}, f32[768,128]{1,0:T(8,128)S(1)}, u32[]{:S(2)}, u32[]{:S(2)}) collective-permute-start(f32[768,128]{1,0:T(8,128)} %copy-done.40), channel_id=1, source_target_pairs={{4,0},{8,4},{12,8},{16,12},{20,16},{24,20},{28,24},{32,28},{36,32}... | collective-permute-start | bytes 1179656 | tf_op jit(solution)/shard_map/ppermute | solution.py:25
  150.6 16.6 %collective-permute-done.7.refs_10_ = f32[768,128]{1,0:T(8,128)S(1)} collective-permute-done((f32[768,128]{1,0:T(8,128)}, f32[768,128]{1,0:T(8,128)S(1)}, u32[]{:S(2)}, u32[]{:S(2)}) %collective-permute-start.7) | collective-permute-done | bytes 393248 | tf_op jit(solution)/shard_map/ppermute | solution.py:25
  168.8 1.3 copy-done.9
  170.0 1.3 copy-done.11
  171.3 1.1 copy-done.21
  177.4 6.0 %step.6 = (f32[3,768,128]{2,1,0:T(8,128)S(1)}, f32[1,128]{1,0:T(1,128)S(1)}, f32[3,768,128]{2,1,0:T(8,128)S(1)}, f32[2,768,128]{2,1,0:T(8,128)S(1)}, f32[768,128...) custom-call(s32[3]{0:T(128)S(1)} %slice_reduce_fusion.sizes_ref.refs_0_, ...), custom_call_target="tpu_custom_call" | custom-call | flops 1000000000 | bytes 15000000 | tf_op jit(solution)/shard_map/step/pallas_call | solution.py:315
  184.5 1.1 copy-done.6
  188.7 1.1 broadcast_in_dim.27
  189.7 3.9 %all-to-all-start.3 = ((f32[32,4,16,128]{3,2,1,0:T(8,128)}), f32[32,4,16,128]{3,2,1,0:T(8,128)S(1)}, u32[]{:S(2)}, u32[]{:S(2)}) async-start(f32[32,4,16,128]{3,2,1,0:T(8,128)} %broadcast_in_dim.27), calls=%async_computation.3 | async-start | bytes 2097152 | tf_op jit(solution)/shard_map/all_to_all | solution.py:331
  193.7 5.0 %collective-permute-start.10 = (f32[768,128]{1,0:T(8,128)}, f32[768,128]{1,0:T(8,128)S(1)}, u32[]{:S(2)}, u32[]{:S(2)}) collective-permute-start(f32[768,128]{1,0:T(8,128)} %copy-done.34), channel_id=1, source_target_pairs={{4,0},{8,4},{12,8},{16,12},{20,16},{24,20},{28,24},{32,28},{36,32}... | collective-permute-start | bytes 1179656 | tf_op jit(solution)/shard_map/ppermute | solution.py:25
  198.7 11.5 %collective-permute-done.10.refs_11_ = f32[768,128]{1,0:T(8,128)S(1)} collective-permute-done((f32[768,128]{1,0:T(8,128)}, f32[768,128]{1,0:T(8,128)S(1)}, u32[]{:S(2)}, u32[]{:S(2)}) %collective-permute-start.10) | collective-permute-done | bytes 393248 | tf_op jit(solution)/shard_map/ppermute | solution.py:25
  211.0 4.5 %collective-permute-done.9.refs_10_ = f32[768,128]{1,0:T(8,128)S(1)} collective-permute-done((f32[768,128]{1,0:T(8,128)}, f32[768,128]{1,0:T(8,128)S(1)}, u32[]{:S(2)}, u32[]{:S(2)}) %collective-permute-start.9) | collective-permute-done | bytes 393248 | tf_op jit(solution)/shard_map/ppermute | solution.py:25
  216.2 1.3 copy-done.5
  217.5 1.3 copy-done.7
  218.7 1.1 copy-done.19
  224.8 7.4 %step.7 = (f32[3,768,128]{2,1,0:T(8,128)S(1)}, f32[1,128]{1,0:T(1,128)S(1)}, f32[3,768,128]{2,1,0:T(8,128)}, f32[2,768,128]{2,1,0:T(8,128)}, f32[768,128]{1,0:T(...) custom-call(s32[3]{0:T(128)S(1)} %slice_reduce_fusion.sizes_ref.refs_0_, ...), custom_call_target="tpu_custom_call" | custom-call | flops 1000000000 | bytes 15000000 | tf_op jit(solution)/shard_map/step/pallas_call | solution.py:315
  232.2 1.0 copy-done.16
  235.5 1.1 broadcast_in_dim.28
  236.6 4.1 %all-to-all-start.4 = ((f32[32,4,16,128]{3,2,1,0:T(8,128)}), f32[32,4,16,128]{3,2,1,0:T(8,128)S(1)}, u32[]{:S(2)}, u32[]{:S(2)}) async-start(f32[32,4,16,128]{3,2,1,0:T(8,128)} %broadcast_in_dim.28), calls=%async_computation.4 | async-start | bytes 2097152 | tf_op jit(solution)/shard_map/all_to_all | solution.py:331
  240.9 4.9 %collective-permute-start.12 = (f32[768,128]{1,0:T(8,128)S(1)}, f32[768,128]{1,0:T(8,128)S(1)}, u32[]{:S(2)}, u32[]{:S(2)}) collective-permute-start(f32[768,128]{1,0:T(8,128)S(1)} %copy-done.25), channel_id=1, source_target_pairs={{4,0},{8,4},{12,8},{16,12},{20,16},{24,20},{28,24},{32,28},{36,32}... | collective-permute-start | bytes 1179656 | tf_op jit(solution)/shard_map/ppermute | solution.py:25
  245.8 16.6 %collective-permute-done.11.refs_10_ = f32[768,128]{1,0:T(8,128)S(1)} collective-permute-done((f32[768,128]{1,0:T(8,128)}, f32[768,128]{1,0:T(8,128)S(1)}, u32[]{:S(2)}, u32[]{:S(2)}) %collective-permute-start.11) | collective-permute-done | bytes 393248 | tf_op jit(solution)/shard_map/ppermute | solution.py:25
  267.9 1.9 last_step.1
  270.6 5.4 %all-to-all-start.5 = ((f32[128,4,128]{2,1,0:T(4,128)}), f32[128,4,128]{2,1,0:T(4,128)S(1)}, u32[]{:S(2)}, u32[]{:S(2)}) async-start(f32[128,4,128]{2,1,0:T(4,128)} %broadcast_in_dim.29), calls=%async_computation.5 | async-start | bytes 524288 | tf_op jit(solution)/shard_map/all_to_all | solution.py:331
  276.0 10.5 %all-to-all-done.5 = f32[128,4,128]{2,1,0:T(4,128)S(1)} async-done(((f32[128,4,128]{2,1,0:T(4,128)}), f32[128,4,128]{2,1,0:T(4,128)S(1)}, u32[]{:S(2)}, u32[]{:S(2)}) %all-to-all-start.5) | async-done | bytes 262176 | tf_op jit(solution)/shard_map/all_to_all | solution.py:331
  (155 shorter events, 48.0 us)
Async XLA Ops:
  3.2 39.3 %collective-permute-start = (f32[24,128]{1,0:T(8,128)S(1)}, f32[24,128]{1,0:T(8,128)S(1)}, u32[]{:S(2)}, u32[]{:S(2)}) collective-permute-start(f32[24,128]{1,0:T(8,128)S(1)} %get-tuple-element.94), channel_id=1, source_target_pairs={{124,0},{0,4},{4,8},{8,12},{12,16},{16,20},{20,24},{24,28},{28,32}... | collective-permute-start | bytes 36872 | tf_op jit(solution)/shard_map/ppermute | solution.py:25
  3.3 39.2 %collective-permute-start.1 = (f32[24,128]{1,0:T(8,128)S(1)}, f32[24,128]{1,0:T(8,128)S(1)}, u32[]{:S(2)}, u32[]{:S(2)}) collective-permute-start(f32[24,128]{1,0:T(8,128)S(1)} %get-tuple-element.95), channel_id=1, source_target_pairs={{4,0},{8,4},{12,8},{16,12},{20,16},{24,20},{28,24},{32,28},{36,32}... | collective-permute-start | bytes 36872 | tf_op jit(solution)/shard_map/ppermute | solution.py:25
  12.3 30.5 %collective-permute-start.2 = (bf16[16,768]{1,0:T(8,128)(2,1)S(1)}, bf16[16,768]{1,0:T(8,128)(2,1)S(1)}, u32[]{:S(2)}, u32[]{:S(2)}) collective-permute-start(bf16[16,768]{1,0:T(8,128)(2,1)S(1)} %get-tuple-element.50), channel_id=1, source_target_pairs={{124,0},{0,4},{4,8},{8,12},{12,16},{16,20},{20,24},{24,28},{28,32}... | collective-permute-start | bytes 73736 | tf_op jit(solution)/shard_map/ppermute | solution.py:25
  12.3 30.5 %collective-permute-start.3 = (bf16[16,768]{1,0:T(8,128)(2,1)S(1)}, bf16[16,768]{1,0:T(8,128)(2,1)S(1)}, u32[]{:S(2)}, u32[]{:S(2)}) collective-permute-start(bf16[16,768]{1,0:T(8,128)(2,1)S(1)} %get-tuple-element.51), channel_id=1, source_target_pairs={{4,0},{8,4},{12,8},{16,12},{20,16},{24,20},{28,24},{32,28},{36,32}... | collective-permute-start | bytes 73736 | tf_op jit(solution)/shard_map/ppermute | solution.py:25
  19.1 56.0 %collective-permute-start.4 = (f32[768,128]{1,0:T(8,128)}, f32[768,128]{1,0:T(8,128)}, u32[]{:S(2)}, u32[]{:S(2)}) collective-permute-start(f32[768,128]{1,0:T(8,128)} %slice_bitcast_fusion), channel_id=1, source_target_pairs={{124,0},{0,4},{4,8},{8,12},{12,16},{16,20},{20,24},{24,28},{28,32}... | collective-permute-start | bytes 1179656 | tf_op jit(solution)/shard_map/ppermute | solution.py:25
  19.2 23.7 %copy-start.3 = (f32[2,768,128]{2,1,0:T(8,128)S(1)}, f32[2,768,128]{2,1,0:T(8,128)}, u32[]{:S(2)}) copy-start(f32[2,768,128]{2,1,0:T(8,128)} %refs_7_.1) | copy-start | bytes 2359300
  40.3 2.2 copy-start
  44.9 30.3 %all-to-all-start = ((f32[32,4,16,128]{3,2,1,0:T(8,128)}), f32[32,4,16,128]{3,2,1,0:T(8,128)}, u32[]{:S(2)}, u32[]{:S(2)}) async-start(f32[32,4,16,128]{3,2,1,0:T(8,128)} %broadcast_in_dim.24), calls=%async_computation | async-start | bytes 2097152 | tf_op jit(solution)/shard_map/all_to_all | solution.py:331
  72.9 2.2 copy-start.2
  75.2 2.3 copy-start.1
  83.6 1.0 copy-start.12
  84.6 1.1 copy-start.14
  89.9 30.4 %all-to-all-start.1 = ((f32[32,4,16,128]{3,2,1,0:T(8,128)}), f32[32,4,16,128]{3,2,1,0:T(8,128)S(1)}, u32[]{:S(2)}, u32[]{:S(2)}) async-start(f32[32,4,16,128]{3,2,1,0:T(8,128)} %broadcast_in_dim.25), calls=%async_computation.1 | async-start | bytes 2097152 | tf_op jit(solution)/shard_map/all_to_all | solution.py:331
  97.0 21.7 %collective-permute-start.5 = (f32[768,128]{1,0:T(8,128)}, f32[768,128]{1,0:T(8,128)S(1)}, u32[]{:S(2)}, u32[]{:S(2)}) collective-permute-start(f32[768,128]{1,0:T(8,128)} %copy-done.50), channel_id=1, source_target_pairs={{124,0},{0,4},{4,8},{8,12},{12,16},{16,20},{20,24},{24,28},{28,32}... | collective-permute-start | bytes 1179656 | tf_op jit(solution)/shard_map/ppermute | solution.py:25
  97.4 22.2 %collective-permute-start.6 = (f32[768,128]{1,0:T(8,128)}, f32[768,128]{1,0:T(8,128)S(1)}, u32[]{:S(2)}, u32[]{:S(2)}) collective-permute-start(f32[768,128]{1,0:T(8,128)} %copy-done.46), channel_id=1, source_target_pairs={{4,0},{8,4},{12,8},{16,12},{20,16},{24,20},{28,24},{32,28},{36,32}... | collective-permute-start | bytes 1179656 | tf_op jit(solution)/shard_map/ppermute | solution.py:25
  120.3 1.3 copy-start.13
  121.6 1.3 copy-start.15
  122.9 1.1 copy-start.23
  124.0 1.0 copy-start.47
  125.0 1.0 copy-start.49
  128.0 1.0 copy-start.61
  135.0 1.0 copy-start.8
  136.0 1.1 copy-start.10
  141.3 27.4 %all-to-all-start.2 = ((f32[32,4,16,128]{3,2,1,0:T(8,128)}), f32[32,4,16,128]{3,2,1,0:T(8,128)S(1)}, u32[]{:S(2)}, u32[]{:S(2)}) async-start(f32[32,4,16,128]{3,2,1,0:T(8,128)} %broadcast_in_dim.26), calls=%async_computation.2 | async-start | bytes 2097152 | tf_op jit(solution)/shard_map/all_to_all | solution.py:331
  145.5 21.7 %collective-permute-start.7 = (f32[768,128]{1,0:T(8,128)}, f32[768,128]{1,0:T(8,128)S(1)}, u32[]{:S(2)}, u32[]{:S(2)}) collective-permute-start(f32[768,128]{1,0:T(8,128)} %copy-done.44), channel_id=1, source_target_pairs={{124,0},{0,4},{4,8},{8,12},{12,16},{16,20},{20,24},{24,28},{28,32}... | collective-permute-start | bytes 1179656 | tf_op jit(solution)/shard_map/ppermute | solution.py:25
  145.7 22.3 %collective-permute-start.8 = (f32[768,128]{1,0:T(8,128)}, f32[768,128]{1,0:T(8,128)S(1)}, u32[]{:S(2)}, u32[]{:S(2)}) collective-permute-start(f32[768,128]{1,0:T(8,128)} %copy-done.40), channel_id=1, source_target_pairs={{4,0},{8,4},{12,8},{16,12},{20,16},{24,20},{28,24},{32,28},{36,32}... | collective-permute-start | bytes 1179656 | tf_op jit(solution)/shard_map/ppermute | solution.py:25
  168.8 1.3 copy-start.9
  170.0 1.3 copy-start.11
  171.3 1.1 copy-start.21
  172.4 1.0 copy-start.41
  175.4 1.0 copy-start.59
  176.4 1.0 copy-start.63
  183.5 1.0 copy-start.4
  184.5 1.1 copy-start.6
  189.7 26.4 %all-to-all-start.3 = ((f32[32,4,16,128]{3,2,1,0:T(8,128)}), f32[32,4,16,128]{3,2,1,0:T(8,128)S(1)}, u32[]{:S(2)}, u32[]{:S(2)}) async-start(f32[32,4,16,128]{3,2,1,0:T(8,128)} %broadcast_in_dim.27), calls=%async_computation.3 | async-start | bytes 2097152 | tf_op jit(solution)/shard_map/all_to_all | solution.py:331
  193.7 16.5 %collective-permute-start.10 = (f32[768,128]{1,0:T(8,128)}, f32[768,128]{1,0:T(8,128)S(1)}, u32[]{:S(2)}, u32[]{:S(2)}) collective-permute-start(f32[768,128]{1,0:T(8,128)} %copy-done.34), channel_id=1, source_target_pairs={{4,0},{8,4},{12,8},{16,12},{20,16},{24,20},{28,24},{32,28},{36,32}... | collective-permute-start | bytes 1179656 | tf_op jit(solution)/shard_map/ppermute | solution.py:25
  198.7 16.7 %collective-permute-start.9 = (f32[768,128]{1,0:T(8,128)}, f32[768,128]{1,0:T(8,128)S(1)}, u32[]{:S(2)}, u32[]{:S(2)}) collective-permute-start(f32[768,128]{1,0:T(8,128)} %copy-done.38), channel_id=1, source_target_pairs={{124,0},{0,4},{4,8},{8,12},{12,16},{16,20},{20,24},{24,28},{28,32}... | collective-permute-start | bytes 1179656 | tf_op jit(solution)/shard_map/ppermute | solution.py:25
  216.2 1.3 copy-start.5
  217.5 1.3 copy-start.7
  218.7 1.1 copy-start.19
  232.2 1.0 copy-start.16
  236.6 4.3 %copy-start.25 = (f32[768,128]{1,0:T(8,128)S(1)}, f32[768,128]{1,0:T(8,128)}, u32[]{:S(2)}) copy-start(f32[768,128]{1,0:T(8,128)} %copy-done.24) | copy-start | bytes 1179652
  236.6 27.3 %copy-start.17 = (f32[3,768,128]{2,1,0:T(8,128)S(1)}, f32[3,768,128]{2,1,0:T(8,128)}, u32[]{:S(2)}) copy-start(f32[3,768,128]{2,1,0:T(8,128)} %copy-done.16) | copy-start | bytes 3538948
  236.6 27.3 %all-to-all-start.4 = ((f32[32,4,16,128]{3,2,1,0:T(8,128)}), f32[32,4,16,128]{3,2,1,0:T(8,128)S(1)}, u32[]{:S(2)}, u32[]{:S(2)}) async-start(f32[32,4,16,128]{3,2,1,0:T(8,128)} %broadcast_in_dim.28), calls=%async_computation.4 | async-start | bytes 2097152 | tf_op jit(solution)/shard_map/all_to_all | solution.py:331
  240.7 21.7 %collective-permute-start.11 = (f32[768,128]{1,0:T(8,128)}, f32[768,128]{1,0:T(8,128)S(1)}, u32[]{:S(2)}, u32[]{:S(2)}) collective-permute-start(f32[768,128]{1,0:T(8,128)} %copy-done.28), channel_id=1, source_target_pairs={{124,0},{0,4},{4,8},{8,12},{12,16},{16,20},{20,24},{24,28},{28,32}... | collective-permute-start | bytes 1179656 | tf_op jit(solution)/shard_map/ppermute | solution.py:25
  240.9 22.3 %collective-permute-start.12 = (f32[768,128]{1,0:T(8,128)S(1)}, f32[768,128]{1,0:T(8,128)S(1)}, u32[]{:S(2)}, u32[]{:S(2)}) collective-permute-start(f32[768,128]{1,0:T(8,128)S(1)} %copy-done.25), channel_id=1, source_target_pairs={{4,0},{8,4},{12,8},{16,12},{20,16},{24,20},{28,24},{32,28},{36,32}... | collective-permute-start | bytes 1179656 | tf_op jit(solution)/shard_map/ppermute | solution.py:25
  263.9 1.0 copy-start.27
  270.6 15.9 %all-to-all-start.5 = ((f32[128,4,128]{2,1,0:T(4,128)}), f32[128,4,128]{2,1,0:T(4,128)S(1)}, u32[]{:S(2)}, u32[]{:S(2)}) async-start(f32[128,4,128]{2,1,0:T(4,128)} %broadcast_in_dim.29), calls=%async_computation.5 | async-start | bytes 524288 | tf_op jit(solution)/shard_map/all_to_all | solution.py:331
  (37 other events, 31.3 us)

commit v2 on v1

v2 whole, which is shorter than its diff:
```python
import jax
import jax.numpy as jnp
from jax import lax
from jax.experimental import pallas as pl
from jax.experimental.pallas import tpu as pltpu
from jax.sharding import PartitionSpec as P

STEPS = 4

low_bound = 2.0
high_bound = 14.0
epsilon = 1e-06
f32 = jnp.float32
bf16 = jnp.bfloat16
BLK = 256
OPBLK = 512
VECBLK = 768
VMEM = pl.BlockSpec(memory_space=pltpu.VMEM)
SMEM = pl.BlockSpec(memory_space=pltpu.SMEM)
ANY = pl.BlockSpec(memory_space=pl.ANY)
PARAMS = pltpu.CompilerParams(vmem_limit_bytes=60 * 1024 * 1024)


def from_behind(block, axis, distance):
    count = lax.axis_size(axis)
    route = [((i - distance) % count, i) for i in range(count)]
    return lax.ppermute(block, axis, route)


def dot(a, b):
    return jnp.dot(a, b, preferred_element_type=f32)


def split(value):
    high = value.astype(bf16)
    low = (value - high.astype(f32)).astype(bf16)
    return high, low


def slot_modes_kernel(modes_ref, perm_ref, left_ref, right_ref, to_next_ref, to_prior_ref):
    count, rows, width = modes_ref.shape
    half = width // 2
    for s in range(count):
        for at in range(0, width, BLK):
            one_hot = (
                lax.broadcasted_iota(jnp.int32, (width, BLK), 0) == perm_ref[s : s + 1, at : at + BLK]
            ).astype(f32).astype(bf16)
            part = dot(modes_ref[s], one_hot).astype(bf16)
            if at < half:
                left_ref[s, :, at : at + BLK] = part
                if s == 0:
                    to_prior_ref[:, at : at + BLK] = part
            else:
                right_ref[s, :, at - half : at - half + BLK] = part
                if s == count - 1:
                    to_next_ref[:, at - half : at - half + BLK] = part


def slot_modes(modes, row_perm):
    count, rows, width = modes.shape
    half = width // 2
    side = jax.ShapeDtypeStruct((count, rows, half), bf16)
    rim = jax.ShapeDtypeStruct((rows, half), bf16)
    return pl.pallas_call(
        slot_modes_kernel,
        out_shape=(side, side, rim, rim),
        in_specs=[VMEM, VMEM],
        out_specs=[VMEM] * 4,
        compiler_params=PARAMS,
        name="slot_modes",
    )(modes, row_perm)


def slot_op_kernel(ops_ref, perm_ref, out_ref, diag_ref, cols_done, one_hot, diag_row):
    width = one_hot.shape[0]
    blocks = width // OPBLK
    at = pl.program_id(0)

    @pl.when(at == 0)
    def _():
        for k in range(blocks):
            one_hot[k * OPBLK : (k + 1) * OPBLK, :] = (
                lax.broadcasted_iota(jnp.int32, (OPBLK, width), 0) + k * OPBLK == perm_ref[...]
            ).astype(f32).astype(bf16)
        diag_row[...] = jnp.zeros_like(diag_row)

    @pl.when(at < blocks)
    def _():
        block = ops_ref[0]
        on_diag = lax.broadcasted_iota(jnp.int32, (OPBLK, width), 0) + at * OPBLK == (
            lax.broadcasted_iota(jnp.int32, (OPBLK, width), 1)
        )
        diag_row[0:1, :] += jnp.sum(jnp.where(on_diag, block, 0.0), axis=0, keepdims=True)
        rest = jnp.where(on_diag, 0.0, block).astype(bf16)
        rows = pl.ds(pl.multiple_of(at * OPBLK, OPBLK), OPBLK)
        cols_done[rows, :] = dot(rest, one_hot[...]).astype(bf16)

    @pl.when(at >= blocks)
    def _():
        place = pl.multiple_of((at - blocks) * OPBLK, OPBLK)
        perm_part = perm_ref[:, pl.ds(place, OPBLK)].astype(f32)
        owner = jnp.transpose(jnp.broadcast_to(perm_part, (128, OPBLK)))
        total = jnp.zeros((OPBLK, 128), f32)
        pieces = []
        for k in range(0, width, 128):
            here = (lax.broadcasted_iota(jnp.int32, (OPBLK, 128), 1) + k).astype(f32) == owner
            pieces.append(here.astype(f32).astype(bf16))
            total += jnp.where(here, diag_row[0:1, k : k + 128], 0.0)
        out_ref[...] = dot(jnp.concatenate(pieces, axis=1), cols_done[...]).astype(bf16)
        diag_ref[...] = jnp.broadcast_to(jnp.sum(total, axis=1, keepdims=True), (OPBLK, 128))


def slot_op(dual_ops, perm_row, which):
    width = dual_ops.shape[1]
    blocks = width // OPBLK
    return pl.pallas_call(
        slot_op_kernel,
        grid=(2 * blocks,),
        out_shape=(
            jax.ShapeDtypeStruct((width, width), bf16),
            jax.ShapeDtypeStruct((width, 128), f32),
        ),
        in_specs=[
            pl.BlockSpec((1, OPBLK, width), lambda i: (which, jnp.minimum(i, blocks - 1), 0)),
            pl.BlockSpec((1, width), lambda i: (0, 0)),
        ],
        out_specs=[
            pl.BlockSpec((OPBLK, width), lambda i: (jnp.maximum(i - blocks, 0), 0)),
            pl.BlockSpec((OPBLK, 128), lambda i: (jnp.maximum(i - blocks, 0), 0)),
        ],
        scratch_shapes=[
            pltpu.VMEM((width, width), bf16),
            pltpu.VMEM((width, width), bf16),
            pltpu.VMEM((8, width), f32),
        ],
        compiler_params=PARAMS,
        cost_estimate=pl.CostEstimate(
            flops=4 * width**3, bytes_accessed=6 * width * width, transcendentals=0
        ),
        name="slot_op",
    )(dual_ops, perm_row)


def alive(size, rows):
    return lax.broadcasted_iota(jnp.int32, (rows, 128), 0) < size


def partial_coefficients(rows_ref, shares, part_ref):
    modes = part_ref.shape[2]
    sums = []
    for e, share in enumerate(shares):
        if share is None:
            sums.append(jnp.zeros((2 * modes, 128), f32))
            continue
        high, low = split(share)
        both = dot(rows_ref[e], jnp.concatenate([high, low], axis=1))
        sums.append(both[:, :128] + both[:, 128:])
    parts = [
        sums[0][:modes],
        sums[0][modes:] + sums[1][:modes],
        sums[1][modes:] + sums[2][:modes],
        sums[2][modes:],
    ]
    for k, part in enumerate(parts):
        part = part.astype(bf16)
        for device in range(part_ref.shape[0]):
            part_ref[device, k] = part


def start_kernel(
    sizes_ref, left_ref, right_ref, prior_ref, next_ref, rhs_ref, rows_ref, cols_ref, part_ref
):
    half = rhs_ref.shape[1]
    pairs = [
        (prior_ref[...], left_ref[0]),
        (right_ref[0], left_ref[1]),
        (right_ref[1], next_ref[...]),
    ]
    for e, (above, below) in enumerate(pairs):
        stack = jnp.concatenate([above.astype(f32), -below.astype(f32)], axis=0)
        rows_ref[e] = stack.astype(bf16)
        cols_ref[e] = jnp.transpose(jnp.concatenate([stack, stack], axis=0)).astype(bf16)
    shares = [None]
    for e in range(2):
        shares.append(jnp.where(alive(sizes_ref[e + 1], half), -rhs_ref[e], 0.0))
    partial_coefficients(rows_ref, shares, part_ref)


def start(sizes, left, right, prior, following, rhs):
    half = rhs.shape[1]
    modes = left.shape[1]
    return pl.pallas_call(
        start_kernel,
        out_shape=(
            jax.ShapeDtypeStruct((3, 2 * modes, half), bf16),
            jax.ShapeDtypeStruct((3, half, 4 * modes), bf16),
            jax.ShapeDtypeStruct((lax.axis_size("dom"), 4, modes, 128), bf16),
        ),
        in_specs=[SMEM] + [VMEM] * 5,
        out_specs=[VMEM] * 3,
        compiler_params=PARAMS,
        name="start",
    )(sizes, left, right, prior, following, rhs)


def triple(value):
    high, low = split(value)
    return jnp.concatenate([high, low, high, jnp.zeros_like(high)], axis=1)


def triple_rows(value):
    high, low = split(value)
    return jnp.concatenate([high, high, low, jnp.zeros_like(high)], axis=0)


def share_sums(rows_ref, shares):
    modes = rows_ref.shape[1] // 2
    sums = []
    for e, share in enumerate(shares):
        lanes = share.shape[1]
        high, low = split(share)
        both = dot(rows_ref[e], jnp.concatenate([high, low], axis=1))
        sums.append(both[:, :lanes] + both[:, lanes:])
    return jnp.concatenate(
        [
            sums[0][:modes],
            sums[0][modes:] + sums[1][:modes],
            sums[1][modes:] + sums[2][:modes],
            sums[2][modes:],
        ],
        axis=0,
    )


def own_shares(live, sides):
    return [
        jnp.where(live[0], -sides[0], 0.0),
        jnp.where(live[1], sides[1] - sides[2], 0.0),
        jnp.where(live[2], sides[3], 0.0),
    ]


def apply_operator(copies, held, slots, diag_refs, exact):
    sides = []
    half = exact(0).shape[0]
    for s in range(2):
        copies[s].wait()
        for side in range(2):
            here = slice(side * half, side * half + half)
            value = dot(held[s, here, :], slots[s])
            sign = 1.0 if side else -1.0
            lanes = exact(s + side).shape[1]
            diag = diag_refs[s][here, :]
            if lanes > 128:
                diag = jnp.concatenate([diag, diag], axis=1)
            sides.append(value + sign * (diag * exact(s + side)))
    return sides


def take_amounts(own_ref, other_ref, all_ref, blocks_ref, picked):
    modes = all_ref.shape[1]
    subs, _, width = blocks_ref.shape
    count = width // modes
    amounts = []
    for s in range(subs):
        for q in range(count):
            here = q * modes
            picked[s, here : here + modes, :] = all_ref[own_ref[s * count + q]]
            picked[s, width + here : width + here + modes, :] = all_ref[other_ref[s * count + q]]
        high, low = split(blocks_ref[s])
        rows = jnp.concatenate([high, low], axis=0)
        both = dot(jnp.concatenate([rows, rows], axis=1), picked[s])
        amounts.append(both[:modes] + both[modes:])
    return jnp.concatenate(amounts, axis=0)


def first_kernel(
    scale, sizes_ref, rhs_ref, prior_ref, rows_ref, cols_ref, op_a, op_b, diag_a, diag_b,
    res_out, dir_out, wa_out, wb_out, wc_out, sums_out, fields_out, links_out,
    held, slots, wide, sems,
):
    copies = []
    for s, op in enumerate((op_a, op_b)):
        copies.append(pltpu.make_async_copy(op, held.at[s], sems.at[s]))
        copies[-1].start()
    half = rhs_ref.shape[1]
    modes = rows_ref.shape[1] // 2
    live = [alive(sizes_ref[e], half) for e in range(3)]
    for e in range(3):
        start = jnp.where(live[e], prior_ref[...] if e == 0 else rhs_ref[e - 1], 0.0)
        direction = scale * start
        res_out[e] = start
        dir_out[e] = direction
        pair = cols_ref[e][:, : 2 * modes].astype(f32)
        parts = [pair, jnp.zeros((half, 128 - 2 * modes), f32)]
        if e > 0:
            parts = [jnp.zeros((half, e * modes), f32), pair]
            parts.append(jnp.zeros((half, 128 - (2 + e) * modes), f32))
        coarse = jnp.where(live[e], jnp.concatenate(parts, axis=1), 0.0)
        both = jnp.concatenate([direction, coarse], axis=1)
        wide[e] = both
        low_form = both.astype(bf16)
        if e < 2:
            slots[e, :half] = -low_form
        if e > 0:
            slots[e - 1, half:] = low_form
    sides = apply_operator(copies, held, slots, (diag_a, diag_b), lambda e: wide[e])
    live = [jnp.concatenate([mask, mask], axis=1) for mask in live]
    shares = own_shares(live, sides)
    wa_out[...], wb_out[...], wc_out[...] = [share[:, :128] for share in shares]
    sums = share_sums(rows_ref, shares)
    sums_out[...] = sums[:, :128]
    for e in range(3):
        fields_out[e] = triple(shares[e][:, 128 : 128 + 4 * modes])
    links_out[...] = triple(sums[:, 128 : 128 + 4 * modes])


def scratch_of(half, lanes):
    return [
        pltpu.VMEM((2, 2 * half, 2 * half), bf16),
        pltpu.VMEM((2, 2 * half, lanes), bf16),
    ]


def first(scale, sizes, rhs, prior_rhs, rows, cols, ops):
    half, lanes = rhs.shape[1:]
    modes = rows.shape[1] // 2
    field = jax.ShapeDtypeStruct((half, lanes), f32)
    three = jax.ShapeDtypeStruct((3, half, lanes), f32)

    def body(*refs):
        first_kernel(scale, *refs)

    return pl.pallas_call(
        body,
        out_shape=(
            three,
            three,
            field,
            field,
            field,
            jax.ShapeDtypeStruct((4 * modes, lanes), f32),
            jax.ShapeDtypeStruct((3, half, 16 * modes), bf16),
            jax.ShapeDtypeStruct((4 * modes, 16 * modes), bf16),
        ),
        in_specs=[SMEM] + [VMEM] * 4 + [ANY, ANY, VMEM, VMEM],
        out_specs=[VMEM] * 8,
        scratch_shapes=scratch_of(half, 2 * lanes)
        + [pltpu.VMEM((3, half, 2 * lanes), f32), pltpu.SemaphoreType.DMA((2,))],
        compiler_params=PARAMS,
        cost_estimate=pl.CostEstimate(
            flops=2 * 10**9, bytes_accessed=2 * 10**7, transcendentals=0
        ),
        name="first",
    )(sizes, rhs, prior_rhs, rows, cols, *ops)


def coarse_kernel(
    new, own_ref, other_ref, all_ref, blocks_ref, wa_ref, wc_ref, fields_ref,
    amounts_out, wa_out, wc_out, to_prior_out, to_next_out, picked,
):
    amounts = take_amounts(own_ref, other_ref, all_ref, blocks_ref, picked)
    amounts_out[...] = amounts
    scaled = triple_rows(new * amounts)
    wa = wa_ref[...] + dot(fields_ref[0], scaled)
    wc = wc_ref[...] + dot(fields_ref[2], scaled)
    wa_out[...], wc_out[...] = wa, wc
    to_prior_out[...], to_next_out[...] = wa.astype(bf16), wc.astype(bf16)


def share_kernel(new, amounts_ref, sums_ref, links_ref, part_out):
    modes = part_out.shape[2]
    scaled = triple_rows(new * amounts_ref[...])
    sums = (sums_ref[...] + dot(links_ref[...], scaled)).astype(bf16)
    for k in range(4):
        for device in range(part_out.shape[0]):
            part_out[device, k] = sums[k * modes : (k + 1) * modes]


def share(new, amounts, sums, links):
    rows, lanes = amounts.shape

    def body(*refs):
        share_kernel(new, *refs)

    return pl.pallas_call(
        body,
        out_shape=jax.ShapeDtypeStruct((lax.axis_size("dom"), 4, rows // 4, lanes), bf16),
        in_specs=[VMEM] * 3,
        out_specs=VMEM,
        compiler_params=PARAMS,
        cost_estimate=pl.CostEstimate(
            flops=10**11, bytes_accessed=10**9, transcendentals=0
        ),
        name="share",
    )(amounts, sums, links)


def coarse(new, ints, everything, blocks, wa, wc, fields):
    modes = everything.shape[1]
    half, lanes = wa.shape
    subs, _, width = blocks.shape
    field = jax.ShapeDtypeStruct((half, lanes), f32)
    rim = jax.ShapeDtypeStruct((half, lanes), bf16)

    def body(*refs):
        coarse_kernel(new, *refs)

    return pl.pallas_call(
        body,
        out_shape=(
            jax.ShapeDtypeStruct((4 * modes, lanes), f32),
            field,
            field,
            rim,
            rim,
        ),
        in_specs=[SMEM, SMEM] + [VMEM] * 5,
        out_specs=[VMEM] * 5,
        scratch_shapes=[pltpu.VMEM((subs, 2 * width, lanes), bf16)],
        compiler_params=PARAMS,
        cost_estimate=pl.CostEstimate(
            flops=10**8, bytes_accessed=4 * 10**6, transcendentals=0
        ),
        name="coarse",
    )(*ints, everything, blocks, wa, wc, fields)


def step_kernel(begin, last, new, old_next, new_next, *refs):
    refs = list(refs)
    take = lambda n: [refs.pop(0) for _ in range(n)]
    (sizes_ref, amounts_ref, cols_ref, fields_ref) = take(4)
    wa_ref, wb_ref, wc_ref, prior_ref, next_ref, res_ref, dir_ref = take(7)
    sol_ref = None if begin else take(1)[0]
    if not last:
        rows_ref, op_a, op_b, diag_a, diag_b = take(5)
    res_out, sol_out, norm_out = take(3)
    if not last:
        dir_out, wa_out, wb_out, wc_out, sums_out = take(5)
        held, slots, sems = take(3)
        copies = []
        for s, op in enumerate((op_a, op_b)):
            copies.append(pltpu.make_async_copy(op, held.at[s], sems.at[s]))
            copies[-1].start()
    half = wa_ref.shape[0]
    modes = amounts_ref.shape[0] // 4
    amounts = amounts_ref[...]
    high, low = split(amounts)
    live = [alive(sizes_ref[e], half) for e in range(3)]
    total = jnp.zeros((1, 128), f32)
    for e in range(3):
        if last and e == 0:
            continue
        at = slice(e * modes, (e + 2) * modes)
        spread = dot(cols_ref[e], jnp.concatenate([high[at], low[at]], axis=0))
        spread = jnp.where(live[e], spread, 0.0)
        if e == 0:
            field = wa_ref[...] + prior_ref[...].astype(f32)
        elif e == 1:
            field = wb_ref[...] + dot(fields_ref[1], triple_rows(new * amounts))
        else:
            field = wc_ref[...] + next_ref[...].astype(f32)
        residual = res_ref[e] + spread
        direction = dir_ref[e] + new * spread
        if e > 0:
            total += jnp.sum(residual * residual, axis=0, keepdims=True)
            sol_out[e - 1] = direction if begin else sol_ref[e - 1] + direction
        residual = residual - field
        if last:
            res_out[e - 1] = residual
            continue
        res_out[e] = residual
        direction = old_next * direction + new_next * residual
        dir_out[e] = direction
        low_form = direction.astype(bf16)
        if e < 2:
            slots[e, :half] = -low_form
        if e > 0:
            slots[e - 1, half:] = low_form
    norm_out[...] = total
    if last:
        return
    sides = apply_operator(copies, held, slots, (diag_a, diag_b), lambda e: dir_out[e])
    shares = own_shares(live, sides)
    wa_out[...], wb_out[...], wc_out[...] = shares
    sums_out[...] = share_sums(rows_ref, shares)


def step(begin, last, factors, sizes, amounts, cols, coarse_fields, fields, rows=None, ops=()):
    half, lanes = fields[0].shape
    field = jax.ShapeDtypeStruct((half, lanes), f32)
    three = jax.ShapeDtypeStruct((3, half, lanes), f32)
    two = jax.ShapeDtypeStruct((2, half, lanes), f32)
    out = [two if last else three, two, jax.ShapeDtypeStruct((1, lanes), f32)]
    args = [sizes, amounts, cols, coarse_fields, *fields]
    specs = [SMEM] + [VMEM] * (len(args) - 1)
    scratch = []
    if not last:
        out += [three, field, field, field, jax.ShapeDtypeStruct(amounts.shape, f32)]
        scratch += scratch_of(half, lanes) + [pltpu.SemaphoreType.DMA((2,))]
        args += [rows, *ops]
        specs += [VMEM, ANY, ANY, VMEM, VMEM]

    def body(*refs):
        step_kernel(begin, last, *factors, *refs)

    return pl.pallas_call(
        body,
        out_shape=tuple(out),
        in_specs=specs,
        out_specs=[VMEM] * len(out),
        scratch_shapes=scratch,
        compiler_params=PARAMS,
        cost_estimate=pl.CostEstimate(
            flops=10**11, bytes_accessed=10**9, transcendentals=0
        ),
        name="last_step" if last else "step",
    )(*args)


def final_kernel(own_ref, other_ref, sizes_ref, all_ref, blocks_ref, cols_ref, res_ref, res_out, norm_out, picked):
    amounts = take_amounts(own_ref, other_ref, all_ref, blocks_ref, picked)
    modes = amounts.shape[0] // 4
    half = res_ref.shape[1]
    high, low = split(amounts)
    total = jnp.zeros((1, 128), f32)
    for e in range(1, 3):
        at = slice(e * modes, (e + 2) * modes)
        spread = dot(cols_ref[e], jnp.concatenate([high[at], low[at]], axis=0))
        residual = res_ref[e - 1] + jnp.where(alive(sizes_ref[e], half), spread, 0.0)
        res_out[e - 1] = residual
        total += jnp.sum(residual * residual, axis=0, keepdims=True)
    norm_out[...] = total


def final(ints, sizes, everything, blocks, cols, residual):
    subs, _, width = blocks.shape
    lanes = residual.shape[-1]
    return pl.pallas_call(
        final_kernel,
        out_shape=(
            jax.ShapeDtypeStruct(residual.shape, f32),
            jax.ShapeDtypeStruct((1, lanes), f32),
        ),
        in_specs=[SMEM] * 3 + [VMEM] * 4,
        out_specs=[VMEM] * 2,
        scratch_shapes=[pltpu.VMEM((subs, 2 * width, lanes), bf16)],
        compiler_params=PARAMS,
        name="final",
    )(*ints, sizes, everything, blocks, cols, residual)


def trade(copies, axis):
    return lax.all_to_all(copies, axis, 0, 0, tiled=True)


def to_everyone(value, axis):
    size = lax.psum(1, axis)
    return trade(jnp.broadcast_to(value[None], (size, *value.shape)), axis)


def shards(dual_ops, modes, coarse_rows, coarse_cols, row_perm, iface_size, rhs):
    doms = lax.axis_size("dom")
    count, blocks, rows, _ = coarse_rows.shape
    flat = jnp.swapaxes(coarse_rows, 1, 2).reshape(count, rows, blocks * rows)
    whole = jnp.concatenate([coarse_cols, iface_size[:, None]], axis=1).astype(f32)
    whole = jnp.pad(whole, ((0, 0), (0, blocks * rows - whole.shape[1])))
    pack = jnp.concatenate([flat, jnp.broadcast_to(whole[:, None], (count, 8, blocks * rows))], axis=1)
    prior_pack = from_behind(pack[-1], "dom", 1)
    next_pack = from_behind(pack[0], "dom", -1)
    prior_rhs = from_behind(rhs[-1], "dom", 1)
    left, right, to_next, to_prior = slot_modes(modes, row_perm)
    prior_modes = from_behind(to_next, "dom", 1)
    next_modes = from_behind(to_prior, "dom", -1)
    ext = jnp.concatenate([prior_pack[None], pack, next_pack[None]], axis=0)
    ext_blocks = ext[:, :rows]
    ext_whole = ext[:, rows].astype(jnp.int32)
    cols = ext_whole[:, :blocks].reshape(-1)
    sizes = ext_whole[:3, blocks]
    odd = cols % 2
    own = 4 * (cols // 2) + 1 + odd
    other = (own + 4 * odd - 2) % (4 * doms)
    ints = (own, other)

    ops_a, diag_a = slot_op(dual_ops, row_perm[0:1], 0)
    row_forms, col_forms, part = start(sizes, left, right, prior_modes, next_modes, rhs)
    second_perm, _ = lax.optimization_barrier((row_perm[1:2], part))
    everything = trade(part, "dom").reshape(4 * doms, rows, -1)
    ops_b, diag_b = slot_op(dual_ops, second_perm, 1)
    ops = (ops_a, ops_b, diag_a, diag_b)

    centre = 0.5 * (high_bound + low_bound)
    radius = 0.5 * (high_bound - low_bound)
    spread_ratio = centre / radius
    ratios = [1.0 / spread_ratio]
    for _ in range(STEPS - 1):
        ratios.append(1.0 / (2.0 * spread_ratio - ratios[-1]))
    old = [0.0] + [ratios[t] * ratios[t - 1] for t in range(1, STEPS)]
    new = [1.0 / centre] + [2.0 * ratios[t] / radius for t in range(1, STEPS)]
    norms = []
    residual, direction, wa, wb, wc, sums, coarse_fields, links = first(
        new[0], sizes, rhs, prior_rhs, row_forms, col_forms, ops
    )
    solution = None
    for turn in range(STEPS):
        amounts, wa, wc, to_prior, to_next = coarse(
            new[turn], ints, everything, ext_blocks, wa, wc, coarse_fields
        )
        part = share(new[turn], amounts, sums, links)
        from_prior = from_behind(to_next, "dom", 1)
        from_next = from_behind(to_prior, "dom", -1)
        everything = trade(part, "dom").reshape(4 * doms, rows, -1)
        begin, last = turn == 0, turn + 1 == STEPS
        fields = (wa, wb, wc, from_prior, from_next, residual, direction)
        if not begin:
            fields += (solution,)
        if last:
            residual, solution, norm = step(
                begin, last, (new[turn], 0.0, 0.0), sizes, amounts, col_forms, coarse_fields, fields
            )
        else:
            factors = (new[turn], old[turn + 1], new[turn + 1])
            residual, solution, norm, direction, wa, wb, wc, sums = step(
                begin, last, factors, sizes, amounts, col_forms, coarse_fields, fields, row_forms, ops
            )
        if not begin:
            norms.append(norm)
    residual, norm = final(ints, sizes, everything, ext_blocks, col_forms, residual)
    norms.append(norm)
    sums = to_everyone(jnp.concatenate(norms, axis=0), ("dom", "case"))
    cases = lax.axis_size("case")
    totals = jnp.sum(sums.reshape(doms, cases, STEPS, -1), axis=0)
    whole_history = jnp.sqrt(totals + epsilon)
    history = lax.dynamic_index_in_dim(whole_history, lax.axis_index("case"), 0, keepdims=False)
    peak_norm = jnp.max(whole_history, axis=(0, 2))
    return (solution, residual, history, peak_norm)


def solution(mesh):
    in_specs = (
        P("dom", None, None),
        P("dom", None, None),
        P("dom", None, None, None),
        P("dom", None),
        P("dom", None),
        P("dom"),
        P("dom", None, "case"),
    )
    out_specs = (P("dom", None, "case"), P("dom", None, "case"), P(None, "case"), P())
    return jax.shard_map(shards, mesh=mesh, in_specs=in_specs, out_specs=out_specs, check_vma=False)
```

time: 291 us -> 216 us (0.74)
  local copies, waits for them, and re-layouts: 73.8 us -> 13.8 us
  waiting for transfers between devices: 76.3 us -> 19.1 us
  Pallas kernels: 71.9 us -> 113 us
    ppermute x13, waiting for transfers between devices: 65.8 us -> 0.11 us  [from_behind(): return lax.ppermute(block, axis, route)]
    unnamed x132 -> x40, local copies, waits for them, and re-layouts: 63.2 us -> 8.25 us
    pallas_call x0 -> x10, Pallas kernels: none -> 32.6 us  [the longest x4 13.2 us: coarse(): pl.pallas_call(body, out_shape=(jax.ShapeDtypeStruct((4 * modes, lanes),...]
    all_to_all x6, waiting for transfers between devices: 10.5 us -> 19 us  [trade(): return lax.all_to_all(copies, axis, 0, 0, tiled=True)]
    broadcast_in_dim x6 -> x1, local copies, waits for them, and re-layouts: 6.22 us -> 0.73 us  [to_everyone(): return trade(jnp.broadcast_to(value[None], (size, *value.shape)), axis)]
    pallas_call x5 -> x4, Pallas kernels: 27.5 us -> 32.9 us  [step(): pl.pallas_call(body, out_shape=tuple(out), in_specs=specs, out_specs=[VME...]
  transfers between devices with their start and end apart: 19 -> 19, of which waited for: 6 -> 6; matrix products, arithmetic and copies ran while one was open for 1% -> 2% of each run, Pallas kernels for 15% -> 46%
where the time goes in v2:
time: 216 us; the launch traced here: 213 us
  Pallas kernels  113 us (52%)
  starting transfers between devices  62.9 us (29%)
  waiting for transfers between devices  19.1 us (9%)
  local copies, waits for them, and re-layouts  13.8 us (6%)
  other arithmetic  3.34 us (2%)
    pallas_call x2, Pallas kernels, slot_op(): pl.pallas_call(slot_op_kernel, grid=(2 * blocks,), out_shape=(jax.ShapeDt...  42.4 us
    pallas_call x4, Pallas kernels, step(): pl.pallas_call(body, out_shape=tuple(out), in_specs=specs, out_specs=[VME...  32.9 us
    all_to_all x6, starting transfers between devices, trade(): return lax.all_to_all(copies, axis, 0, 0, tiled=True)  32.3 us
    ppermute x13, starting transfers between devices, from_behind(): return lax.ppermute(block, axis, route)  30.6 us
    all_to_all x6, waiting for transfers between devices, trade(): return lax.all_to_all(copies, axis, 0, 0, tiled=True)  19 us
    pallas_call x4, Pallas kernels, coarse(): pl.pallas_call(body, out_shape=(jax.ShapeDtypeStruct((4 * modes, lanes),...  13.2 us
    pallas_call x1, Pallas kernels, first(): pl.pallas_call(body, out_shape=(three, three, field, field, field, jax.Sh...  9.39 us
    unnamed x40, local copies, waits for them, and re-layouts  8.25 us
  transfers between devices with their start and end apart: 19, of which 6 were waited for; matrix products, arithmetic and copies ran while one was open for 2% of the time, Pallas kernels for 46%

profile of v2, /device:TPU:0, one launch (start us, length us, event | category | flops | bytes accessed | tf_op | source)
XLA Modules:
  0.0 213.4 jit_solution(5216812619637244922)
XLA Ops:
  0.6 1.0 copy.20
  1.7 0.7 copy.21
  2.4 0.8 add_convert_fusion
  3.3 6.1 %collective-permute-start.1 = (f32[24,128]{1,0:T(8,128)S(1)}, f32[24,128]{1,0:T(8,128)S(1)}, u32[]{:S(2)}, u32[]{:S(2)}) collective-permute-start(f32[24,128]{1,0:T(8,128)S(1)} %get-tuple-element.143), channel_id=1, source_target_pairs={{4,0},{8,4},{12,8},{16,12},{20,16},{24,20},{28,24},{32,28},{36,32}... | collective-permute-start | bytes 36872 | tf_op jit(solution)/shard_map/ppermute | solution.py:27
  9.4 2.9 %slot_modes.1 = (bf16[2,16,768]{2,1,0:T(8,128)(2,1)}, bf16[2,16,768]{2,1,0:T(8,128)(2,1)}, bf16[16,768]{1,0:T(8,128)(2,1)}, bf16[16,768]{1,0:T(8,128)(2,1)}) custom-call(bf16[2,16,1536]{2,1,0:T(8,128)(2,1)} %modes_ref.1, s32[2,1536]{1,0:T(2,128)} %perm_ref.1), custom_call_target="tpu_custom_call" | custom-call | tf_op jit(solution)/shard_map/slot_modes/pallas_call | solution.py:64
  12.2 5.1 %collective-permute-start.3 = (bf16[16,768]{1,0:T(8,128)(2,1)}, bf16[16,768]{1,0:T(8,128)(2,1)S(1)}, u32[]{:S(2)}, u32[]{:S(2)}) collective-permute-start(bf16[16,768]{1,0:T(8,128)(2,1)} %get-tuple-element.75), channel_id=1, source_target_pairs={{4,0},{8,4},{12,8},{16,12},{20,16},{24,20},{28,24},{32,28},{36,32}... | collective-permute-start | bytes 73736 | tf_op jit(solution)/shard_map/ppermute | solution.py:27
  17.3 1.0 slice_bitcast_fusion
  19.0 21.2 %slot_op.2 = (bf16[1536,1536]{1,0:T(8,128)(2,1)}, f32[1536,128]{1,0:T(8,128)}) custom-call(f32[2,1536,1536]{2,1,0:T(8,128)} %ops_ref.3, s32[1,1536]{1,0:T(1,128)} %get-tuple-element.145.perm_ref), custom_call_target="tpu_custom_call" | custom-call | flops 14495514624 | bytes 14155776 | tf_op jit(solution)/shard_map/slot_op/pallas_call | solution.py:116
  42.8 2.6 %start.1 = (bf16[3,32,768]{2,1,0:T(8,128)(2,1)}, bf16[3,768,64]{2,1,0:T(8,128)(2,1)}, bf16[32,4,16,128]{3,2,1,0:T(8,128)(2,1)}) custom-call(s32[3]{0:T(128)} %slice_reduce_fusion.sizes_ref.refs_0_, bf16[2,16,768]{2,1,0:T(8,128)(2,1)} %get-tuple-element.72.left_ref, bf16[2,16,768]{2,1,0:T(8,128)(2,1)} %get-tuple-element.73.right_ref, ...), custom_call_target="tpu_custom_call" | custom-call | tf_op jit(solution)/shard_map/start/pallas_call | solution.py:192
  45.5 6.9 %all-to-all-start = ((bf16[32,4,16,128]{3,2,1,0:T(8,128)(2,1)}), bf16[32,4,16,128]{3,2,1,0:T(8,128)(2,1)S(1)}, u32[]{:S(2)}, u32[]{:S(2)}) async-start(bf16[32,4,16,128]{3,2,1,0:T(8,128)(2,1)} %get-tuple-element.76), calls=%async_computation | async-start | bytes 1048576 | tf_op jit(solution)/shard_map/all_to_all | solution.py:554
  52.4 21.2 %slot_op.3 = (bf16[1536,1536]{1,0:T(8,128)(2,1)}, f32[1536,128]{1,0:T(8,128)}) custom-call(f32[2,1536,1536]{2,1,0:T(8,128)} %ops_ref.3, s32[1,1536]{1,0:T(1,128)} %get-tuple-element.80.perm_ref), custom_call_target="tpu_custom_call" | custom-call | flops 14495514624 | bytes 14155776 | tf_op jit(solution)/shard_map/slot_op/pallas_call | solution.py:116
  73.6 0.8 copy-done.5
  74.3 9.4 %first.1 = (f32[3,768,128]{2,1,0:T(8,128)}, f32[3,768,128]{2,1,0:T(8,128)}, f32[768,128]{1,0:T(8,128)}, f32[768,128]{1,0:T(8,128)}, f32[768,128]{1,0:T(8,128)}, ...) custom-call(s32[3]{0:T(128)} %slice_reduce_fusion.sizes_ref.refs_0_, ...), custom_call_target="tpu_custom_call" | custom-call | flops 2000000000 | bytes 20000000 | tf_op jit(solution)/shard_map/first/pallas_call | solution.py:334
  83.8 0.8 copy-done.4
  84.6 3.3 %coarse.4 = (f32[64,128]{1,0:T(8,128)}, f32[768,128]{1,0:T(8,128)}, f32[768,128]{1,0:T(8,128)}, bf16[768,128]{1,0:T(8,128)(2,1)}, bf16[768,128]{1,0:T(8,128)(2,1)}) custom-call(s32[32]{0:T(128)} %get-tuple-element.141.refs_0_.own_ref, s32[32]{0:T(128)} %get-tuple-element.140.refs_1_.other_ref, bf16[128,16,128]{2,1,0:T(8,128)(2,1)} %bitcast.26, ...), custom_call_target="tpu_custom_call" | custom-call | flops 100000000 | bytes 4000000 | tf_op jit(solution)/shard_map/coarse/pallas_call | solution.py:409
  87.9 5.0 %collective-permute-start.6 = (bf16[768,128]{1,0:T(8,128)(2,1)}, bf16[768,128]{1,0:T(8,128)(2,1)S(1)}, u32[]{:S(2)}, u32[]{:S(2)}) collective-permute-start(bf16[768,128]{1,0:T(8,128)(2,1)} %get-tuple-element.94), channel_id=1, source_target_pairs={{4,0},{8,4},{12,8},{16,12},{20,16},{24,20},{28,24},{32,28},{36,32}... | collective-permute-start | bytes 589832 | tf_op jit(solution)/shard_map/ppermute | solution.py:27
  92.9 1.8 share.4
  94.7 4.1 %all-to-all-start.1 = ((bf16[32,4,16,128]{3,2,1,0:T(8,128)(2,1)}), bf16[32,4,16,128]{3,2,1,0:T(8,128)(2,1)S(1)}, u32[]{:S(2)}, u32[]{:S(2)}) async-start(bf16[32,4,16,128]{3,2,1,0:T(8,128)(2,1)} %share.4), calls=%async_computation.1 | async-start | bytes 1048576 | tf_op jit(solution)/shard_map/all_to_all | solution.py:554
  99.6 9.3 %step.3 = (f32[3,768,128]{2,1,0:T(8,128)}, f32[2,768,128]{2,1,0:T(8,128)}, f32[1,128]{1,0:T(1,128)}, f32[3,768,128]{2,1,0:T(8,128)}, f32[768,128]{1,0:T(8,128)},...) custom-call(s32[3]{0:T(128)} %slice_reduce_fusion.sizes_ref.refs_0_, ...), custom_call_target="tpu_custom_call" | custom-call | flops 99999997952 | bytes 1000000000 | tf_op jit(solution)/shard_map/step/pallas_call | solution.py:507
  108.9 0.8 all-to-all-done.1
  109.8 0.8 copy-done.1
  110.6 3.3 %coarse.5 = (f32[64,128]{1,0:T(8,128)}, f32[768,128]{1,0:T(8,128)}, f32[768,128]{1,0:T(8,128)}, bf16[768,128]{1,0:T(8,128)(2,1)}, bf16[768,128]{1,0:T(8,128)(2,1)}) custom-call(s32[32]{0:T(128)} %get-tuple-element.141.refs_0_.own_ref, s32[32]{0:T(128)} %get-tuple-element.140.refs_1_.other_ref, bf16[128,16,128]{2,1,0:T(8,128)(2,1)} %bitcast.23, ...), custom_call_target="tpu_custom_call" | custom-call | flops 100000000 | bytes 4000000 | tf_op jit(solution)/shard_map/coarse/pallas_call | solution.py:409
  113.9 0.7 collective-permute-start.7
  114.6 4.4 %collective-permute-start.8 = (bf16[768,128]{1,0:T(8,128)(2,1)}, bf16[768,128]{1,0:T(8,128)(2,1)S(1)}, u32[]{:S(2)}, u32[]{:S(2)}) collective-permute-start(bf16[768,128]{1,0:T(8,128)(2,1)} %get-tuple-element.105), channel_id=1, source_target_pairs={{4,0},{8,4},{12,8},{16,12},{20,16},{24,20},{28,24},{32,28},{36,32}... | collective-permute-start | bytes 589832 | tf_op jit(solution)/shard_map/ppermute | solution.py:27
  119.0 1.8 share.5
  120.8 3.9 %all-to-all-start.2 = ((bf16[32,4,16,128]{3,2,1,0:T(8,128)(2,1)}), bf16[32,4,16,128]{3,2,1,0:T(8,128)(2,1)S(1)}, u32[]{:S(2)}, u32[]{:S(2)}) async-start(bf16[32,4,16,128]{3,2,1,0:T(8,128)(2,1)} %share.5), calls=%async_computation.2 | async-start | bytes 1048576 | tf_op jit(solution)/shard_map/all_to_all | solution.py:554
  125.4 9.6 %step.4 = (f32[3,768,128]{2,1,0:T(8,128)}, f32[2,768,128]{2,1,0:T(8,128)}, f32[1,128]{1,0:T(1,128)}, f32[3,768,128]{2,1,0:T(8,128)}, f32[768,128]{1,0:T(8,128)},...) custom-call(s32[3]{0:T(128)} %slice_reduce_fusion.sizes_ref.refs_0_, ...), custom_call_target="tpu_custom_call" | custom-call | flops 99999997952 | bytes 1000000000 | tf_op jit(solution)/shard_map/step/pallas_call | solution.py:507
  135.0 0.8 all-to-all-done.2
  135.9 0.8 copy-done.2
  136.7 3.3 %coarse.6 = (f32[64,128]{1,0:T(8,128)}, f32[768,128]{1,0:T(8,128)}, f32[768,128]{1,0:T(8,128)}, bf16[768,128]{1,0:T(8,128)(2,1)}, bf16[768,128]{1,0:T(8,128)(2,1)}) custom-call(s32[32]{0:T(128)} %get-tuple-element.141.refs_0_.own_ref, s32[32]{0:T(128)} %get-tuple-element.140.refs_1_.other_ref, bf16[128,16,128]{2,1,0:T(8,128)(2,1)} %bitcast.24, ...), custom_call_target="tpu_custom_call" | custom-call | flops 100000000 | bytes 4000000 | tf_op jit(solution)/shard_map/coarse/pallas_call | solution.py:409
  139.9 4.2 %collective-permute-start.10 = (bf16[768,128]{1,0:T(8,128)(2,1)}, bf16[768,128]{1,0:T(8,128)(2,1)S(1)}, u32[]{:S(2)}, u32[]{:S(2)}) collective-permute-start(bf16[768,128]{1,0:T(8,128)(2,1)} %get-tuple-element.117), channel_id=1, source_target_pairs={{4,0},{8,4},{12,8},{16,12},{20,16},{24,20},{28,24},{32,28},{36,32}... | collective-permute-start | bytes 589832 | tf_op jit(solution)/shard_map/ppermute | solution.py:27
  144.1 1.8 share.6
  145.9 6.7 %all-to-all-start.3 = ((bf16[32,4,16,128]{3,2,1,0:T(8,128)(2,1)}), bf16[32,4,16,128]{3,2,1,0:T(8,128)(2,1)S(1)}, u32[]{:S(2)}, u32[]{:S(2)}) async-start(bf16[32,4,16,128]{3,2,1,0:T(8,128)(2,1)} %share.6), calls=%async_computation.3 | async-start | bytes 1048576 | tf_op jit(solution)/shard_map/all_to_all | solution.py:554
  153.4 9.6 %step.5 = (f32[3,768,128]{2,1,0:T(8,128)}, f32[2,768,128]{2,1,0:T(8,128)}, f32[1,128]{1,0:T(1,128)}, f32[3,768,128]{2,1,0:T(8,128)}, f32[768,128]{1,0:T(8,128)},...) custom-call(s32[3]{0:T(128)} %slice_reduce_fusion.sizes_ref.refs_0_, ...), custom_call_target="tpu_custom_call" | custom-call | flops 99999997952 | bytes 1000000000 | tf_op jit(solution)/shard_map/step/pallas_call | solution.py:507
  163.0 0.8 all-to-all-done.3
  163.8 0.8 copy-done
  164.6 3.3 %coarse.7 = (f32[64,128]{1,0:T(8,128)}, f32[768,128]{1,0:T(8,128)}, f32[768,128]{1,0:T(8,128)}, bf16[768,128]{1,0:T(8,128)(2,1)}, bf16[768,128]{1,0:T(8,128)(2,1)}) custom-call(s32[32]{0:T(128)} %get-tuple-element.141.refs_0_.own_ref, s32[32]{0:T(128)} %get-tuple-element.140.refs_1_.other_ref, bf16[128,16,128]{2,1,0:T(8,128)(2,1)} %bitcast.22, ...), custom_call_target="tpu_custom_call" | custom-call | flops 100000000 | bytes 4000000 | tf_op jit(solution)/shard_map/coarse/pallas_call | solution.py:409
  167.9 0.7 collective-permute-start.11
  168.6 4.4 %collective-permute-start.12 = (bf16[768,128]{1,0:T(8,128)(2,1)}, bf16[768,128]{1,0:T(8,128)(2,1)S(1)}, u32[]{:S(2)}, u32[]{:S(2)}) collective-permute-start(bf16[768,128]{1,0:T(8,128)(2,1)} %get-tuple-element.128), channel_id=1, source_target_pairs={{4,0},{8,4},{12,8},{16,12},{20,16},{24,20},{28,24},{32,28},{36,32}... | collective-permute-start | bytes 589832 | tf_op jit(solution)/shard_map/ppermute | solution.py:27
  172.9 1.8 share.7
  174.7 3.9 %all-to-all-start.4 = ((bf16[32,4,16,128]{3,2,1,0:T(8,128)(2,1)}), bf16[32,4,16,128]{3,2,1,0:T(8,128)(2,1)S(1)}, u32[]{:S(2)}, u32[]{:S(2)}) async-start(bf16[32,4,16,128]{3,2,1,0:T(8,128)(2,1)} %share.7), calls=%async_computation.4 | async-start | bytes 1048576 | tf_op jit(solution)/shard_map/all_to_all | solution.py:554
  179.4 4.4 %last_step.1 = (f32[2,768,128]{2,1,0:T(8,128)}, f32[2,768,128]{2,1,0:T(8,128)}, f32[1,128]{1,0:T(1,128)}) custom-call(s32[3]{0:T(128)} %slice_reduce_fusion.sizes_ref.refs_0_, f32[64,128]{1,0:T(8,128)} %get-tuple-element.123.refs_1_.refs_0_, bf16[3,768,64]{2,1,0:T(8,128)(2,1)} %get-tuple-element.78.refs_4_.refs_2_.cols_ref, ...), custom_call_target="tpu_custom_call" | custom-call | flops 99999997952 | bytes 1000000000 | tf_op jit(solution)/shard_map/last_step/pallas_call | solution.py:507
  183.8 6.0 %all-to-all-done.4 = bf16[32,4,16,128]{3,2,1,0:T(8,128)(2,1)S(1)} async-done(((bf16[32,4,16,128]{3,2,1,0:T(8,128)(2,1)}), bf16[32,4,16,128]{3,2,1,0:T(8,128)(2,1)S(1)}, u32[]{:S(2)}, u32[]{:S(2)}) %all-to-all-start.4) | async-done | bytes 524320 | tf_op jit(solution)/shard_map/all_to_all | solution.py:554
  189.8 0.8 copy-done.3
  190.6 2.8 %final.1 = (f32[2,768,128]{2,1,0:T(8,128)}, f32[1,128]{1,0:T(1,128)}) custom-call(s32[32]{0:T(128)} %get-tuple-element.141.refs_0_.own_ref, s32[32]{0:T(128)} %get-tuple-element.140.refs_1_.other_ref, s32[3]{0:T(128)} %slice_reduce_fusion.sizes_ref.refs_0_, bf16[128,16,128]{2,1,0:T(8,128)(2,1)} %bitcast.25, ...), custom_call_target="tpu_custom_call" | custom-call | tf_op jit(solution)/shard_map/final/pallas_call | solution.py:539
  194.1 0.7 broadcast_in_dim.25
  194.9 6.8 %all-to-all-start.5 = ((f32[128,4,128]{2,1,0:T(4,128)}), f32[128,4,128]{2,1,0:T(4,128)S(1)}, u32[]{:S(2)}, u32[]{:S(2)}) async-start(f32[128,4,128]{2,1,0:T(4,128)} %broadcast_in_dim.25), calls=%async_computation.5 | async-start | bytes 524288 | tf_op jit(solution)/shard_map/all_to_all | solution.py:554
  201.6 10.5 %all-to-all-done.5 = f32[128,4,128]{2,1,0:T(4,128)S(1)} async-done(((f32[128,4,128]{2,1,0:T(4,128)}), f32[128,4,128]{2,1,0:T(4,128)S(1)}, u32[]{:S(2)}, u32[]{:S(2)}) %all-to-all-start.5) | async-done | bytes 262176 | tf_op jit(solution)/shard_map/all_to_all | solution.py:554
  (67 shorter events, 8.5 us)
Async XLA Ops:
  0.6 17.8 %copy-start.6 = (s32[2,1536]{1,0:T(2,128)S(1)}, s32[2,1536]{1,0:T(2,128)}, u32[]{:S(2)}) copy-start(s32[2,1536]{1,0:T(2,128)} %perm_ref.1) | copy-start | bytes 36868
  3.2 37.0 %collective-permute-start = (f32[24,128]{1,0:T(8,128)S(1)}, f32[24,128]{1,0:T(8,128)S(1)}, u32[]{:S(2)}, u32[]{:S(2)}) collective-permute-start(f32[24,128]{1,0:T(8,128)S(1)} %get-tuple-element.142), channel_id=1, source_target_pairs={{124,0},{0,4},{4,8},{8,12},{12,16},{16,20},{20,24},{24,28},{28,32}... | collective-permute-start | bytes 36872 | tf_op jit(solution)/shard_map/ppermute | solution.py:27
  3.3 36.9 %collective-permute-start.1 = (f32[24,128]{1,0:T(8,128)S(1)}, f32[24,128]{1,0:T(8,128)S(1)}, u32[]{:S(2)}, u32[]{:S(2)}) collective-permute-start(f32[24,128]{1,0:T(8,128)S(1)} %get-tuple-element.143), channel_id=1, source_target_pairs={{4,0},{8,4},{12,8},{16,12},{20,16},{24,20},{28,24},{32,28},{36,32}... | collective-permute-start | bytes 36872 | tf_op jit(solution)/shard_map/ppermute | solution.py:27
  12.2 30.0 %collective-permute-start.2 = (bf16[16,768]{1,0:T(8,128)(2,1)}, bf16[16,768]{1,0:T(8,128)(2,1)S(1)}, u32[]{:S(2)}, u32[]{:S(2)}) collective-permute-start(bf16[16,768]{1,0:T(8,128)(2,1)} %get-tuple-element.74), channel_id=1, source_target_pairs={{124,0},{0,4},{4,8},{8,12},{12,16},{16,20},{20,24},{24,28},{28,32}... | collective-permute-start | bytes 73736 | tf_op jit(solution)/shard_map/ppermute | solution.py:27
  12.2 30.0 %collective-permute-start.3 = (bf16[16,768]{1,0:T(8,128)(2,1)}, bf16[16,768]{1,0:T(8,128)(2,1)S(1)}, u32[]{:S(2)}, u32[]{:S(2)}) collective-permute-start(bf16[16,768]{1,0:T(8,128)(2,1)} %get-tuple-element.75), channel_id=1, source_target_pairs={{4,0},{8,4},{12,8},{16,12},{20,16},{24,20},{28,24},{32,28},{36,32}... | collective-permute-start | bytes 73736 | tf_op jit(solution)/shard_map/ppermute | solution.py:27
  18.3 55.2 %collective-permute-start.4 = (f32[768,128]{1,0:T(8,128)S(1)}, f32[768,128]{1,0:T(8,128)S(1)}, u32[]{:S(2)}, u32[]{:S(2)}) collective-permute-start(f32[768,128]{1,0:T(8,128)S(1)} %slice_bitcast_fusion), channel_id=1, source_target_pairs={{124,0},{0,4},{4,8},{8,12},{12,16},{16,20},{20,24},{24,28},{28,32}... | collective-permute-start | bytes 1179656 | tf_op jit(solution)/shard_map/ppermute | solution.py:27
  42.2 0.6 copy-start.7
  42.2 0.6 copy-start.8
  45.5 38.3 %all-to-all-start = ((bf16[32,4,16,128]{3,2,1,0:T(8,128)(2,1)}), bf16[32,4,16,128]{3,2,1,0:T(8,128)(2,1)S(1)}, u32[]{:S(2)}, u32[]{:S(2)}) async-start(bf16[32,4,16,128]{3,2,1,0:T(8,128)(2,1)} %get-tuple-element.76), calls=%async_computation | async-start | bytes 1048576 | tf_op jit(solution)/shard_map/all_to_all | solution.py:554
  73.6 0.8 copy-start.5
  83.7 0.8 copy-start.4
  87.8 11.0 %collective-permute-start.5 = (bf16[768,128]{1,0:T(8,128)(2,1)}, bf16[768,128]{1,0:T(8,128)(2,1)S(1)}, u32[]{:S(2)}, u32[]{:S(2)}) collective-permute-start(bf16[768,128]{1,0:T(8,128)(2,1)} %get-tuple-element.93), channel_id=1, source_target_pairs={{124,0},{0,4},{4,8},{8,12},{12,16},{16,20},{20,24},{24,28},{28,32}... | collective-permute-start | bytes 589832 | tf_op jit(solution)/shard_map/ppermute | solution.py:27
  87.9 10.9 %collective-permute-start.6 = (bf16[768,128]{1,0:T(8,128)(2,1)}, bf16[768,128]{1,0:T(8,128)(2,1)S(1)}, u32[]{:S(2)}, u32[]{:S(2)}) collective-permute-start(bf16[768,128]{1,0:T(8,128)(2,1)} %get-tuple-element.94), channel_id=1, source_target_pairs={{4,0},{8,4},{12,8},{16,12},{20,16},{24,20},{28,24},{32,28},{36,32}... | collective-permute-start | bytes 589832 | tf_op jit(solution)/shard_map/ppermute | solution.py:27
  94.7 15.1 %all-to-all-start.1 = ((bf16[32,4,16,128]{3,2,1,0:T(8,128)(2,1)}), bf16[32,4,16,128]{3,2,1,0:T(8,128)(2,1)S(1)}, u32[]{:S(2)}, u32[]{:S(2)}) async-start(bf16[32,4,16,128]{3,2,1,0:T(8,128)(2,1)} %share.4), calls=%async_computation.1 | async-start | bytes 1048576 | tf_op jit(solution)/shard_map/all_to_all | solution.py:554
  98.8 0.7 copy-start.15
  98.9 0.7 copy-start.17
  109.8 0.8 copy-start.1
  113.9 10.8 %collective-permute-start.7 = (bf16[768,128]{1,0:T(8,128)(2,1)}, bf16[768,128]{1,0:T(8,128)(2,1)S(1)}, u32[]{:S(2)}, u32[]{:S(2)}) collective-permute-start(bf16[768,128]{1,0:T(8,128)(2,1)} %get-tuple-element.104), channel_id=1, source_target_pairs={{124,0},{0,4},{4,8},{8,12},{12,16},{16,20},{20,24},{24,28},{28,32}... | collective-permute-start | bytes 589832 | tf_op jit(solution)/shard_map/ppermute | solution.py:27
  114.6 10.1 %collective-permute-start.8 = (bf16[768,128]{1,0:T(8,128)(2,1)}, bf16[768,128]{1,0:T(8,128)(2,1)S(1)}, u32[]{:S(2)}, u32[]{:S(2)}) collective-permute-start(bf16[768,128]{1,0:T(8,128)(2,1)} %get-tuple-element.105), channel_id=1, source_target_pairs={{4,0},{8,4},{12,8},{16,12},{20,16},{24,20},{28,24},{32,28},{36,32}... | collective-permute-start | bytes 589832 | tf_op jit(solution)/shard_map/ppermute | solution.py:27
  120.8 15.1 %all-to-all-start.2 = ((bf16[32,4,16,128]{3,2,1,0:T(8,128)(2,1)}), bf16[32,4,16,128]{3,2,1,0:T(8,128)(2,1)S(1)}, u32[]{:S(2)}, u32[]{:S(2)}) async-start(bf16[32,4,16,128]{3,2,1,0:T(8,128)(2,1)} %share.5), calls=%async_computation.2 | async-start | bytes 1048576 | tf_op jit(solution)/shard_map/all_to_all | solution.py:554
  124.7 0.7 copy-start.14
  124.7 0.7 copy-start.16
  135.9 0.8 copy-start.2
  139.9 12.7 %collective-permute-start.10 = (bf16[768,128]{1,0:T(8,128)(2,1)}, bf16[768,128]{1,0:T(8,128)(2,1)S(1)}, u32[]{:S(2)}, u32[]{:S(2)}) collective-permute-start(bf16[768,128]{1,0:T(8,128)(2,1)} %get-tuple-element.117), channel_id=1, source_target_pairs={{4,0},{8,4},{12,8},{16,12},{20,16},{24,20},{28,24},{32,28},{36,32}... | collective-permute-start | bytes 589832 | tf_op jit(solution)/shard_map/ppermute | solution.py:27
  144.1 8.6 %collective-permute-start.9 = (bf16[768,128]{1,0:T(8,128)(2,1)}, bf16[768,128]{1,0:T(8,128)(2,1)S(1)}, u32[]{:S(2)}, u32[]{:S(2)}) collective-permute-start(bf16[768,128]{1,0:T(8,128)(2,1)} %get-tuple-element.116), channel_id=1, source_target_pairs={{124,0},{0,4},{4,8},{8,12},{12,16},{16,20},{20,24},{24,28},{28,32}... | collective-permute-start | bytes 589832 | tf_op jit(solution)/shard_map/ppermute | solution.py:27
  145.9 17.9 %all-to-all-start.3 = ((bf16[32,4,16,128]{3,2,1,0:T(8,128)(2,1)}), bf16[32,4,16,128]{3,2,1,0:T(8,128)(2,1)S(1)}, u32[]{:S(2)}, u32[]{:S(2)}) async-start(bf16[32,4,16,128]{3,2,1,0:T(8,128)(2,1)} %share.6), calls=%async_computation.3 | async-start | bytes 1048576 | tf_op jit(solution)/shard_map/all_to_all | solution.py:554
  152.6 0.7 copy-start.12
  152.7 0.7 copy-start.13
  163.8 0.8 copy-start
  167.9 10.8 %collective-permute-start.11 = (bf16[768,128]{1,0:T(8,128)(2,1)}, bf16[768,128]{1,0:T(8,128)(2,1)S(1)}, u32[]{:S(2)}, u32[]{:S(2)}) collective-permute-start(bf16[768,128]{1,0:T(8,128)(2,1)} %get-tuple-element.127), channel_id=1, source_target_pairs={{124,0},{0,4},{4,8},{8,12},{12,16},{16,20},{20,24},{24,28},{28,32}... | collective-permute-start | bytes 589832 | tf_op jit(solution)/shard_map/ppermute | solution.py:27
  168.6 10.1 %collective-permute-start.12 = (bf16[768,128]{1,0:T(8,128)(2,1)}, bf16[768,128]{1,0:T(8,128)(2,1)S(1)}, u32[]{:S(2)}, u32[]{:S(2)}) collective-permute-start(bf16[768,128]{1,0:T(8,128)(2,1)} %get-tuple-element.128), channel_id=1, source_target_pairs={{4,0},{8,4},{12,8},{16,12},{20,16},{24,20},{28,24},{32,28},{36,32}... | collective-permute-start | bytes 589832 | tf_op jit(solution)/shard_map/ppermute | solution.py:27
  174.7 15.1 %all-to-all-start.4 = ((bf16[32,4,16,128]{3,2,1,0:T(8,128)(2,1)}), bf16[32,4,16,128]{3,2,1,0:T(8,128)(2,1)S(1)}, u32[]{:S(2)}, u32[]{:S(2)}) async-start(bf16[32,4,16,128]{3,2,1,0:T(8,128)(2,1)} %share.7), calls=%async_computation.4 | async-start | bytes 1048576 | tf_op jit(solution)/shard_map/all_to_all | solution.py:554
  178.6 0.7 copy-start.18
  178.7 0.7 copy-start.19
  183.8 9.6 %copy-start.9 = (f32[1,128]{1,0:T(1,128)S(1)}, f32[1,128]{1,0:T(1,128)}, u32[]{:S(2)}) copy-start(f32[1,128]{1,0:T(1,128)} %get-tuple-element.136) | copy-start | bytes 1540
  183.8 9.6 %copy-start.10 = (f32[1,128]{1,0:T(1,128)S(1)}, f32[1,128]{1,0:T(1,128)}, u32[]{:S(2)}) copy-start(f32[1,128]{1,0:T(1,128)} %get-tuple-element.137) | copy-start | bytes 1540
  183.8 9.6 %copy-start.11 = (f32[1,128]{1,0:T(1,128)S(1)}, f32[1,128]{1,0:T(1,128)}, u32[]{:S(2)}) copy-start(f32[1,128]{1,0:T(1,128)} %get-tuple-element.138) | copy-start | bytes 1540
  189.8 0.8 copy-start.3
  194.9 17.3 %all-to-all-start.5 = ((f32[128,4,128]{2,1,0:T(4,128)}), f32[128,4,128]{2,1,0:T(4,128)S(1)}, u32[]{:S(2)}, u32[]{:S(2)}) async-start(f32[128,4,128]{2,1,0:T(4,128)} %broadcast_in_dim.25), calls=%async_computation.5 | async-start | bytes 524288 | tf_op jit(solution)/shard_map/all_to_all | solution.py:554

commit v3 on v2

--- a/solution.py
+++ b/solution.py
@@ -18,7 +18,7 @@
 VMEM = pl.BlockSpec(memory_space=pltpu.VMEM)
 SMEM = pl.BlockSpec(memory_space=pltpu.SMEM)
 ANY = pl.BlockSpec(memory_space=pl.ANY)
-PARAMS = pltpu.CompilerParams(vmem_limit_bytes=60 * 1024 * 1024)
+PARAMS = pltpu.CompilerParams(vmem_limit_bytes=53000000)
 
 
 def from_behind(block, axis, distance):
@@ -37,38 +37,75 @@
     return high, low
 
 
-def slot_modes_kernel(modes_ref, perm_ref, left_ref, right_ref, to_next_ref, to_prior_ref):
+def prepare_kernel(
+    cols_ref, size_ref, modes_ref, perm_ref, coarse_ref, rhs_ref,
+    left_ref, right_ref, own_ref, to_next_ref, to_prior_ref, rhs_rim, sem,
+):
     count, rows, width = modes_ref.shape
     half = width // 2
+    blocks = coarse_ref.shape[1]
+    copy = pltpu.make_async_copy(rhs_ref.at[count - 1], rhs_rim, sem)
+    copy.start()
+    lane = lax.broadcasted_iota(jnp.int32, (8, 128), 1)
     for s in range(count):
+        whole = jnp.zeros((8, 128), jnp.int32)
+        for q in range(blocks):
+            whole = jnp.where(lane == q, cols_ref[s, q], whole)
+        whole = jnp.where(lane == blocks, size_ref[s], whole).astype(f32)
+        flat = jnp.concatenate([coarse_ref[s, q] for q in range(blocks)], axis=1)
+        both = jnp.concatenate([flat, whole], axis=0)
+        own_ref[s] = both
+        if s == 0:
+            to_prior_ref[: rows + 8] = both
+        if s == count - 1:
+            to_next_ref[: rows + 8] = both
         for at in range(0, width, BLK):
             one_hot = (
                 lax.broadcasted_iota(jnp.int32, (width, BLK), 0) == perm_ref[s : s + 1, at : at + BLK]
             ).astype(f32).astype(bf16)
-            part = dot(modes_ref[s], one_hot).astype(bf16)
-            if at < half:
-                left_ref[s, :, at : at + BLK] = part
-                if s == 0:
-                    to_prior_ref[:, at : at + BLK] = part
-            else:
-                right_ref[s, :, at - half : at - half + BLK] = part
-                if s == count - 1:
-                    to_next_ref[:, at - half : at - half + BLK] = part
-
-
-def slot_modes(modes, row_perm):
+            part = dot(modes_ref[s], one_hot)
+            side, place = (left_ref, at) if at < half else (right_ref, at - half)
+            side[s, :, place : place + BLK] = part.astype(bf16)
+            rim = None
+            if at < half and s == 0:
+                rim = to_prior_ref
+            if at >= half and s == count - 1:
+                rim = to_next_ref
+            if rim is not None:
+                for k in range(0, BLK, 128):
+                    row = rows + 8 + (place + k) // 128 * rows
+                    rim[row : row + rows] = part[:, k : k + 128]
+    copy.wait()
+
+
+def prepare(coarse_cols, iface_size, modes, row_perm, coarse_rows, rhs):
     count, rows, width = modes.shape
     half = width // 2
     side = jax.ShapeDtypeStruct((count, rows, half), bf16)
-    rim = jax.ShapeDtypeStruct((rows, half), bf16)
+    rim = jax.ShapeDtypeStruct((rows + 8 + half // 128 * rows, 128), f32)
     return pl.pallas_call(
-        slot_modes_kernel,
-        out_shape=(side, side, rim, rim),
-        in_specs=[VMEM, VMEM],
-        out_specs=[VMEM] * 4,
+        prepare_kernel,
+        out_shape=(
+            side,
+            side,
+            jax.ShapeDtypeStruct((count, rows + 8, 128), f32),
+            rim,
+            rim,
+            jax.ShapeDtypeStruct(rhs.shape[1:], f32),
+        ),
+        in_specs=[SMEM, SMEM, VMEM, VMEM, VMEM, ANY],
+        out_specs=[VMEM] * 5 + [ANY],
+        scratch_shapes=[pltpu.SemaphoreType.DMA(())],
         compiler_params=PARAMS,
-        name="slot_modes",
-    )(modes, row_perm)
+        name="prepare",
+    )(coarse_cols, iface_size, modes, row_perm, coarse_rows, rhs)
+
+
+def rim_modes(rim_ref, rows, half):
+    first_row = rows + 8
+    return jnp.concatenate(
+        [rim_ref[first_row + k * rows : first_row + (k + 1) * rows] for k in range(half // 128)], axis=1
+    )
 
 
 def slot_op_kernel(ops_ref, perm_ref, out_ref, diag_ref, cols_done, one_hot, diag_row):
@@ -168,13 +205,14 @@
 
 
 def start_kernel(
-    sizes_ref, left_ref, right_ref, prior_ref, next_ref, rhs_ref, rows_ref, cols_ref, part_ref
+    count, ints_ref, left_ref, right_ref, prior_ref, next_ref, rhs_ref, rows_ref, cols_ref, part_ref
 ):
     half = rhs_ref.shape[1]
+    modes = left_ref.shape[1]
     pairs = [
-        (prior_ref[...], left_ref[0]),
+        (rim_modes(prior_ref, modes, half), left_ref[0]),
         (right_ref[0], left_ref[1]),
-        (right_ref[1], next_ref[...]),
+        (right_ref[1], rim_modes(next_ref, modes, half)),
     ]
     for e, (above, below) in enumerate(pairs):
         stack = jnp.concatenate([above.astype(f32), -below.astype(f32)], axis=0)
@@ -182,15 +220,19 @@
         cols_ref[e] = jnp.transpose(jnp.concatenate([stack, stack], axis=0)).astype(bf16)
     shares = [None]
     for e in range(2):
-        shares.append(jnp.where(alive(sizes_ref[e + 1], half), -rhs_ref[e], 0.0))
+        shares.append(jnp.where(alive(ints_ref[0, e + 1, count], half), -rhs_ref[e], 0.0))
     partial_coefficients(rows_ref, shares, part_ref)
 
 
-def start(sizes, left, right, prior, following, rhs):
+def start(count, ints, left, right, prior, following, rhs):
     half = rhs.shape[1]
     modes = left.shape[1]
+
+    def body(*refs):
+        start_kernel(count, *refs)
+
     return pl.pallas_call(
-        start_kernel,
+        body,
         out_shape=(
             jax.ShapeDtypeStruct((3, 2 * modes, half), bf16),
             jax.ShapeDtypeStruct((3, half, 4 * modes), bf16),
@@ -200,7 +242,7 @@
         out_specs=[VMEM] * 3,
         compiler_params=PARAMS,
         name="start",
-    )(sizes, left, right, prior, following, rhs)
+    )(ints, left, right, prior, following, rhs)
 
 
 def triple(value):
@@ -257,17 +299,19 @@
     return sides
 
 
-def take_amounts(own_ref, other_ref, all_ref, blocks_ref, picked):
+def take_amounts(ints_ref, all_ref, packs, picked):
+    prior_ref, own_ref, next_ref = packs
     modes = all_ref.shape[1]
-    subs, _, width = blocks_ref.shape
+    width = picked.shape[1] // 2
     count = width // modes
+    blocks = [prior_ref[:modes], own_ref[0, :modes], own_ref[1, :modes], next_ref[:modes]]
     amounts = []
-    for s in range(subs):
+    for s, block in enumerate(blocks):
         for q in range(count):
             here = q * modes
-            picked[s, here : here + modes, :] = all_ref[own_ref[s * count + q]]
-            picked[s, width + here : width + here + modes, :] = all_ref[other_ref[s * count + q]]
-        high, low = split(blocks_ref[s])
+            picked[s, here : here + modes, :] = all_ref[ints_ref[1, s, q]]
+            picked[s, width + here : width + here + modes, :] = all_ref[ints_ref[2, s, q]]
+        high, low = split(block)
         rows = jnp.concatenate([high, low], axis=0)
         both = dot(jnp.concatenate([rows, rows], axis=1), picked[s])
         amounts.append(both[:modes] + both[modes:])
@@ -275,7 +319,7 @@
 
 
 def first_kernel(
-    scale, sizes_ref, rhs_ref, prior_ref, rows_ref, cols_ref, op_a, op_b, diag_a, diag_b,
+    scale, count, ints_ref, rhs_ref, prior_ref, rows_ref, cols_ref, op_a, op_b, diag_a, diag_b,
     res_out, dir_out, wa_out, wb_out, wc_out, sums_out, fields_out, links_out,
     held, slots, wide, sems,
 ):
@@ -285,7 +329,7 @@
         copies[-1].start()
     half = rhs_ref.shape[1]
     modes = rows_ref.shape[1] // 2
-    live = [alive(sizes_ref[e], half) for e in range(3)]
+    live = [alive(ints_ref[0, e, count], half) for e in range(3)]
     for e in range(3):
         start = jnp.where(live[e], prior_ref[...] if e == 0 else rhs_ref[e - 1], 0.0)
         direction = scale * start
@@ -322,14 +366,14 @@
     ]
 
 
-def first(scale, sizes, rhs, prior_rhs, rows, cols, ops):
+def first(scale, count, ints, rhs, prior_rhs, rows, cols, ops):
     half, lanes = rhs.shape[1:]
     modes = rows.shape[1] // 2
     field = jax.ShapeDtypeStruct((half, lanes), f32)
     three = jax.ShapeDtypeStruct((3, half, lanes), f32)
 
     def body(*refs):
-        first_kernel(scale, *refs)
+        first_kernel(scale, count, *refs)
 
     return pl.pallas_call(
         body,
@@ -352,54 +396,32 @@
             flops=2 * 10**9, bytes_accessed=2 * 10**7, transcendentals=0
         ),
         name="first",
-    )(sizes, rhs, prior_rhs, rows, cols, *ops)
+    )(ints, rhs, prior_rhs, rows, cols, *ops)
 
 
 def coarse_kernel(
-    new, own_ref, other_ref, all_ref, blocks_ref, wa_ref, wc_ref, fields_ref,
-    amounts_out, wa_out, wc_out, to_prior_out, to_next_out, picked,
+    new, ints_ref, all_ref, prior_ref, own_ref, next_ref,
+    wa_ref, wc_ref, sums_ref, fields_ref, links_ref,
+    amounts_out, wa_out, wc_out, to_prior_out, to_next_out, part_out, picked,
 ):
-    amounts = take_amounts(own_ref, other_ref, all_ref, blocks_ref, picked)
+    amounts = take_amounts(ints_ref, all_ref, (prior_ref, own_ref, next_ref), picked)
     amounts_out[...] = amounts
     scaled = triple_rows(new * amounts)
+    modes = part_out.shape[2]
+    sums = (sums_ref[...] + dot(links_ref[...], scaled)).astype(bf16)
+    for k in range(4):
+        for device in range(part_out.shape[0]):
+            part_out[device, k] = sums[k * modes : (k + 1) * modes]
     wa = wa_ref[...] + dot(fields_ref[0], scaled)
     wc = wc_ref[...] + dot(fields_ref[2], scaled)
     wa_out[...], wc_out[...] = wa, wc
     to_prior_out[...], to_next_out[...] = wa.astype(bf16), wc.astype(bf16)
 
 
-def share_kernel(new, amounts_ref, sums_ref, links_ref, part_out):
-    modes = part_out.shape[2]
-    scaled = triple_rows(new * amounts_ref[...])
-    sums = (sums_ref[...] + dot(links_ref[...], scaled)).astype(bf16)
-    for k in range(4):
-        for device in range(part_out.shape[0]):
-            part_out[device, k] = sums[k * modes : (k + 1) * modes]
-
-
-def share(new, amounts, sums, links):
-    rows, lanes = amounts.shape
-
-    def body(*refs):
-        share_kernel(new, *refs)
-
-    return pl.pallas_call(
-        body,
-        out_shape=jax.ShapeDtypeStruct((lax.axis_size("dom"), 4, rows // 4, lanes), bf16),
-        in_specs=[VMEM] * 3,
-        out_specs=VMEM,
-        compiler_params=PARAMS,
-        cost_estimate=pl.CostEstimate(
-            flops=10**11, bytes_accessed=10**9, transcendentals=0
-        ),
-        name="share",
-    )(amounts, sums, links)
-
-
-def coarse(new, ints, everything, blocks, wa, wc, fields):
+def coarse(new, ints, everything, packs, wa, wc, sums, fields, links):
     modes = everything.shape[1]
     half, lanes = wa.shape
-    subs, _, width = blocks.shape
+    subs, width = 4, packs[0].shape[1]
     field = jax.ShapeDtypeStruct((half, lanes), f32)
     rim = jax.ShapeDtypeStruct((half, lanes), bf16)
 
@@ -414,22 +436,23 @@
             field,
             rim,
             rim,
-        ),
-        in_specs=[SMEM, SMEM] + [VMEM] * 5,
-        out_specs=[VMEM] * 5,
+            jax.ShapeDtypeStruct((everything.shape[0] // 4, 4, modes, lanes), bf16),
+        ),
+        in_specs=[SMEM] + [VMEM] * 9,
+        out_specs=[VMEM] * 6,
         scratch_shapes=[pltpu.VMEM((subs, 2 * width, lanes), bf16)],
         compiler_params=PARAMS,
         cost_estimate=pl.CostEstimate(
             flops=10**8, bytes_accessed=4 * 10**6, transcendentals=0
         ),
         name="coarse",
-    )(*ints, everything, blocks, wa, wc, fields)
-
-
-def step_kernel(begin, last, new, old_next, new_next, *refs):
+    )(ints, everything, *packs, wa, wc, sums, fields, links)
+
+
+def step_kernel(count, begin, last, new, old_next, new_next, *refs):
     refs = list(refs)
     take = lambda n: [refs.pop(0) for _ in range(n)]
-    (sizes_ref, amounts_ref, cols_ref, fields_ref) = take(4)
+    (ints_ref, amounts_ref, cols_ref, fields_ref) = take(4)
     wa_ref, wb_ref, wc_ref, prior_ref, next_ref, res_ref, dir_ref = take(7)
     sol_ref = None if begin else take(1)[0]
     if not last:
@@ -446,7 +469,7 @@
     modes = amounts_ref.shape[0] // 4
     amounts = amounts_ref[...]
     high, low = split(amounts)
-    live = [alive(sizes_ref[e], half) for e in range(3)]
+    live = [alive(ints_ref[0, e, count], half) for e in range(3)]
     total = jnp.zeros((1, 128), f32)
     for e in range(3):
         if last and e == 0:
@@ -486,13 +509,13 @@
     sums_out[...] = share_sums(rows_ref, shares)
 
 
-def step(begin, last, factors, sizes, amounts, cols, coarse_fields, fields, rows=None, ops=()):
+def step(count, begin, last, factors, ints, amounts, cols, coarse_fields, fields, rows=None, ops=()):
     half, lanes = fields[0].shape
     field = jax.ShapeDtypeStruct((half, lanes), f32)
     three = jax.ShapeDtypeStruct((3, half, lanes), f32)
     two = jax.ShapeDtypeStruct((2, half, lanes), f32)
     out = [two if last else three, two, jax.ShapeDtypeStruct((1, lanes), f32)]
-    args = [sizes, amounts, cols, coarse_fields, *fields]
+    args = [ints, amounts, cols, coarse_fields, *fields]
     specs = [SMEM] + [VMEM] * (len(args) - 1)
     scratch = []
     if not last:
@@ -502,7 +525,7 @@
         specs += [VMEM, ANY, ANY, VMEM, VMEM]
 
     def body(*refs):
-        step_kernel(begin, last, *factors, *refs)
+        step_kernel(count, begin, last, *factors, *refs)
 
     return pl.pallas_call(
         body,
@@ -518,8 +541,11 @@
     )(*args)
 
 
-def final_kernel(own_ref, other_ref, sizes_ref, all_ref, blocks_ref, cols_ref, res_ref, res_out, norm_out, picked):
-    amounts = take_amounts(own_ref, other_ref, all_ref, blocks_ref, picked)
+def final_kernel(
+    count, ints_ref, all_ref, prior_ref, own_ref, next_ref, cols_ref, res_ref, norm_a, norm_b, norm_c,
+    res_out, norm_out, picked,
+):
+    amounts = take_amounts(ints_ref, all_ref, (prior_ref, own_ref, next_ref), picked)
     modes = amounts.shape[0] // 4
     half = res_ref.shape[1]
     high, low = split(amounts)
@@ -527,63 +553,61 @@
     for e in range(1, 3):
         at = slice(e * modes, (e + 2) * modes)
         spread = dot(cols_ref[e], jnp.concatenate([high[at], low[at]], axis=0))
-        residual = res_ref[e - 1] + jnp.where(alive(sizes_ref[e], half), spread, 0.0)
+        residual = res_ref[e - 1] + jnp.where(alive(ints_ref[0, e, count], half), spread, 0.0)
         res_out[e - 1] = residual
         total += jnp.sum(residual * residual, axis=0, keepdims=True)
-    norm_out[...] = total
-
-
-def final(ints, sizes, everything, blocks, cols, residual):
-    subs, _, width = blocks.shape
+    norms = jnp.concatenate([norm_a[...], norm_b[...], norm_c[...], total], axis=0)
+    for device in range(norm_out.shape[0]):
+        norm_out[device] = norms
+
+
+def final(count, ints, everything, packs, cols, residual, norms, devices):
+    subs, width = 4, packs[0].shape[1]
     lanes = residual.shape[-1]
+
+    def body(*refs):
+        final_kernel(count, *refs)
+
     return pl.pallas_call(
-        final_kernel,
+        body,
         out_shape=(
             jax.ShapeDtypeStruct(residual.shape, f32),
-            jax.ShapeDtypeStruct((1, lanes), f32),
-        ),
-        in_specs=[SMEM] * 3 + [VMEM] * 4,
+            jax.ShapeDtypeStruct((devices, STEPS, lanes), f32),
+        ),
+        in_specs=[SMEM] + [VMEM] * 9,
         out_specs=[VMEM] * 2,
         scratch_shapes=[pltpu.VMEM((subs, 2 * width, lanes), bf16)],
         compiler_params=PARAMS,
         name="final",
-    )(*ints, sizes, everything, blocks, cols, residual)
+    )(ints, everything, *packs, cols, residual, *norms)
 
 
 def trade(copies, axis):
     return lax.all_to_all(copies, axis, 0, 0, tiled=True)
-
-
-def to_everyone(value, axis):
-    size = lax.psum(1, axis)
-    return trade(jnp.broadcast_to(value[None], (size, *value.shape)), axis)
 
 
 def shards(dual_ops, modes, coarse_rows, coarse_cols, row_perm, iface_size, rhs):
     doms = lax.axis_size("dom")
     count, blocks, rows, _ = coarse_rows.shape
-    flat = jnp.swapaxes(coarse_rows, 1, 2).reshape(count, rows, blocks * rows)
-    whole = jnp.concatenate([coarse_cols, iface_size[:, None]], axis=1).astype(f32)
-    whole = jnp.pad(whole, ((0, 0), (0, blocks * rows - whole.shape[1])))
-    pack = jnp.concatenate([flat, jnp.broadcast_to(whole[:, None], (count, 8, blocks * rows))], axis=1)
-    prior_pack = from_behind(pack[-1], "dom", 1)
-    next_pack = from_behind(pack[0], "dom", -1)
-    prior_rhs = from_behind(rhs[-1], "dom", 1)
-    left, right, to_next, to_prior = slot_modes(modes, row_perm)
-    prior_modes = from_behind(to_next, "dom", 1)
-    next_modes = from_behind(to_prior, "dom", -1)
-    ext = jnp.concatenate([prior_pack[None], pack, next_pack[None]], axis=0)
-    ext_blocks = ext[:, :rows]
-    ext_whole = ext[:, rows].astype(jnp.int32)
-    cols = ext_whole[:, :blocks].reshape(-1)
-    sizes = ext_whole[:3, blocks]
-    odd = cols % 2
-    own = 4 * (cols // 2) + 1 + odd
-    other = (own + 4 * odd - 2) % (4 * doms)
-    ints = (own, other)
+    left, right, own_pack, to_next, to_prior, rhs_rim = prepare(
+        coarse_cols, iface_size, modes, row_perm, coarse_rows, rhs
+    )
+    prior_pack = from_behind(to_next, "dom", 1)
+    next_pack = from_behind(to_prior, "dom", -1)
+    prior_rhs = from_behind(rhs_rim, "dom", 1)
+    packs = (prior_pack, own_pack, next_pack)
+    whole = jnp.concatenate(
+        [prior_pack[rows : rows + 1], own_pack[:, rows], next_pack[rows : rows + 1]], axis=0
+    ).astype(jnp.int32)
+    odd = whole & 1
+    own = 2 * (whole - odd) + 1 + odd
+    other = own + 4 * odd - 2
+    other = jnp.where(other < 0, other + 4 * doms, other)
+    other = jnp.where(other >= 4 * doms, other - 4 * doms, other)
+    ints = jnp.stack([whole, own, other])
 
     ops_a, diag_a = slot_op(dual_ops, row_perm[0:1], 0)
-    row_forms, col_forms, part = start(sizes, left, right, prior_modes, next_modes, rhs)
+    row_forms, col_forms, part = start(blocks, ints, left, right, prior_pack, next_pack, rhs)
     second_perm, _ = lax.optimization_barrier((row_perm[1:2], part))
     everything = trade(part, "dom").reshape(4 * doms, rows, -1)
     ops_b, diag_b = slot_op(dual_ops, second_perm, 1)
@@ -599,14 +623,13 @@
     new = [1.0 / centre] + [2.0 * ratios[t] / radius for t in range(1, STEPS)]
     norms = []
     residual, direction, wa, wb, wc, sums, coarse_fields, links = first(
-        new[0], sizes, rhs, prior_rhs, row_forms, col_forms, ops
+        new[0], blocks, ints, rhs, prior_rhs, row_forms, col_forms, ops
     )
     solution = None
     for turn in range(STEPS):
-        amounts, wa, wc, to_prior, to_next = coarse(
-            new[turn], ints, everything, ext_blocks, wa, wc, coarse_fields
+        amounts, wa, wc, to_prior, to_next, part = coarse(
+            new[turn], ints, everything, packs, wa, wc, sums, coarse_fields, links
         )
-        part = share(new[turn], amounts, sums, links)
         from_prior = from_behind(to_next, "dom", 1)
         from_next = from_behind(to_prior, "dom", -1)
         everything = trade(part, "dom").reshape(4 * doms, rows, -1)
@@ -616,19 +639,20 @@
             fields += (solution,)
         if last:
             residual, solution, norm = step(
-                begin, last, (new[turn], 0.0, 0.0), sizes, amounts, col_forms, coarse_fields, fields
+                blocks, begin, last, (new[turn], 0.0, 0.0), ints, amounts, col_forms, coarse_fields, fields
             )
         else:
             factors = (new[turn], old[turn + 1], new[turn + 1])
             residual, solution, norm, direction, wa, wb, wc, sums = step(
-                begin, last, factors, sizes, amounts, col_forms, coarse_fields, fields, row_forms, ops
+                blocks, begin, last, factors, ints, amounts, col_forms, coarse_fields, fields, row_forms, ops
             )
         if not begin:
             norms.append(norm)
-    residual, norm = final(ints, sizes, everything, ext_blocks, col_forms, residual)
-    norms.append(norm)
-    sums = to_everyone(jnp.concatenate(norms, axis=0), ("dom", "case"))
     cases = lax.axis_size("case")
+    residual, sums = final(
+        blocks, ints, everything, packs, col_forms, residual, norms, doms * cases
+    )
+    sums = trade(sums, ("dom", "case"))
     totals = jnp.sum(sums.reshape(doms, cases, STEPS, -1), axis=0)
     whole_history = jnp.sqrt(totals + epsilon)
     history = lax.dynamic_index_in_dim(whole_history, lax.axis_index("case"), 0, keepdims=False)

time: 216 us -> 197 us (0.912)
  Pallas kernels: 113 us -> 100 us
  starting transfers between devices: 62.9 us -> 56.5 us
  local copies, waits for them, and re-layouts: 13.8 us -> 19.5 us
  waiting for transfers between devices: 19.1 us -> 16.2 us
  other arithmetic: 3.34 us -> 0.74 us
    unnamed x40 -> x54, local copies, waits for them, and re-layouts: 8.25 us -> 18.9 us
    pallas_call x7 -> x3, Pallas kernels: 15.5 us -> 5.98 us  [the longest x1 2.1 us: prepare(): pl.pallas_call(prepare_kernel, out_shape=(side, side, jax.ShapeDtypeStruc...]
    ppermute x13 -> x11, starting transfers between devices: 30.6 us -> 26.3 us  [from_behind(): return lax.ppermute(block, axis, route)]
    all_to_all x6, waiting for transfers between devices: 19 us -> 16.2 us  [trade(): return lax.all_to_all(copies, axis, 0, 0, tiled=True)]
    pallas_call x4, Pallas kernels: 13.2 us -> 10.4 us  [coarse(): pl.pallas_call(body, out_shape=(jax.ShapeDtypeStruct((4 * modes, lanes),...]
  transfers between devices with their start and end apart: 19 -> 17, of which waited for: 6 -> 2; matrix products, arithmetic and copies ran while one was open for 2% -> 0% of each run, Pallas kernels for 46% -> 44%
where the time goes in v3:
time: 197 us; the launch traced here: 194 us
  Pallas kernels  100 us (51%)
  starting transfers between devices  56.5 us (29%)
  local copies, waits for them, and re-layouts  19.5 us (10%)
  waiting for transfers between devices  16.2 us (8%)
    pallas_call x2, Pallas kernels, slot_op(): pl.pallas_call(slot_op_kernel, grid=(2 * blocks,), out_shape=(jax.ShapeDt...  42.3 us
    pallas_call x4, Pallas kernels, step(): pl.pallas_call(body, out_shape=tuple(out), in_specs=specs, out_specs=[VME...  32.8 us
    all_to_all x6, starting transfers between devices, trade(): return lax.all_to_all(copies, axis, 0, 0, tiled=True)  30.2 us
    ppermute x11, starting transfers between devices, from_behind(): return lax.ppermute(block, axis, route)  26.3 us
    unnamed x54, local copies, waits for them, and re-layouts  18.9 us
    all_to_all x6, waiting for transfers between devices, trade(): return lax.all_to_all(copies, axis, 0, 0, tiled=True)  16.2 us
    pallas_call x4, Pallas kernels, coarse(): pl.pallas_call(body, out_shape=(jax.ShapeDtypeStruct((4 * modes, lanes),...  10.4 us
    pallas_call x1, Pallas kernels, first(): pl.pallas_call(body, out_shape=(three, three, field, field, field, jax.Sh...  8.81 us
  transfers between devices with their start and end apart: 17, of which 2 were waited for; matrix products, arithmetic and copies ran while one was open for 0% of the time, Pallas kernels for 44%

profile of v3, /device:TPU:0, one launch (start us, length us, event | category | flops | bytes accessed | tf_op | source)
XLA Modules:
  0.0 194.2 jit_solution(12279486542237876612)
XLA Ops:
  0.6 1.1 copy-done
  1.8 0.9 copy-done.8
  2.7 0.9 copy-done.9
  3.6 0.7 copy-done.10
  4.3 0.7 copy-done.11
  5.6 2.1 %prepare.1 = (bf16[2,16,768]{2,1,0:T(8,128)(2,1)S(1)}, bf16[2,16,768]{2,1,0:T(8,128)(2,1)S(1)}, f32[2,24,128]{2,1,0:T(8,128)S(1)}, f32[120,128]{1,0:T(8,128)S(1)...) custom-call(s32[2,8]{1,0:T(2,128)S(1)} %copy-done.11, s32[2]{0:T(128)S(1)} %copy-done.12, ...), custom_call_target="tpu_custom_call" | custom-call | tf_op jit(solution)/shard_map/prepare/pallas_call | solution.py:86
  7.7 6.1 %collective-permute-start.1 = (f32[120,128]{1,0:T(8,128)S(1)}, f32[120,128]{1,0:T(8,128)S(1)}, u32[]{:S(2)}, u32[]{:S(2)}) collective-permute-start(f32[120,128]{1,0:T(8,128)S(1)} %get-tuple-element.80), channel_id=1, source_target_pairs={{4,0},{8,4},{12,8},{16,12},{20,16},{24,20},{28,24},{32,28},{36,32}... | collective-permute-start | bytes 184328 | tf_op jit(solution)/shard_map/ppermute | solution.py:27
  13.9 21.2 %slot_op.2 = (bf16[1536,1536]{1,0:T(8,128)(2,1)}, f32[1536,128]{1,0:T(8,128)S(1)}) custom-call(f32[2,1536,1536]{2,1,0:T(8,128)} %ops_ref.3, s32[1,1536]{1,0:T(1,128)S(1)} %get-tuple-element.153.perm_ref), custom_call_target="tpu_custom_call" | custom-call | flops 14495514624 | bytes 14155776 | tf_op jit(solution)/shard_map/slot_op/pallas_call | solution.py:153
  35.0 0.9 copy-done.4
  36.0 1.8 start.1
  37.8 7.3 %all-to-all-start = ((bf16[32,4,16,128]{3,2,1,0:T(8,128)(2,1)}), bf16[32,4,16,128]{3,2,1,0:T(8,128)(2,1)S(1)}, u32[]{:S(2)}, u32[]{:S(2)}) async-start(bf16[32,4,16,128]{3,2,1,0:T(8,128)(2,1)} %get-tuple-element.83), calls=%async_computation | async-start | bytes 1048576 | tf_op jit(solution)/shard_map/all_to_all | solution.py:586
  45.1 21.1 %slot_op.3 = (bf16[1536,1536]{1,0:T(8,128)(2,1)}, f32[1536,128]{1,0:T(8,128)S(1)}) custom-call(f32[2,1536,1536]{2,1,0:T(8,128)} %ops_ref.3, s32[1,1536]{1,0:T(1,128)S(1)} %get-tuple-element.88.perm_ref), custom_call_target="tpu_custom_call" | custom-call | flops 14495514624 | bytes 14155776 | tf_op jit(solution)/shard_map/slot_op/pallas_call | solution.py:153
  66.2 0.9 copy-done.5
  67.1 8.8 %first.1 = (f32[3,768,128]{2,1,0:T(8,128)}, f32[3,768,128]{2,1,0:T(8,128)}, f32[768,128]{1,0:T(8,128)S(1)}, f32[768,128]{1,0:T(8,128)S(1)}, f32[768,128]{1,0:T(8...) custom-call(s32[3,4,128]{2,1,0:T(4,128)S(1)} %pad_add_fusion.refs_0_, ...), custom_call_target="tpu_custom_call" | custom-call | flops 2000000000 | bytes 20000000 | tf_op jit(solution)/shard_map/first/pallas_call | solution.py:378
  75.9 0.7 copy-done.6
  76.7 0.7 copy-done.13
  77.4 1.0 copy-done.7
  78.4 2.7 %coarse.4 = (f32[64,128]{1,0:T(8,128)S(1)}, f32[768,128]{1,0:T(8,128)S(1)}, f32[768,128]{1,0:T(8,128)S(1)}, bf16[768,128]{1,0:T(8,128)(2,1)S(1)}, bf16[768,128]{...) custom-call(s32[3,4,128]{2,1,0:T(4,128)S(1)} %pad_add_fusion.refs_0_, bf16[128,16,128]{2,1,0:T(8,128)(2,1)S(1)} %bitcast.18, ...), custom_call_target="tpu_custom_call" | custom-call | flops 100000000 | bytes 4000000 | tf_op jit(solution)/shard_map/coarse/pallas_call | solution.py:431
  81.2 5.0 %collective-permute-start.4 = (bf16[768,128]{1,0:T(8,128)(2,1)S(1)}, bf16[768,128]{1,0:T(8,128)(2,1)S(1)}, u32[]{:S(2)}, u32[]{:S(2)}) collective-permute-start(bf16[768,128]{1,0:T(8,128)(2,1)S(1)} %get-tuple-element.103), channel_id=1, source_target_pairs={{4,0},{8,4},{12,8},{16,12},{20,16},{24,20},{28,24},{32,28},{36,32}... | collective-permute-start | bytes 589832 | tf_op jit(solution)/shard_map/ppermute | solution.py:27
  86.1 4.1 %all-to-all-start.1 = ((bf16[32,4,16,128]{3,2,1,0:T(8,128)(2,1)}), bf16[32,4,16,128]{3,2,1,0:T(8,128)(2,1)S(1)}, u32[]{:S(2)}, u32[]{:S(2)}) async-start(bf16[32,4,16,128]{3,2,1,0:T(8,128)(2,1)} %get-tuple-element.97), calls=%async_computation.1 | async-start | bytes 1048576 | tf_op jit(solution)/shard_map/all_to_all | solution.py:586
  90.3 1.0 copy-done.18
  91.3 9.4 %step.3 = (f32[3,768,128]{2,1,0:T(8,128)}, f32[2,768,128]{2,1,0:T(8,128)}, f32[1,128]{1,0:T(1,128)}, f32[3,768,128]{2,1,0:T(8,128)}, f32[768,128]{1,0:T(8,128)S(...) custom-call(s32[3,4,128]{2,1,0:T(4,128)S(1)} %pad_add_fusion.refs_0_, ...), custom_call_target="tpu_custom_call" | custom-call | flops 99999997952 | bytes 1000000000 | tf_op jit(solution)/shard_map/step/pallas_call | solution.py:530
  100.7 0.7 copy-done.25
  101.4 2.5 %coarse.5 = (f32[64,128]{1,0:T(8,128)S(1)}, f32[768,128]{1,0:T(8,128)S(1)}, f32[768,128]{1,0:T(8,128)S(1)}, bf16[768,128]{1,0:T(8,128)(2,1)S(1)}, bf16[768,128]{...) custom-call(s32[3,4,128]{2,1,0:T(4,128)S(1)} %pad_add_fusion.refs_0_, bf16[128,16,128]{2,1,0:T(8,128)(2,1)S(1)} %bitcast.16, ...), custom_call_target="tpu_custom_call" | custom-call | flops 100000000 | bytes 4000000 | tf_op jit(solution)/shard_map/coarse/pallas_call | solution.py:431
  104.5 4.6 %collective-permute-start.6 = (bf16[768,128]{1,0:T(8,128)(2,1)S(1)}, bf16[768,128]{1,0:T(8,128)(2,1)S(1)}, u32[]{:S(2)}, u32[]{:S(2)}) collective-permute-start(bf16[768,128]{1,0:T(8,128)(2,1)S(1)} %get-tuple-element.115), channel_id=1, source_target_pairs={{4,0},{8,4},{12,8},{16,12},{20,16},{24,20},{28,24},{32,28},{36,32}... | collective-permute-start | bytes 589832 | tf_op jit(solution)/shard_map/ppermute | solution.py:27
  109.0 3.9 %all-to-all-start.2 = ((bf16[32,4,16,128]{3,2,1,0:T(8,128)(2,1)}), bf16[32,4,16,128]{3,2,1,0:T(8,128)(2,1)S(1)}, u32[]{:S(2)}, u32[]{:S(2)}) async-start(bf16[32,4,16,128]{3,2,1,0:T(8,128)(2,1)} %get-tuple-element.109), calls=%async_computation.2 | async-start | bytes 1048576 | tf_op jit(solution)/shard_map/all_to_all | solution.py:586
  112.9 1.0 copy-done.26
  113.9 9.9 %step.4 = (f32[3,768,128]{2,1,0:T(8,128)}, f32[2,768,128]{2,1,0:T(8,128)}, f32[1,128]{1,0:T(1,128)S(1)}, f32[3,768,128]{2,1,0:T(8,128)}, f32[768,128]{1,0:T(8,12...) custom-call(s32[3,4,128]{2,1,0:T(4,128)S(1)} %pad_add_fusion.refs_0_, ...), custom_call_target="tpu_custom_call" | custom-call | flops 99999997952 | bytes 1000000000 | tf_op jit(solution)/shard_map/step/pallas_call | solution.py:530
  123.9 0.7 copy-done.21
  124.6 2.6 %coarse.6 = (f32[64,128]{1,0:T(8,128)S(1)}, f32[768,128]{1,0:T(8,128)S(1)}, f32[768,128]{1,0:T(8,128)S(1)}, bf16[768,128]{1,0:T(8,128)(2,1)S(1)}, bf16[768,128]{...) custom-call(s32[3,4,128]{2,1,0:T(4,128)S(1)} %pad_add_fusion.refs_0_, bf16[128,16,128]{2,1,0:T(8,128)(2,1)S(1)} %bitcast.17, ...), custom_call_target="tpu_custom_call" | custom-call | flops 100000000 | bytes 4000000 | tf_op jit(solution)/shard_map/coarse/pallas_call | solution.py:431
  127.2 0.7 copy-done.15
  128.2 4.8 %collective-permute-start.8 = (bf16[768,128]{1,0:T(8,128)(2,1)S(1)}, bf16[768,128]{1,0:T(8,128)(2,1)S(1)}, u32[]{:S(2)}, u32[]{:S(2)}) collective-permute-start(bf16[768,128]{1,0:T(8,128)(2,1)S(1)} %get-tuple-element.128), channel_id=1, source_target_pairs={{4,0},{8,4},{12,8},{16,12},{20,16},{24,20},{28,24},{32,28},{36,32}... | collective-permute-start | bytes 589832 | tf_op jit(solution)/shard_map/ppermute | solution.py:27
  133.0 4.1 %all-to-all-start.3 = ((bf16[32,4,16,128]{3,2,1,0:T(8,128)(2,1)}), bf16[32,4,16,128]{3,2,1,0:T(8,128)(2,1)S(1)}, u32[]{:S(2)}, u32[]{:S(2)}) async-start(bf16[32,4,16,128]{3,2,1,0:T(8,128)(2,1)} %get-tuple-element.122), calls=%async_computation.3 | async-start | bytes 1048576 | tf_op jit(solution)/shard_map/all_to_all | solution.py:586
  137.1 1.0 copy-done.16
  138.1 1.0 copy-done.22
  139.1 9.9 %step.5 = (f32[3,768,128]{2,1,0:T(8,128)}, f32[2,768,128]{2,1,0:T(8,128)}, f32[1,128]{1,0:T(1,128)S(1)}, f32[3,768,128]{2,1,0:T(8,128)}, f32[768,128]{1,0:T(8,12...) custom-call(s32[3,4,128]{2,1,0:T(4,128)S(1)} %pad_add_fusion.refs_0_, ...), custom_call_target="tpu_custom_call" | custom-call | flops 99999997952 | bytes 1000000000 | tf_op jit(solution)/shard_map/step/pallas_call | solution.py:530
  149.1 0.7 copy-done.23
  149.8 2.6 %coarse.7 = (f32[64,128]{1,0:T(8,128)S(1)}, f32[768,128]{1,0:T(8,128)S(1)}, f32[768,128]{1,0:T(8,128)S(1)}, bf16[768,128]{1,0:T(8,128)(2,1)S(1)}, bf16[768,128]{...) custom-call(s32[3,4,128]{2,1,0:T(4,128)S(1)} %pad_add_fusion.refs_0_, bf16[128,16,128]{2,1,0:T(8,128)(2,1)S(1)} %bitcast.15, ...), custom_call_target="tpu_custom_call" | custom-call | flops 100000000 | bytes 4000000 | tf_op jit(solution)/shard_map/coarse/pallas_call | solution.py:431
  152.4 0.8 copy-done.19
  153.5 4.8 %collective-permute-start.10 = (bf16[768,128]{1,0:T(8,128)(2,1)S(1)}, bf16[768,128]{1,0:T(8,128)(2,1)S(1)}, u32[]{:S(2)}, u32[]{:S(2)}) collective-permute-start(bf16[768,128]{1,0:T(8,128)(2,1)S(1)} %get-tuple-element.140), channel_id=1, source_target_pairs={{4,0},{8,4},{12,8},{16,12},{20,16},{24,20},{28,24},{32,28},{36,32}... | collective-permute-start | bytes 589832 | tf_op jit(solution)/shard_map/ppermute | solution.py:27
  158.3 4.1 %all-to-all-start.4 = ((bf16[32,4,16,128]{3,2,1,0:T(8,128)(2,1)}), bf16[32,4,16,128]{3,2,1,0:T(8,128)(2,1)S(1)}, u32[]{:S(2)}, u32[]{:S(2)}) async-start(bf16[32,4,16,128]{3,2,1,0:T(8,128)(2,1)} %get-tuple-element.145), calls=%async_computation.4 | async-start | bytes 1048576 | tf_op jit(solution)/shard_map/all_to_all | solution.py:586
  162.4 1.0 copy-done.20
  163.4 1.0 copy-done.24
  164.4 3.5 %last_step.1 = (f32[2,768,128]{2,1,0:T(8,128)S(1)}, f32[2,768,128]{2,1,0:T(8,128)}, f32[1,128]{1,0:T(1,128)S(1)}) custom-call(s32[3,4,128]{2,1,0:T(4,128)S(1)} %pad_add_fusion.refs_0_, f32[64,128]{1,0:T(8,128)S(1)} %get-tuple-element.135.refs_1_, bf16[3,768,64]{2,1,0:T(8,128)(2,1)S(1)} %copy-done.3, bf16[3,768,256]{2,1,0:T(8,128)(2,1)} %get-tuple-element.95.refs_8_.refs_3_, ...), custom_call_target="tpu_custom_call" | custom-call | flops 99999997952 | bytes 1000000000 | tf_op jit(solution)/shard_map/last_step/pallas_call | solution.py:530
  167.9 5.6 %all-to-all-done.4 = bf16[32,4,16,128]{3,2,1,0:T(8,128)(2,1)S(1)} async-done(((bf16[32,4,16,128]{3,2,1,0:T(8,128)(2,1)}), bf16[32,4,16,128]{3,2,1,0:T(8,128)(2,1)S(1)}, u32[]{:S(2)}, u32[]{:S(2)}) %all-to-all-start.4) | async-done | bytes 524320 | tf_op jit(solution)/shard_map/all_to_all | solution.py:586
  173.5 2.1 %final.1 = (f32[2,768,128]{2,1,0:T(8,128)}, f32[128,4,128]{2,1,0:T(4,128)}) custom-call(s32[3,4,128]{2,1,0:T(4,128)S(1)} %pad_add_fusion.refs_0_, bf16[128,16,128]{2,1,0:T(8,128)(2,1)S(1)} %bitcast.14, f32[120,128]{1,0:T(8,128)S(1)} %collective-permute-done.refs_3_.refs_2_, f32[2,24,128]{2,1,0:T(8,128)S(1)} %get-tuple-element.79.refs_3_, ...), custom_call_target="tpu_custom_call" | custom-call | tf_op jit(solution)/shard_map/final/pallas_call | solution.py:571
  175.6 6.8 %all-to-all-start.5 = ((f32[128,4,128]{2,1,0:T(4,128)}), f32[128,4,128]{2,1,0:T(4,128)S(1)}, u32[]{:S(2)}, u32[]{:S(2)}) async-start(f32[128,4,128]{2,1,0:T(4,128)} %get-tuple-element.151), calls=%async_computation.5 | async-start | bytes 524288 | tf_op jit(solution)/shard_map/all_to_all | solution.py:586
  182.4 10.5 %all-to-all-done.5 = f32[128,4,128]{2,1,0:T(4,128)S(1)} async-done(((f32[128,4,128]{2,1,0:T(4,128)}), f32[128,4,128]{2,1,0:T(4,128)S(1)}, u32[]{:S(2)}, u32[]{:S(2)}) %all-to-all-start.5) | async-done | bytes 262176 | tf_op jit(solution)/shard_map/all_to_all | solution.py:586
  (65 shorter events, 3.2 us)
Async XLA Ops:
  0.6 1.1 copy-start
  1.8 0.9 copy-start.8
  2.7 0.9 copy-start.9
  3.6 0.7 copy-start.10
  4.3 0.7 copy-start.11
  5.0 0.7 copy-start.12
  7.7 28.2 %collective-permute-start.1 = (f32[120,128]{1,0:T(8,128)S(1)}, f32[120,128]{1,0:T(8,128)S(1)}, u32[]{:S(2)}, u32[]{:S(2)}) collective-permute-start(f32[120,128]{1,0:T(8,128)S(1)} %get-tuple-element.80), channel_id=1, source_target_pairs={{4,0},{8,4},{12,8},{16,12},{20,16},{24,20},{28,24},{32,28},{36,32}... | collective-permute-start | bytes 184328 | tf_op jit(solution)/shard_map/ppermute | solution.py:27
  13.8 22.1 %collective-permute-start = (f32[120,128]{1,0:T(8,128)S(1)}, f32[120,128]{1,0:T(8,128)S(1)}, u32[]{:S(2)}, u32[]{:S(2)}) collective-permute-start(f32[120,128]{1,0:T(8,128)S(1)} %get-tuple-element.78), channel_id=1, source_target_pairs={{124,0},{0,4},{4,8},{8,12},{12,16},{16,20},{20,24},{24,28},{28,32}... | collective-permute-start | bytes 184328 | tf_op jit(solution)/shard_map/ppermute | solution.py:27
  13.8 53.3 %collective-permute-start.2 = (f32[768,128]{1,0:T(8,128)S(1)}, f32[768,128]{1,0:T(8,128)S(1)}, u32[]{:S(2)}, u32[]{:S(2)}) collective-permute-start(f32[768,128]{1,0:T(8,128)S(1)} %get-tuple-element.84), channel_id=1, source_target_pairs={{124,0},{0,4},{4,8},{8,12},{12,16},{16,20},{20,24},{24,28},{28,32}... | collective-permute-start | bytes 1179656 | tf_op jit(solution)/shard_map/ppermute | solution.py:27
  13.8 22.1 %copy-start.1 = (f32[2,768,128]{2,1,0:T(8,128)S(1)}, f32[2,768,128]{2,1,0:T(8,128)}, u32[]{:S(2)}) copy-start(f32[2,768,128]{2,1,0:T(8,128)} %refs_1_.1) | copy-start | bytes 2359300
  35.0 0.9 copy-start.4
  37.8 29.3 %copy-start.2 = (bf16[3,768,64]{2,1,0:T(8,128)(2,1)}, bf16[3,768,64]{2,1,0:T(8,128)(2,1)S(1)}, u32[]{:S(2)}) copy-start(bf16[3,768,64]{2,1,0:T(8,128)(2,1)S(1)} %get-tuple-element.86.refs_4_.refs_2_.refs_5_) | copy-start | bytes 884740
  37.8 39.6 %all-to-all-start = ((bf16[32,4,16,128]{3,2,1,0:T(8,128)(2,1)}), bf16[32,4,16,128]{3,2,1,0:T(8,128)(2,1)S(1)}, u32[]{:S(2)}, u32[]{:S(2)}) async-start(bf16[32,4,16,128]{3,2,1,0:T(8,128)(2,1)} %get-tuple-element.83), calls=%async_computation | async-start | bytes 1048576 | tf_op jit(solution)/shard_map/all_to_all | solution.py:586
  66.2 0.9 copy-start.5
  75.9 0.8 copy-start.6
  76.7 0.7 copy-start.13
  77.4 1.0 copy-start.7
  78.4 11.9 %copy-start.14 = (f32[768,128]{1,0:T(8,128)S(1)}, f32[768,128]{1,0:T(8,128)}, u32[]{:S(2)}) copy-start(f32[768,128]{1,0:T(8,128)} %copy-done.13) | copy-start | bytes 1179652
  81.1 9.2 %copy-start.17 = (f32[768,128]{1,0:T(8,128)}, f32[768,128]{1,0:T(8,128)S(1)}, u32[]{:S(2)}) copy-start(f32[768,128]{1,0:T(8,128)S(1)} %get-tuple-element.101.refs_6_) | copy-start | bytes 1179652
  81.1 9.2 %collective-permute-start.3 = (bf16[768,128]{1,0:T(8,128)(2,1)}, bf16[768,128]{1,0:T(8,128)(2,1)S(1)}, u32[]{:S(2)}, u32[]{:S(2)}) collective-permute-start(bf16[768,128]{1,0:T(8,128)(2,1)} %get-tuple-element.102), channel_id=1, source_target_pairs={{124,0},{0,4},{4,8},{8,12},{12,16},{16,20},{20,24},{24,28},{28,32}... | collective-permute-start | bytes 589832 | tf_op jit(solution)/shard_map/ppermute | solution.py:27
  81.2 9.1 %collective-permute-start.4 = (bf16[768,128]{1,0:T(8,128)(2,1)S(1)}, bf16[768,128]{1,0:T(8,128)(2,1)S(1)}, u32[]{:S(2)}, u32[]{:S(2)}) collective-permute-start(bf16[768,128]{1,0:T(8,128)(2,1)S(1)} %get-tuple-element.103), channel_id=1, source_target_pairs={{4,0},{8,4},{12,8},{16,12},{20,16},{24,20},{28,24},{32,28},{36,32}... | collective-permute-start | bytes 589832 | tf_op jit(solution)/shard_map/ppermute | solution.py:27
  86.1 15.3 %all-to-all-start.1 = ((bf16[32,4,16,128]{3,2,1,0:T(8,128)(2,1)}), bf16[32,4,16,128]{3,2,1,0:T(8,128)(2,1)S(1)}, u32[]{:S(2)}, u32[]{:S(2)}) async-start(bf16[32,4,16,128]{3,2,1,0:T(8,128)(2,1)} %get-tuple-element.97), calls=%async_computation.1 | async-start | bytes 1048576 | tf_op jit(solution)/shard_map/all_to_all | solution.py:586
  90.3 1.0 copy-start.18
  100.7 0.7 copy-start.25
  103.9 9.0 %collective-permute-start.5 = (bf16[768,128]{1,0:T(8,128)(2,1)S(1)}, bf16[768,128]{1,0:T(8,128)(2,1)S(1)}, u32[]{:S(2)}, u32[]{:S(2)}) collective-permute-start(bf16[768,128]{1,0:T(8,128)(2,1)S(1)} %get-tuple-element.114), channel_id=1, source_target_pairs={{124,0},{0,4},{4,8},{8,12},{12,16},{16,20},{20,24},{24,28},{28,32}... | collective-permute-start | bytes 589832 | tf_op jit(solution)/shard_map/ppermute | solution.py:27
  104.5 8.5 %collective-permute-start.6 = (bf16[768,128]{1,0:T(8,128)(2,1)S(1)}, bf16[768,128]{1,0:T(8,128)(2,1)S(1)}, u32[]{:S(2)}, u32[]{:S(2)}) collective-permute-start(bf16[768,128]{1,0:T(8,128)(2,1)S(1)} %get-tuple-element.115), channel_id=1, source_target_pairs={{4,0},{8,4},{12,8},{16,12},{20,16},{24,20},{28,24},{32,28},{36,32}... | collective-permute-start | bytes 589832 | tf_op jit(solution)/shard_map/ppermute | solution.py:27
  109.0 15.6 %all-to-all-start.2 = ((bf16[32,4,16,128]{3,2,1,0:T(8,128)(2,1)}), bf16[32,4,16,128]{3,2,1,0:T(8,128)(2,1)S(1)}, u32[]{:S(2)}, u32[]{:S(2)}) async-start(bf16[32,4,16,128]{3,2,1,0:T(8,128)(2,1)} %get-tuple-element.109), calls=%async_computation.2 | async-start | bytes 1048576 | tf_op jit(solution)/shard_map/all_to_all | solution.py:586
  112.9 1.0 copy-start.26
  123.9 0.8 copy-start.21
  127.2 0.7 copy-start.15
  128.0 9.1 %collective-permute-start.7 = (bf16[768,128]{1,0:T(8,128)(2,1)}, bf16[768,128]{1,0:T(8,128)(2,1)S(1)}, u32[]{:S(2)}, u32[]{:S(2)}) collective-permute-start(bf16[768,128]{1,0:T(8,128)(2,1)} %get-tuple-element.127), channel_id=1, source_target_pairs={{124,0},{0,4},{4,8},{8,12},{12,16},{16,20},{20,24},{24,28},{28,32}... | collective-permute-start | bytes 589832 | tf_op jit(solution)/shard_map/ppermute | solution.py:27
  128.2 8.9 %collective-permute-start.8 = (bf16[768,128]{1,0:T(8,128)(2,1)S(1)}, bf16[768,128]{1,0:T(8,128)(2,1)S(1)}, u32[]{:S(2)}, u32[]{:S(2)}) collective-permute-start(bf16[768,128]{1,0:T(8,128)(2,1)S(1)} %get-tuple-element.128), channel_id=1, source_target_pairs={{4,0},{8,4},{12,8},{16,12},{20,16},{24,20},{28,24},{32,28},{36,32}... | collective-permute-start | bytes 589832 | tf_op jit(solution)/shard_map/ppermute | solution.py:27
  133.0 16.8 %all-to-all-start.3 = ((bf16[32,4,16,128]{3,2,1,0:T(8,128)(2,1)}), bf16[32,4,16,128]{3,2,1,0:T(8,128)(2,1)S(1)}, u32[]{:S(2)}, u32[]{:S(2)}) async-start(bf16[32,4,16,128]{3,2,1,0:T(8,128)(2,1)} %get-tuple-element.122), calls=%async_computation.3 | async-start | bytes 1048576 | tf_op jit(solution)/shard_map/all_to_all | solution.py:586
  137.1 1.0 copy-start.16
  138.1 1.0 copy-start.22
  149.0 0.7 copy-start.23
  149.8 12.6 %copy-start.3 = (bf16[3,768,64]{2,1,0:T(8,128)(2,1)S(1)}, bf16[3,768,64]{2,1,0:T(8,128)(2,1)}, u32[]{:S(2)}) copy-start(bf16[3,768,64]{2,1,0:T(8,128)(2,1)} %copy-done.2) | copy-start | bytes 884740
  152.4 0.8 copy-start.19
  153.2 9.1 %collective-permute-start.9 = (bf16[768,128]{1,0:T(8,128)(2,1)}, bf16[768,128]{1,0:T(8,128)(2,1)S(1)}, u32[]{:S(2)}, u32[]{:S(2)}) collective-permute-start(bf16[768,128]{1,0:T(8,128)(2,1)} %get-tuple-element.139), channel_id=1, source_target_pairs={{124,0},{0,4},{4,8},{8,12},{12,16},{16,20},{20,24},{24,28},{28,32}... | collective-permute-start | bytes 589832 | tf_op jit(solution)/shard_map/ppermute | solution.py:27
  153.5 8.9 %collective-permute-start.10 = (bf16[768,128]{1,0:T(8,128)(2,1)S(1)}, bf16[768,128]{1,0:T(8,128)(2,1)S(1)}, u32[]{:S(2)}, u32[]{:S(2)}) collective-permute-start(bf16[768,128]{1,0:T(8,128)(2,1)S(1)} %get-tuple-element.140), channel_id=1, source_target_pairs={{4,0},{8,4},{12,8},{16,12},{20,16},{24,20},{28,24},{32,28},{36,32}... | collective-permute-start | bytes 589832 | tf_op jit(solution)/shard_map/ppermute | solution.py:27
  158.3 15.3 %all-to-all-start.4 = ((bf16[32,4,16,128]{3,2,1,0:T(8,128)(2,1)}), bf16[32,4,16,128]{3,2,1,0:T(8,128)(2,1)S(1)}, u32[]{:S(2)}, u32[]{:S(2)}) async-start(bf16[32,4,16,128]{3,2,1,0:T(8,128)(2,1)} %get-tuple-element.145), calls=%async_computation.4 | async-start | bytes 1048576 | tf_op jit(solution)/shard_map/all_to_all | solution.py:586
  162.4 1.0 copy-start.20
  163.4 1.0 copy-start.24
  175.6 17.3 %all-to-all-start.5 = ((f32[128,4,128]{2,1,0:T(4,128)}), f32[128,4,128]{2,1,0:T(4,128)S(1)}, u32[]{:S(2)}, u32[]{:S(2)}) async-start(f32[128,4,128]{2,1,0:T(4,128)} %get-tuple-element.151), calls=%async_computation.5 | async-start | bytes 524288 | tf_op jit(solution)/shard_map/all_to_all | solution.py:586

commit v4 on v3

--- a/solution.py
+++ b/solution.py
@@ -18,6 +18,7 @@
 VMEM = pl.BlockSpec(memory_space=pltpu.VMEM)
 SMEM = pl.BlockSpec(memory_space=pltpu.SMEM)
 ANY = pl.BlockSpec(memory_space=pl.ANY)
+WHOLE = pltpu.CompilerParams(vmem_limit_bytes=60 * 1024 * 1024)
 PARAMS = pltpu.CompilerParams(vmem_limit_bytes=53000000)
 
 
@@ -94,9 +95,9 @@
             jax.ShapeDtypeStruct(rhs.shape[1:], f32),
         ),
         in_specs=[SMEM, SMEM, VMEM, VMEM, VMEM, ANY],
-        out_specs=[VMEM] * 5 + [ANY],
+        out_specs=[VMEM] * 6,
         scratch_shapes=[pltpu.SemaphoreType.DMA(())],
-        compiler_params=PARAMS,
+        compiler_params=WHOLE,
         name="prepare",
     )(coarse_cols, iface_size, modes, row_perm, coarse_rows, rhs)
 

time: 197 us -> 194 us (0.985)
  local copies, waits for them, and re-layouts: 19.5 us -> 16.1 us
    unnamed x54 -> x48, local copies, waits for them, and re-layouts: 18.9 us -> 14 us
  transfers between devices with their start and end apart: 17 -> 17, of which waited for: 2 -> 2; matrix products, arithmetic and copies ran while one was open for 0% -> 1% of each run, Pallas kernels for 44% -> 45%
where the time goes in v4:
time: 194 us; the launch traced here: 192 us
  Pallas kernels  101 us (52%)
  starting transfers between devices  56.6 us (29%)
  waiting for transfers between devices  16.2 us (8%)
  local copies, waits for them, and re-layouts  16.1 us (8%)
    pallas_call x2, Pallas kernels, slot_op(): pl.pallas_call(slot_op_kernel, grid=(2 * blocks,), out_shape=(jax.ShapeDt...  42.3 us
    pallas_call x4, Pallas kernels, step(): pl.pallas_call(body, out_shape=tuple(out), in_specs=specs, out_specs=[VME...  32.7 us
    all_to_all x6, starting transfers between devices, trade(): return lax.all_to_all(copies, axis, 0, 0, tiled=True)  30.2 us
    ppermute x11, starting transfers between devices, from_behind(): return lax.ppermute(block, axis, route)  26.3 us
    all_to_all x6, waiting for transfers between devices, trade(): return lax.all_to_all(copies, axis, 0, 0, tiled=True)  16.2 us
    unnamed x48, local copies, waits for them, and re-layouts  14 us
    pallas_call x4, Pallas kernels, coarse(): pl.pallas_call(body, out_shape=(jax.ShapeDtypeStruct((4 * modes, lanes),...  10.5 us
    pallas_call x1, Pallas kernels, first(): pl.pallas_call(body, out_shape=(three, three, field, field, field, jax.Sh...  8.82 us
  transfers between devices with their start and end apart: 17, of which 2 were waited for; matrix products, arithmetic and copies ran while one was open for 1% of the time, Pallas kernels for 45%

profile of v4, /device:TPU:0, one launch (start us, length us, event | category | flops | bytes accessed | tf_op | source)
XLA Modules:
  0.0 192.0 jit_solution(3869617842274541570)
XLA Ops:
  0.6 3.2 %prepare.1 = (bf16[2,16,768]{2,1,0:T(8,128)(2,1)}, bf16[2,16,768]{2,1,0:T(8,128)(2,1)}, f32[2,24,128]{2,1,0:T(8,128)}, f32[120,128]{1,0:T(8,128)}, f32[120,128]{1,0:T(8,128)}, /*index=5*/f32[768,128]{1,0:T(8,128)}) custom-call(s32[2,8]{1,0:T(2,128)} %cols_ref.1, s32[2]{0:T(128)} %size_ref.1, bf16[2,16,1536]{2,1,0:T(8,128)(2,1)} %modes_ref.1, ...), custom_call_target="tpu_custom_call" | custom-call | tf_op jit(solution)/shard_map/prepare/pallas_call | solution.py:87
  3.8 6.1 %collective-permute-start.1 = (f32[120,128]{1,0:T(8,128)}, f32[120,128]{1,0:T(8,128)S(1)}, u32[]{:S(2)}, u32[]{:S(2)}) collective-permute-start(f32[120,128]{1,0:T(8,128)} %get-tuple-element.80), channel_id=1, source_target_pairs={{4,0},{8,4},{12,8},{16,12},{20,16},{24,20},{28,24},{32,28},{36,32}... | collective-permute-start | bytes 184328 | tf_op jit(solution)/shard_map/ppermute | solution.py:28
  9.9 0.8 fusion.4
  10.7 0.8 copy.11
  11.5 21.2 %slot_op.2 = (bf16[1536,1536]{1,0:T(8,128)(2,1)}, f32[1536,128]{1,0:T(8,128)S(1)}) custom-call(f32[2,1536,1536]{2,1,0:T(8,128)} %ops_ref.3, s32[1,1536]{1,0:T(1,128)S(1)} %get-tuple-element.153.perm_ref), custom_call_target="tpu_custom_call" | custom-call | flops 14495514624 | bytes 14155776 | tf_op jit(solution)/shard_map/slot_op/pallas_call | solution.py:154
  32.6 0.9 copy-done.4
  33.6 1.8 start.1
  35.5 7.3 %all-to-all-start = ((bf16[32,4,16,128]{3,2,1,0:T(8,128)(2,1)}), bf16[32,4,16,128]{3,2,1,0:T(8,128)(2,1)S(1)}, u32[]{:S(2)}, u32[]{:S(2)}) async-start(bf16[32,4,16,128]{3,2,1,0:T(8,128)(2,1)} %get-tuple-element.83), calls=%async_computation | async-start | bytes 1048576 | tf_op jit(solution)/shard_map/all_to_all | solution.py:587
  42.8 21.1 %slot_op.3 = (bf16[1536,1536]{1,0:T(8,128)(2,1)}, f32[1536,128]{1,0:T(8,128)S(1)}) custom-call(f32[2,1536,1536]{2,1,0:T(8,128)} %ops_ref.3, s32[1,1536]{1,0:T(1,128)S(1)} %get-tuple-element.88.perm_ref), custom_call_target="tpu_custom_call" | custom-call | flops 14495514624 | bytes 14155776 | tf_op jit(solution)/shard_map/slot_op/pallas_call | solution.py:154
  63.9 0.9 copy-done.5
  64.8 8.8 %first.1 = (f32[3,768,128]{2,1,0:T(8,128)}, f32[3,768,128]{2,1,0:T(8,128)}, f32[768,128]{1,0:T(8,128)S(1)}, f32[768,128]{1,0:T(8,128)S(1)}, f32[768,128]{1,0:T(8...) custom-call(s32[3,4,128]{2,1,0:T(4,128)S(1)} %pad_add_fusion.refs_0_, ...), custom_call_target="tpu_custom_call" | custom-call | flops 2000000000 | bytes 20000000 | tf_op jit(solution)/shard_map/first/pallas_call | solution.py:379
  73.6 0.7 copy-done.6
  74.3 0.8 copy-done.10
  75.1 1.0 copy-done.7
  76.1 2.7 %coarse.4 = (f32[64,128]{1,0:T(8,128)S(1)}, f32[768,128]{1,0:T(8,128)S(1)}, f32[768,128]{1,0:T(8,128)S(1)}, bf16[768,128]{1,0:T(8,128)(2,1)S(1)}, bf16[768,128]{...) custom-call(s32[3,4,128]{2,1,0:T(4,128)S(1)} %pad_add_fusion.refs_0_, bf16[128,16,128]{2,1,0:T(8,128)(2,1)S(1)} %bitcast.18, ...), custom_call_target="tpu_custom_call" | custom-call | flops 100000000 | bytes 4000000 | tf_op jit(solution)/shard_map/coarse/pallas_call | solution.py:432
  78.9 5.0 %collective-permute-start.4 = (bf16[768,128]{1,0:T(8,128)(2,1)S(1)}, bf16[768,128]{1,0:T(8,128)(2,1)S(1)}, u32[]{:S(2)}, u32[]{:S(2)}) collective-permute-start(bf16[768,128]{1,0:T(8,128)(2,1)S(1)} %get-tuple-element.103), channel_id=1, source_target_pairs={{4,0},{8,4},{12,8},{16,12},{20,16},{24,20},{28,24},{32,28},{36,32}... | collective-permute-start | bytes 589832 | tf_op jit(solution)/shard_map/ppermute | solution.py:28
  83.9 4.1 %all-to-all-start.1 = ((bf16[32,4,16,128]{3,2,1,0:T(8,128)(2,1)}), bf16[32,4,16,128]{3,2,1,0:T(8,128)(2,1)S(1)}, u32[]{:S(2)}, u32[]{:S(2)}) async-start(bf16[32,4,16,128]{3,2,1,0:T(8,128)(2,1)} %get-tuple-element.97), calls=%async_computation.1 | async-start | bytes 1048576 | tf_op jit(solution)/shard_map/all_to_all | solution.py:587
  88.0 1.0 copy-done.15
  89.0 9.3 %step.3 = (f32[3,768,128]{2,1,0:T(8,128)}, f32[2,768,128]{2,1,0:T(8,128)}, f32[1,128]{1,0:T(1,128)}, f32[3,768,128]{2,1,0:T(8,128)}, f32[768,128]{1,0:T(8,128)S(...) custom-call(s32[3,4,128]{2,1,0:T(4,128)S(1)} %pad_add_fusion.refs_0_, ...), custom_call_target="tpu_custom_call" | custom-call | flops 99999997952 | bytes 1000000000 | tf_op jit(solution)/shard_map/step/pallas_call | solution.py:531
  98.4 0.8 copy-done.22
  99.1 2.5 %coarse.5 = (f32[64,128]{1,0:T(8,128)S(1)}, f32[768,128]{1,0:T(8,128)S(1)}, f32[768,128]{1,0:T(8,128)S(1)}, bf16[768,128]{1,0:T(8,128)(2,1)S(1)}, bf16[768,128]{...) custom-call(s32[3,4,128]{2,1,0:T(4,128)S(1)} %pad_add_fusion.refs_0_, bf16[128,16,128]{2,1,0:T(8,128)(2,1)S(1)} %bitcast.16, ...), custom_call_target="tpu_custom_call" | custom-call | flops 100000000 | bytes 4000000 | tf_op jit(solution)/shard_map/coarse/pallas_call | solution.py:432
  101.7 0.5 collective-permute-start.5
  102.2 4.6 %collective-permute-start.6 = (bf16[768,128]{1,0:T(8,128)(2,1)S(1)}, bf16[768,128]{1,0:T(8,128)(2,1)S(1)}, u32[]{:S(2)}, u32[]{:S(2)}) collective-permute-start(bf16[768,128]{1,0:T(8,128)(2,1)S(1)} %get-tuple-element.115), channel_id=1, source_target_pairs={{4,0},{8,4},{12,8},{16,12},{20,16},{24,20},{28,24},{32,28},{36,32}... | collective-permute-start | bytes 589832 | tf_op jit(solution)/shard_map/ppermute | solution.py:28
  106.7 3.9 %all-to-all-start.2 = ((bf16[32,4,16,128]{3,2,1,0:T(8,128)(2,1)}), bf16[32,4,16,128]{3,2,1,0:T(8,128)(2,1)S(1)}, u32[]{:S(2)}, u32[]{:S(2)}) async-start(bf16[32,4,16,128]{3,2,1,0:T(8,128)(2,1)} %get-tuple-element.109), calls=%async_computation.2 | async-start | bytes 1048576 | tf_op jit(solution)/shard_map/all_to_all | solution.py:587
  110.7 1.0 copy-done.23
  111.7 10.0 %step.4 = (f32[3,768,128]{2,1,0:T(8,128)}, f32[2,768,128]{2,1,0:T(8,128)}, f32[1,128]{1,0:T(1,128)S(1)}, f32[3,768,128]{2,1,0:T(8,128)}, f32[768,128]{1,0:T(8,12...) custom-call(s32[3,4,128]{2,1,0:T(4,128)S(1)} %pad_add_fusion.refs_0_, ...), custom_call_target="tpu_custom_call" | custom-call | flops 99999997952 | bytes 1000000000 | tf_op jit(solution)/shard_map/step/pallas_call | solution.py:531
  121.6 0.7 copy-done.18
  122.4 2.6 %coarse.6 = (f32[64,128]{1,0:T(8,128)S(1)}, f32[768,128]{1,0:T(8,128)S(1)}, f32[768,128]{1,0:T(8,128)S(1)}, bf16[768,128]{1,0:T(8,128)(2,1)S(1)}, bf16[768,128]{...) custom-call(s32[3,4,128]{2,1,0:T(4,128)S(1)} %pad_add_fusion.refs_0_, bf16[128,16,128]{2,1,0:T(8,128)(2,1)S(1)} %bitcast.17, ...), custom_call_target="tpu_custom_call" | custom-call | flops 100000000 | bytes 4000000 | tf_op jit(solution)/shard_map/coarse/pallas_call | solution.py:432
  125.0 0.7 copy-done.12
  126.0 4.8 %collective-permute-start.8 = (bf16[768,128]{1,0:T(8,128)(2,1)S(1)}, bf16[768,128]{1,0:T(8,128)(2,1)S(1)}, u32[]{:S(2)}, u32[]{:S(2)}) collective-permute-start(bf16[768,128]{1,0:T(8,128)(2,1)S(1)} %get-tuple-element.128), channel_id=1, source_target_pairs={{4,0},{8,4},{12,8},{16,12},{20,16},{24,20},{28,24},{32,28},{36,32}... | collective-permute-start | bytes 589832 | tf_op jit(solution)/shard_map/ppermute | solution.py:28
  130.8 4.1 %all-to-all-start.3 = ((bf16[32,4,16,128]{3,2,1,0:T(8,128)(2,1)}), bf16[32,4,16,128]{3,2,1,0:T(8,128)(2,1)S(1)}, u32[]{:S(2)}, u32[]{:S(2)}) async-start(bf16[32,4,16,128]{3,2,1,0:T(8,128)(2,1)} %get-tuple-element.122), calls=%async_computation.3 | async-start | bytes 1048576 | tf_op jit(solution)/shard_map/all_to_all | solution.py:587
  134.9 1.0 copy-done.13
  135.9 1.0 copy-done.19
  136.9 9.9 %step.5 = (f32[3,768,128]{2,1,0:T(8,128)}, f32[2,768,128]{2,1,0:T(8,128)}, f32[1,128]{1,0:T(1,128)S(1)}, f32[3,768,128]{2,1,0:T(8,128)}, f32[768,128]{1,0:T(8,12...) custom-call(s32[3,4,128]{2,1,0:T(4,128)S(1)} %pad_add_fusion.refs_0_, ...), custom_call_target="tpu_custom_call" | custom-call | flops 99999997952 | bytes 1000000000 | tf_op jit(solution)/shard_map/step/pallas_call | solution.py:531
  146.8 0.7 copy-done.20
  147.6 2.7 %coarse.7 = (f32[64,128]{1,0:T(8,128)S(1)}, f32[768,128]{1,0:T(8,128)S(1)}, f32[768,128]{1,0:T(8,128)S(1)}, bf16[768,128]{1,0:T(8,128)(2,1)S(1)}, bf16[768,128]{...) custom-call(s32[3,4,128]{2,1,0:T(4,128)S(1)} %pad_add_fusion.refs_0_, bf16[128,16,128]{2,1,0:T(8,128)(2,1)S(1)} %bitcast.15, ...), custom_call_target="tpu_custom_call" | custom-call | flops 100000000 | bytes 4000000 | tf_op jit(solution)/shard_map/coarse/pallas_call | solution.py:432
  150.2 0.8 copy-done.16
  151.3 4.8 %collective-permute-start.10 = (bf16[768,128]{1,0:T(8,128)(2,1)S(1)}, bf16[768,128]{1,0:T(8,128)(2,1)S(1)}, u32[]{:S(2)}, u32[]{:S(2)}) collective-permute-start(bf16[768,128]{1,0:T(8,128)(2,1)S(1)} %get-tuple-element.140), channel_id=1, source_target_pairs={{4,0},{8,4},{12,8},{16,12},{20,16},{24,20},{28,24},{32,28},{36,32}... | collective-permute-start | bytes 589832 | tf_op jit(solution)/shard_map/ppermute | solution.py:28
  156.1 4.1 %all-to-all-start.4 = ((bf16[32,4,16,128]{3,2,1,0:T(8,128)(2,1)}), bf16[32,4,16,128]{3,2,1,0:T(8,128)(2,1)S(1)}, u32[]{:S(2)}, u32[]{:S(2)}) async-start(bf16[32,4,16,128]{3,2,1,0:T(8,128)(2,1)} %get-tuple-element.145), calls=%async_computation.4 | async-start | bytes 1048576 | tf_op jit(solution)/shard_map/all_to_all | solution.py:587
  160.2 1.0 copy-done.17
  161.2 1.0 copy-done.21
  162.2 3.5 %last_step.1 = (f32[2,768,128]{2,1,0:T(8,128)S(1)}, f32[2,768,128]{2,1,0:T(8,128)}, f32[1,128]{1,0:T(1,128)S(1)}) custom-call(s32[3,4,128]{2,1,0:T(4,128)S(1)} %pad_add_fusion.refs_0_, f32[64,128]{1,0:T(8,128)S(1)} %get-tuple-element.135.refs_1_, bf16[3,768,64]{2,1,0:T(8,128)(2,1)S(1)} %copy-done.2, bf16[3,768,256]{2,1,0:T(8,128)(2,1)} %get-tuple-element.95.refs_8_.refs_3_, ...), custom_call_target="tpu_custom_call" | custom-call | flops 99999997952 | bytes 1000000000 | tf_op jit(solution)/shard_map/last_step/pallas_call | solution.py:531
  165.7 5.6 %all-to-all-done.4 = bf16[32,4,16,128]{3,2,1,0:T(8,128)(2,1)S(1)} async-done(((bf16[32,4,16,128]{3,2,1,0:T(8,128)(2,1)}), bf16[32,4,16,128]{3,2,1,0:T(8,128)(2,1)S(1)}, u32[]{:S(2)}, u32[]{:S(2)}) %all-to-all-start.4) | async-done | bytes 524320 | tf_op jit(solution)/shard_map/all_to_all | solution.py:587
  171.3 2.0 %final.1 = (f32[2,768,128]{2,1,0:T(8,128)}, f32[128,4,128]{2,1,0:T(4,128)}) custom-call(s32[3,4,128]{2,1,0:T(4,128)S(1)} %pad_add_fusion.refs_0_, bf16[128,16,128]{2,1,0:T(8,128)(2,1)S(1)} %bitcast.14, f32[120,128]{1,0:T(8,128)S(1)} %collective-permute-done.refs_3_.refs_2_, f32[2,24,128]{2,1,0:T(8,128)S(1)} %copy-done.3, ...), custom_call_target="tpu_custom_call" | custom-call | tf_op jit(solution)/shard_map/final/pallas_call | solution.py:572
  173.4 6.8 %all-to-all-start.5 = ((f32[128,4,128]{2,1,0:T(4,128)}), f32[128,4,128]{2,1,0:T(4,128)S(1)}, u32[]{:S(2)}, u32[]{:S(2)}) async-start(f32[128,4,128]{2,1,0:T(4,128)} %get-tuple-element.151), calls=%async_computation.5 | async-start | bytes 524288 | tf_op jit(solution)/shard_map/all_to_all | solution.py:587
  180.2 10.5 %all-to-all-done.5 = f32[128,4,128]{2,1,0:T(4,128)S(1)} async-done(((f32[128,4,128]{2,1,0:T(4,128)}), f32[128,4,128]{2,1,0:T(4,128)S(1)}, u32[]{:S(2)}, u32[]{:S(2)}) %all-to-all-start.5) | async-done | bytes 262176 | tf_op jit(solution)/shard_map/all_to_all | solution.py:587
  190.7 0.6 fusion.3
  191.4 0.6 dynamic-slice_bitcast_fusion
  (59 shorter events, 0.8 us)
Async XLA Ops:
  3.8 29.7 %collective-permute-start.1 = (f32[120,128]{1,0:T(8,128)}, f32[120,128]{1,0:T(8,128)S(1)}, u32[]{:S(2)}, u32[]{:S(2)}) collective-permute-start(f32[120,128]{1,0:T(8,128)} %get-tuple-element.80), channel_id=1, source_target_pairs={{4,0},{8,4},{12,8},{16,12},{20,16},{24,20},{28,24},{32,28},{36,32}... | collective-permute-start | bytes 184328 | tf_op jit(solution)/shard_map/ppermute | solution.py:28
  9.9 23.6 %collective-permute-start = (f32[120,128]{1,0:T(8,128)}, f32[120,128]{1,0:T(8,128)S(1)}, u32[]{:S(2)}, u32[]{:S(2)}) collective-permute-start(f32[120,128]{1,0:T(8,128)} %get-tuple-element.78), channel_id=1, source_target_pairs={{124,0},{0,4},{4,8},{8,12},{12,16},{16,20},{20,24},{24,28},{28,32}... | collective-permute-start | bytes 184328 | tf_op jit(solution)/shard_map/ppermute | solution.py:28
  9.9 54.9 %collective-permute-start.2 = (f32[768,128]{1,0:T(8,128)}, f32[768,128]{1,0:T(8,128)S(1)}, u32[]{:S(2)}, u32[]{:S(2)}) collective-permute-start(f32[768,128]{1,0:T(8,128)} %get-tuple-element.84), channel_id=1, source_target_pairs={{124,0},{0,4},{4,8},{8,12},{12,16},{16,20},{20,24},{24,28},{28,32}... | collective-permute-start | bytes 1179656 | tf_op jit(solution)/shard_map/ppermute | solution.py:28
  11.4 22.1 %copy-start = (f32[2,768,128]{2,1,0:T(8,128)S(1)}, f32[2,768,128]{2,1,0:T(8,128)}, u32[]{:S(2)}) copy-start(f32[2,768,128]{2,1,0:T(8,128)} %refs_1_.1) | copy-start | bytes 2359300
  11.5 22.1 %copy-start.8 = (bf16[2,16,768]{2,1,0:T(8,128)(2,1)S(1)}, bf16[2,16,768]{2,1,0:T(8,128)(2,1)}, u32[]{:S(2)}) copy-start(bf16[2,16,768]{2,1,0:T(8,128)(2,1)} %get-tuple-element.81.refs_1_) | copy-start | bytes 147460
  11.5 22.1 %copy-start.9 = (bf16[2,16,768]{2,1,0:T(8,128)(2,1)S(1)}, bf16[2,16,768]{2,1,0:T(8,128)(2,1)}, u32[]{:S(2)}) copy-start(bf16[2,16,768]{2,1,0:T(8,128)(2,1)} %get-tuple-element.82.refs_2_) | copy-start | bytes 147460
  32.6 0.9 copy-start.4
  35.5 29.3 %copy-start.1 = (bf16[3,768,64]{2,1,0:T(8,128)(2,1)}, bf16[3,768,64]{2,1,0:T(8,128)(2,1)S(1)}, u32[]{:S(2)}) copy-start(bf16[3,768,64]{2,1,0:T(8,128)(2,1)S(1)} %get-tuple-element.86.refs_4_.refs_2_.refs_5_) | copy-start | bytes 884740
  35.5 39.7 %all-to-all-start = ((bf16[32,4,16,128]{3,2,1,0:T(8,128)(2,1)}), bf16[32,4,16,128]{3,2,1,0:T(8,128)(2,1)S(1)}, u32[]{:S(2)}, u32[]{:S(2)}) async-start(bf16[32,4,16,128]{3,2,1,0:T(8,128)(2,1)} %get-tuple-element.83), calls=%async_computation | async-start | bytes 1048576 | tf_op jit(solution)/shard_map/all_to_all | solution.py:587
  63.9 0.9 copy-start.5
  64.8 10.3 %copy-start.3 = (f32[2,24,128]{2,1,0:T(8,128)S(1)}, f32[2,24,128]{2,1,0:T(8,128)}, u32[]{:S(2)}) copy-start(f32[2,24,128]{2,1,0:T(8,128)} %get-tuple-element.79.refs_3_) | copy-start | bytes 73732
  73.6 0.7 copy-start.6
  74.3 0.8 copy-start.10
  75.1 1.0 copy-start.7
  76.1 11.9 %copy-start.11 = (f32[768,128]{1,0:T(8,128)S(1)}, f32[768,128]{1,0:T(8,128)}, u32[]{:S(2)}) copy-start(f32[768,128]{1,0:T(8,128)} %copy-done.10) | copy-start | bytes 1179652
  78.8 9.2 %copy-start.14 = (f32[768,128]{1,0:T(8,128)}, f32[768,128]{1,0:T(8,128)S(1)}, u32[]{:S(2)}) copy-start(f32[768,128]{1,0:T(8,128)S(1)} %get-tuple-element.101.refs_6_) | copy-start | bytes 1179652
  78.8 9.2 %collective-permute-start.3 = (bf16[768,128]{1,0:T(8,128)(2,1)}, bf16[768,128]{1,0:T(8,128)(2,1)S(1)}, u32[]{:S(2)}, u32[]{:S(2)}) collective-permute-start(bf16[768,128]{1,0:T(8,128)(2,1)} %get-tuple-element.102), channel_id=1, source_target_pairs={{124,0},{0,4},{4,8},{8,12},{12,16},{16,20},{20,24},{24,28},{28,32}... | collective-permute-start | bytes 589832 | tf_op jit(solution)/shard_map/ppermute | solution.py:28
  78.9 9.1 %collective-permute-start.4 = (bf16[768,128]{1,0:T(8,128)(2,1)S(1)}, bf16[768,128]{1,0:T(8,128)(2,1)S(1)}, u32[]{:S(2)}, u32[]{:S(2)}) collective-permute-start(bf16[768,128]{1,0:T(8,128)(2,1)S(1)} %get-tuple-element.103), channel_id=1, source_target_pairs={{4,0},{8,4},{12,8},{16,12},{20,16},{24,20},{28,24},{32,28},{36,32}... | collective-permute-start | bytes 589832 | tf_op jit(solution)/shard_map/ppermute | solution.py:28
  83.9 15.3 %all-to-all-start.1 = ((bf16[32,4,16,128]{3,2,1,0:T(8,128)(2,1)}), bf16[32,4,16,128]{3,2,1,0:T(8,128)(2,1)S(1)}, u32[]{:S(2)}, u32[]{:S(2)}) async-start(bf16[32,4,16,128]{3,2,1,0:T(8,128)(2,1)} %get-tuple-element.97), calls=%async_computation.1 | async-start | bytes 1048576 | tf_op jit(solution)/shard_map/all_to_all | solution.py:587
  88.0 1.0 copy-start.15
  98.4 0.8 copy-start.22
  101.7 9.0 %collective-permute-start.5 = (bf16[768,128]{1,0:T(8,128)(2,1)S(1)}, bf16[768,128]{1,0:T(8,128)(2,1)S(1)}, u32[]{:S(2)}, u32[]{:S(2)}) collective-permute-start(bf16[768,128]{1,0:T(8,128)(2,1)S(1)} %get-tuple-element.114), channel_id=1, source_target_pairs={{124,0},{0,4},{4,8},{8,12},{12,16},{16,20},{20,24},{24,28},{28,32}... | collective-permute-start | bytes 589832 | tf_op jit(solution)/shard_map/ppermute | solution.py:28
  102.2 8.5 %collective-permute-start.6 = (bf16[768,128]{1,0:T(8,128)(2,1)S(1)}, bf16[768,128]{1,0:T(8,128)(2,1)S(1)}, u32[]{:S(2)}, u32[]{:S(2)}) collective-permute-start(bf16[768,128]{1,0:T(8,128)(2,1)S(1)} %get-tuple-element.115), channel_id=1, source_target_pairs={{4,0},{8,4},{12,8},{16,12},{20,16},{24,20},{28,24},{32,28},{36,32}... | collective-permute-start | bytes 589832 | tf_op jit(solution)/shard_map/ppermute | solution.py:28
  106.7 15.6 %all-to-all-start.2 = ((bf16[32,4,16,128]{3,2,1,0:T(8,128)(2,1)}), bf16[32,4,16,128]{3,2,1,0:T(8,128)(2,1)S(1)}, u32[]{:S(2)}, u32[]{:S(2)}) async-start(bf16[32,4,16,128]{3,2,1,0:T(8,128)(2,1)} %get-tuple-element.109), calls=%async_computation.2 | async-start | bytes 1048576 | tf_op jit(solution)/shard_map/all_to_all | solution.py:587
  110.7 1.0 copy-start.23
  121.6 0.8 copy-start.18
  125.0 0.7 copy-start.12
  125.7 9.1 %collective-permute-start.7 = (bf16[768,128]{1,0:T(8,128)(2,1)}, bf16[768,128]{1,0:T(8,128)(2,1)S(1)}, u32[]{:S(2)}, u32[]{:S(2)}) collective-permute-start(bf16[768,128]{1,0:T(8,128)(2,1)} %get-tuple-element.127), channel_id=1, source_target_pairs={{124,0},{0,4},{4,8},{8,12},{12,16},{16,20},{20,24},{24,28},{28,32}... | collective-permute-start | bytes 589832 | tf_op jit(solution)/shard_map/ppermute | solution.py:28
  126.0 8.9 %collective-permute-start.8 = (bf16[768,128]{1,0:T(8,128)(2,1)S(1)}, bf16[768,128]{1,0:T(8,128)(2,1)S(1)}, u32[]{:S(2)}, u32[]{:S(2)}) collective-permute-start(bf16[768,128]{1,0:T(8,128)(2,1)S(1)} %get-tuple-element.128), channel_id=1, source_target_pairs={{4,0},{8,4},{12,8},{16,12},{20,16},{24,20},{28,24},{32,28},{36,32}... | collective-permute-start | bytes 589832 | tf_op jit(solution)/shard_map/ppermute | solution.py:28
  130.8 16.8 %all-to-all-start.3 = ((bf16[32,4,16,128]{3,2,1,0:T(8,128)(2,1)}), bf16[32,4,16,128]{3,2,1,0:T(8,128)(2,1)S(1)}, u32[]{:S(2)}, u32[]{:S(2)}) async-start(bf16[32,4,16,128]{3,2,1,0:T(8,128)(2,1)} %get-tuple-element.122), calls=%async_computation.3 | async-start | bytes 1048576 | tf_op jit(solution)/shard_map/all_to_all | solution.py:587
  134.9 1.0 copy-start.13
  135.9 1.0 copy-start.19
  146.8 0.7 copy-start.20
  147.6 12.6 %copy-start.2 = (bf16[3,768,64]{2,1,0:T(8,128)(2,1)S(1)}, bf16[3,768,64]{2,1,0:T(8,128)(2,1)}, u32[]{:S(2)}) copy-start(bf16[3,768,64]{2,1,0:T(8,128)(2,1)} %copy-done.1) | copy-start | bytes 884740
  150.2 0.8 copy-start.16
  151.0 9.1 %collective-permute-start.9 = (bf16[768,128]{1,0:T(8,128)(2,1)}, bf16[768,128]{1,0:T(8,128)(2,1)S(1)}, u32[]{:S(2)}, u32[]{:S(2)}) collective-permute-start(bf16[768,128]{1,0:T(8,128)(2,1)} %get-tuple-element.139), channel_id=1, source_target_pairs={{124,0},{0,4},{4,8},{8,12},{12,16},{16,20},{20,24},{24,28},{28,32}... | collective-permute-start | bytes 589832 | tf_op jit(solution)/shard_map/ppermute | solution.py:28
  151.3 8.9 %collective-permute-start.10 = (bf16[768,128]{1,0:T(8,128)(2,1)S(1)}, bf16[768,128]{1,0:T(8,128)(2,1)S(1)}, u32[]{:S(2)}, u32[]{:S(2)}) collective-permute-start(bf16[768,128]{1,0:T(8,128)(2,1)S(1)} %get-tuple-element.140), channel_id=1, source_target_pairs={{4,0},{8,4},{12,8},{16,12},{20,16},{24,20},{28,24},{32,28},{36,32}... | collective-permute-start | bytes 589832 | tf_op jit(solution)/shard_map/ppermute | solution.py:28
  156.1 15.3 %all-to-all-start.4 = ((bf16[32,4,16,128]{3,2,1,0:T(8,128)(2,1)}), bf16[32,4,16,128]{3,2,1,0:T(8,128)(2,1)S(1)}, u32[]{:S(2)}, u32[]{:S(2)}) async-start(bf16[32,4,16,128]{3,2,1,0:T(8,128)(2,1)} %get-tuple-element.145), calls=%async_computation.4 | async-start | bytes 1048576 | tf_op jit(solution)/shard_map/all_to_all | solution.py:587
  160.2 1.0 copy-start.17
  161.2 1.0 copy-start.21
  173.4 17.3 %all-to-all-start.5 = ((f32[128,4,128]{2,1,0:T(4,128)}), f32[128,4,128]{2,1,0:T(4,128)S(1)}, u32[]{:S(2)}, u32[]{:S(2)}) async-start(f32[128,4,128]{2,1,0:T(4,128)} %get-tuple-element.151), calls=%async_computation.5 | async-start | bytes 524288 | tf_op jit(solution)/shard_map/all_to_all | solution.py:587
